TPU v7x, 32 devices: a whole 2x2x4 slice. The times are simulated.
32 devices in a mesh: parts: 2 (over x), dp: 2 (over core), tensor: 8 (over z, y).
Axes of the slice: x: 2, y: 2, z: 4, core: 2. Of those that a mesh axis runs over, the one named last changes fastest.
Arguments:
- home_token_rows: bfloat16 [12288, 8192], P(('parts', 'dp'), 'tensor'), parts along dimension 0, may hold values from -6 to 6
- block_target_group: int32 [96], P(('parts', 'dp')), parts along dimension 0, may hold values from 0 to 1
- block_send_slot: int32 [96], P(('parts', 'dp')), parts along dimension 0, may hold values from 0 to 15, as said below
- block_adapter_job: int32 [96], P(('parts', 'dp')), parts along dimension 0, may hold values from 0 to 15
- key_weight_matrix: bfloat16 [8192, 1024], P('tensor'), may hold values from -0.0625 to 0.0625
- down_factors: bfloat16 [8192, 256], P('tensor'), may hold values from -0.0625 to 0.0625
- up_factors: bfloat16 [256, 1024], P(None, 'tensor'), may hold values from -1.5 to 1.5
- output_gradient: bfloat16 [16384, 1024], P(('parts', 'dp'), 'tensor'), parts along dimension 0, may hold values from -6 to 6
Outputs:
- output: bfloat16 [16384, 1024], P(('parts', 'dp'), 'tensor'), parts along dimension 0
- grad_home: bfloat16 [12288, 8192], P(('parts', 'dp'), 'tensor'), parts along dimension 0
- grad_a: float32 [8192, 512], P('tensor', ('parts', 'dp')), parts along dimension 1
- up_factor_gradient: float32 [512, 1024], P(('parts', 'dp'), 'tensor'), parts along dimension 0
There are 2 independent parts, one for each index of `parts`. A program takes and returns all parts, laid end to end along the dimension named above; an argument that names none is the same for every part. Nothing has to cross between parts.
Inputs may be any that keep to these rules, and one draw needn't show every extreme that they name: `block_send_slot`: among the blocks of one home group with one compute group, slots are distinct and run from 0 without gaps; each home group sends exactly 16 blocks to one of the compute groups.
All inputs are finite; a program needn't handle non-finite values.
Results may differ from a plain program's by a relative error of at most 0.001.
Values may be sent and summed in bfloat16 or wider, within the bound.
No kernel may reach another device: no remote copies, remote signals or barrier semaphores. Data moves between devices by JAX's collectives and lax.ppermute only.
A program may use at most 192 MiB of HBM per device.

v0:
```python
import jax
import jax.numpy as jnp
from jax import lax
from jax.sharding import PartitionSpec as P

ADAPTER_RANK = 16


adapter_scale = 2.0
highest_precision = lax.Precision.HIGHEST


def local(
    home_token_rows,
    block_target_group,
    block_send_slot,
    block_adapter_job,
    key_weight_matrix,
    down_factors,
    up_factors,
    output_gradient,
):
    groups = lax.axis_size("dp")
    feature_columns = home_token_rows.shape[1]
    home_count = block_target_group.shape[0]
    block_len = home_token_rows.shape[0] // home_count
    gathered_rows = output_gradient.shape[0]
    gathered_blocks = gathered_rows // block_len
    capacity = gathered_blocks // groups
    key_columns = output_gradient.shape[1]
    total_per_job = down_factors.shape[1] // ADAPTER_RANK
    target = block_target_group * capacity + block_send_slot
    home_blocks = home_token_rows.reshape(home_count, block_len, feature_columns)
    send_rows = (
        jnp.zeros((gathered_blocks, block_len, feature_columns), jnp.bfloat16)
        .at[target]
        .set(home_blocks)
    )
    send_jobs = jnp.zeros((gathered_blocks,), jnp.int32).at[target].set(block_adapter_job)
    got_rows, got_jobs = (
        lax.all_to_all(
            send_rows.reshape(groups, capacity * block_len, feature_columns),
            "dp",
            split_axis=0,
            concat_axis=0,
            tiled=True,
        ),
        lax.all_to_all(
            send_jobs.reshape(groups, capacity), "dp", split_axis=0, concat_axis=0, tiled=True
        ),
    )
    comp_rows = got_rows.reshape(gathered_rows, feature_columns)
    compute_jobs = got_jobs.reshape(gathered_blocks)
    job_indicator = (
        compute_jobs[:, None] == jnp.arange(total_per_job, dtype=jnp.int32)[None, :]
    ).astype(jnp.float32)
    down_blocks = down_factors.reshape(feature_columns, total_per_job, ADAPTER_RANK).transpose(
        1, 0, 2
    )[compute_jobs]
    up_blocks = up_factors.reshape(total_per_job, ADAPTER_RANK, key_columns)[compute_jobs]
    row_blocks = comp_rows.reshape(gathered_blocks, block_len, feature_columns)
    low_part = jnp.einsum(
        "nbc,ncr->nbr", row_blocks, down_blocks, preferred_element_type=jnp.float32
    )
    lowrank_sum = lax.psum(low_part, "tensor")
    frozen_output = jnp.dot(comp_rows, key_weight_matrix, preferred_element_type=jnp.float32)
    summed_output = lax.psum_scatter(frozen_output, "tensor", scatter_dimension=1, tiled=True)
    adapter_index = jnp.einsum(
        "nbr,nrk->nbk", lowrank_sum, up_blocks.astype(jnp.float32), precision=highest_precision
    )
    output = (
        summed_output + adapter_scale * adapter_index.reshape(gathered_rows, key_columns)
    ).astype(jnp.bfloat16)
    gradient_blocks = output_gradient.reshape(gathered_blocks, block_len, key_columns)
    through_sum = lax.dot_general(
        lax.all_gather(output_gradient, "tensor", axis=1, tiled=True),
        key_weight_matrix,
        (((1,), (1,)), ((), ())),
        preferred_element_type=jnp.float32,
    )
    gradient_share = jnp.einsum(
        "szm,sfm->szf", gradient_blocks, up_blocks, preferred_element_type=jnp.float32
    )
    reduced_gradient = adapter_scale * lax.psum(gradient_share, "tensor")
    lowrank_back = jnp.einsum(
        "nbr,ncr->nbc",
        reduced_gradient,
        down_blocks.astype(jnp.float32),
        precision=highest_precision,
    )
    grad_rows = (through_sum + lowrank_back.reshape(gathered_rows, feature_columns)).astype(
        jnp.bfloat16
    )
    returned = lax.all_to_all(
        grad_rows.reshape(groups, capacity * block_len, feature_columns),
        "dp",
        split_axis=0,
        concat_axis=0,
        tiled=True,
    )
    grad_home = returned.reshape(gathered_blocks, block_len, feature_columns)[target].reshape(
        home_count * block_len, feature_columns
    )
    a_terms = jnp.einsum(
        "nbc,nbr->ncr",
        row_blocks.astype(jnp.float32),
        reduced_gradient,
        precision=highest_precision,
    )
    term_a = jnp.einsum("nj,ncr->cjr", job_indicator, a_terms, precision=highest_precision).reshape(
        feature_columns, total_per_job * ADAPTER_RANK
    )
    up_terms = jnp.einsum(
        "nbr,nbk->nrk",
        lowrank_sum,
        gradient_blocks.astype(jnp.float32),
        precision=highest_precision,
    )
    up_term = adapter_scale * jnp.einsum(
        "wq,wbz->qbz", job_indicator, up_terms, precision=highest_precision
    ).reshape(total_per_job * ADAPTER_RANK, key_columns)
    grad_a, up_factor_gradient = (
        lax.psum_scatter(term_a, "dp", scatter_dimension=1, tiled=True),
        lax.psum_scatter(up_term, "dp", scatter_dimension=0, tiled=True),
    )
    return (output, grad_home, grad_a, up_factor_gradient)


def solution(mesh):
    return jax.shard_map(
        local,
        mesh=mesh,
        in_specs=(
            P(("parts", "dp"), "tensor"),
            P(("parts", "dp")),
            P(("parts", "dp")),
            P(("parts", "dp")),
            P("tensor", None),
            P("tensor", None),
            P(None, "tensor"),
            P(("parts", "dp"), "tensor"),
        ),
        out_specs=(
            P(("parts", "dp"), "tensor"),
            P(("parts", "dp"), "tensor"),
            P("tensor", ("parts", "dp")),
            P(("parts", "dp"), "tensor"),
        ),
        check_vma=False,
    )
```

profile of v0, /device:TPU:1, one launch (start us, length us, event | category | flops | bytes accessed | tf_op | source)
XLA Modules:
  0.0 577.5 jit_solution(13035878225442504244)
XLA Ops:
  7.2 0.0 copy-start
  7.2 0.8 compare_select_fusion.1
  8.0 0.8 scatter_custom_fusion.1
  8.8 0.6 all_to_all.13
  9.4 3.2 all-to-all-start.1
  12.7 4.3 broadcast_in_dim.4
  17.0 16.2 %scatter_fusion = bf16[32,128,1024]{2,1,0:T(8,128)(2,1)} fusion(bf16[32,128,1024]{2,1,0:T(8,128)(2,1)} %broadcast_in_dim.4, s32[24]{0:T(128)S(1)} %compare_select_fusion.1, bf16[24,128,1024]{2,1,0:T(8,128)(2,1)} %bitcast.55), kind=kCustom, calls=%fused_computation.3 | custom fusion | bytes 18874464 | tf_op jit(solution)/shard_map/scatter | solution.py:37
  33.2 7.1 %all-to-all-start = ((bf16[2,2048,1024]{2,1,0:T(8,128)(2,1)}), bf16[2,2048,1024]{2,1,0:T(8,128)(2,1)}, u32[]{:S(2)}, u32[]{:S(2)}) async-start(bf16[2,2048,1024]{2,1,0:T(8,128)(2,1)} %bitcast.49), calls=%async_computation | async-start | bytes 16777216 | tf_op jit(solution)/shard_map/all_to_all | solution.py:41
  40.3 0.0 all-reduce.3.cloned.1.call-start
  40.4 0.5 broadcast.63
  40.9 0.7 reduce.5
  41.5 0.1 reshape.89
  41.6 0.2 copy.16
  41.9 0.0 copy-start.5
  41.9 1.6 gather_fusion
  43.5 0.6 gather_fusion.1
  44.0 3.4 all-to-all-done
  47.4 6.6 %fusion.25 = f32[32,128,16]{1,2,0:T(8,128)} fusion(bf16[32,128,1024]{2,1,0:T(8,128)(2,1)} %bitcast.3, bf16[32,1024,16]{1,2,0:T(8,128)(2,1)} %gather_fusion), kind=kOutput, calls=%fused_computation.36 | convolution fusion | flops 134217728 | bytes 9699328 | tf_op jit(solution)/shard_map/nbc,ncr->nbr/dot_general | solution.py:62
  54.0 1.4 convolution_bitcast_fusion
  55.4 0.0 all-reduce.3.cloned.1.call-update
  55.4 0.0 reduce-scatter.6.cloned.1.call-start
  55.5 0.1 eq.15
  55.6 73.4 %all-reduce.3.cloned.1.call-done = (f32[32,128,16]{1,2,0:T(8,128)}, f32[32,128,16]{1,2,0:T(8,128)}) async-done(((f32[32,128,16]{1,2,0:T(8,128)}, f32[32,128,16]{1,2,0:T(8,128)}), (f32[32,128,16]{1,2,0:T(8,128)}, f32[32,128,16]{1,2,0:T(8,128)})) %all-reduce.3.cloned.1.call-update) | async-done | bytes 524304 | tf_op jit(solution)/shard_map/psum | solution.py:65
  129.0 5.8 fusion.8
  134.7 2.0 fusion.4
  136.8 1.6 copy.19
  138.4 0.0 reduce-scatter.6.cloned.1.call-update
  138.4 0.0 all-gather.2.cloned.1.call-start
  138.5 0.7 all-gather.2.cloned.1.call-update
  139.1 0.2 reduce-scatter.4.cloned.1.call-start
  139.4 14.5 %fusion.24 = f32[4096,1024]{1,0:T(8,128)} fusion(bf16[4096,1024]{1,0:T(8,128)(2,1)} %bitcast.2, bf16[1024,1024]{1,0:T(8,128)(2,1)S(1)} %copy-done), kind=kOutput, calls=%fused_computation.35 | convolution fusion | flops 8589934592 | bytes 27262976 | tf_op jit(solution)/shard_map/dot_general | solution.py:66
  153.9 0.0 reduce-scatter.4.cloned.1.call-update
  153.9 0.0 reduce-scatter.8.cloned.1.call-start
  154.0 2.3 fusion.26
  156.3 0.3 convolution_multiply_fusion.1
  156.6 0.7 copy.21
  157.3 4.2 convolution_multiply_fusion
  161.4 10.2 %fusion.10 = f32[32,128,1024]{2,1,0:T(8,128)} fusion(bf16[32,1024,16]{1,2,0:T(8,128)(2,1)S(1)} %copy-done.1, f32[32,128,16]{1,2,0:T(8,128)S(1)} %copy-done.3), kind=kOutput, calls=%fused_computation.18 | convolution fusion | flops 805371904 | bytes 18087936 | tf_op jit(solution)/shard_map/nbr,ncr->nbc/dot_general | solution.py:85
  171.6 0.0 reduce-scatter.8.cloned.1.call-update
  171.6 0.0 reduce-scatter.6.cloned.1.call-done
  171.7 2.0 copy.22
  173.7 102.5 %all-gather.2.cloned.1.call-done = bf16[4096,1024]{1,0:T(8,128)(2,1)} async-done(((bf16[4096,128]{1,0:T(8,128)(2,1)}), bf16[4096,1024]{1,0:T(8,128)(2,1)}) %all-gather.2.cloned.1.call-update) | async-done | bytes 8388624 | tf_op jit(solution)/shard_map/all_gather | solution.py:76
  276.2 17.0 %fusion = bf16[4096,1024]{1,0:T(8,128)(2,1)} fusion(f32[32,128,1024]{2,1,0:T(8,128)} %fusion.10, bf16[4096,1024]{1,0:T(8,128)(2,1)} %all-gather.2.cloned.1.call-done, bf16[1024,1024]{1,0:T(8,128)(2,1)S(1)} %copy-done), kind=kOutput, calls=%fused_computation.6 | convolution fusion | flops 8598323200 | bytes 35651584 | tf_op jit(solution)/shard_map/dot_general | solution.py:75
  293.2 19.2 %all_to_all.19 = bf16[2,2048,1024]{2,1,0:T(8,128)(2,1)} all-to-all(bf16[2,2048,1024]{2,1,0:T(8,128)(2,1)} %bitcast.53), channel_id=1, replica_groups=mesh['parts'=2,'dp'=2,'tensor'=8] {'dp'}, dimensions={0} | all-to-all | bytes 16777216 | tf_op jit(solution)/shard_map/all_to_all | solution.py:94
  312.4 7.9 %gather_fusion.2 = bf16[24,128,1024]{2,1,0:T(8,128)(2,1)} fusion(bf16[32,128,1024]{2,1,0:T(8,128)(2,1)} %bitcast.50, s32[1024]{0:T(1024)S(1)} %pad_clamp_fusion), kind=kCustom, calls=%fused_computation.2 | custom fusion | bytes 12583008 | tf_op jit(solution)/shard_map/gather | solution.py:101
  320.3 241.0 %reduce-scatter.4.cloned.1.call-done = f32[4096,128]{1,0:T(8,128)} async-done(((f32[4096,1024]{1,0:T(8,128)}), f32[4096,128]{1,0:T(8,128)}) %reduce-scatter.4.cloned.1.call-update) | async-done | bytes 2097168 | tf_op jit(solution)/shard_map/reduce_scatter | solution.py:67
  561.3 3.4 fusion.1
  564.7 6.2 %reduce-scatter.8.cloned.1.call-done = f32[128,128]{1,0:T(8,128)} async-done(((f32[256,128]{1,0:T(8,128)}), f32[128,128]{1,0:T(8,128)}) %reduce-scatter.8.cloned.1.call-update) | async-done | bytes 65552 | tf_op jit(solution)/shard_map/reduce_scatter | solution.py:124
  (14 shorter events, 0.0 us)
Async XLA Ops:
  7.2 132.2 %copy-start = (bf16[1024,1024]{1,0:T(8,128)(2,1)S(1)}, bf16[1024,1024]{1,0:T(8,128)(2,1)}, u32[]{:S(2)}) copy-start(bf16[1024,1024]{1,0:T(8,128)(2,1)} %param.12) | copy-start | bytes 6291460
  9.4 23.8 %all-to-all-start.1 = ((s32[2,1,16]{2,1,0:T(1,128)}), s32[2,1,16]{2,1,0:T(1,128)S(1)}, u32[]{:S(2)}, u32[]{:S(2)}) async-start(s32[2,1,16]{2,1,0:T(1,128)} %bitcast.6), calls=%async_computation.2 | async-start | bytes 2048 | tf_op jit(solution)/shard_map/all_to_all | solution.py:48
  33.2 8.4 %copy-start.4 = (bf16[1024,256]{1,0:T(8,128)(2,1)S(1)}, bf16[1024,256]{1,0:T(8,128)(2,1)}, u32[]{:S(2)}) copy-start(bf16[1024,256]{1,0:T(8,128)(2,1)} %param.13) | copy-start | bytes 1572868
  33.2 14.2 %all-to-all-start = ((bf16[2,2048,1024]{2,1,0:T(8,128)(2,1)}), bf16[2,2048,1024]{2,1,0:T(8,128)(2,1)}, u32[]{:S(2)}, u32[]{:S(2)}) async-start(bf16[2,2048,1024]{2,1,0:T(8,128)(2,1)} %bitcast.49), calls=%async_computation | async-start | bytes 16777216 | tf_op jit(solution)/shard_map/all_to_all | solution.py:41
  40.3 88.7 %all-reduce.3.cloned.1.call-start = ((), (), s32[]{:S(2)}) async-start(), calls=%async_computation.10 | async-start | bytes 1048576 | tf_op jit(solution)/shard_map/psum | solution.py:65
  41.9 1.6 copy-start.5
  43.5 10.6 %copy-start.2 = (bf16[4096,128]{1,0:T(8,128)(2,1)S(1)}, bf16[4096,128]{1,0:T(8,128)(2,1)}, u32[]{:S(2)}) copy-start(bf16[4096,128]{1,0:T(8,128)(2,1)} %param.15) | copy-start | bytes 3145732
  55.4 116.2 %reduce-scatter.6.cloned.1.call-start = ((), (), s32[]{:S(2)}) async-start(), calls=%async_computation.8 | async-start | bytes 1572864 | tf_op jit(solution)/shard_map/reduce_scatter | solution.py:123
  138.4 137.8 %all-gather.2.cloned.1.call-start = ((), (), s32[]{:S(2)}) async-start(), calls=%async_computation.7 | async-start | bytes 9437184 | tf_op jit(solution)/shard_map/all_gather | solution.py:76
  139.1 422.2 %reduce-scatter.4.cloned.1.call-start = ((), (), s32[]{:S(2)}) async-start(), calls=%async_computation.6 | async-start | bytes 18874368 | tf_op jit(solution)/shard_map/reduce_scatter | solution.py:67
  153.9 7.6 %copy-start.1 = (bf16[32,1024,16]{1,2,0:T(8,128)(2,1)S(1)}, bf16[32,1024,16]{1,2,0:T(8,128)(2,1)}, u32[]{:S(2)}) copy-start(bf16[32,1024,16]{1,2,0:T(8,128)(2,1)} %gather_fusion) | copy-start | bytes 3145732
  153.9 7.6 %copy-start.3 = (f32[32,128,16]{1,2,0:T(8,128)S(1)}, f32[32,128,16]{1,2,0:T(8,128)}, u32[]{:S(2)}) copy-start(f32[32,128,16]{1,2,0:T(8,128)} %get-tuple-element.13) | copy-start | bytes 786436
  153.9 417.0 %reduce-scatter.8.cloned.1.call-start = ((), (), s32[]{:S(2)}) async-start(), calls=%async_computation.9 | async-start | bytes 196608 | tf_op jit(solution)/shard_map/reduce_scatter | solution.py:124
Sparse Core Ops, SparseCore 0:
  55.6 73.3 all-reduce.2
  138.5 9.7 reduce-scatter.5
  150.4 125.7 all-gather.1
  279.8 281.4 reduce-scatter.3
  564.1 6.8 reduce-scatter.7
where the time goes:
time: 579 us; the launch traced here: 577 us
  waiting for transfers between devices  427 us (74%)
  matrix products  64.2 us (11%)
  local copies, waits for them, and re-layouts  37.2 us (6%)
  blocking collectives  19.2 us (3%)
  between operations  13.9 us (2%)
  starting transfers between devices  10.7 us (2%)
    reduce_scatter x1, waiting for transfers between devices, local(): lax.psum_scatter(frozen_output, 'tensor', scatter_dimension=1, tiled=True)  241 us
    all_gather x1, waiting for transfers between devices, local(): lax.all_gather(output_gradient, 'tensor', axis=1, tiled=True)  102 us
    psum x1, waiting for transfers between devices, local(): lowrank_sum = lax.psum(low_part, 'tensor')  73.4 us
    all_to_all x1, blocking collectives, local(): lax.all_to_all(grad_rows.reshape(groups, capacity * block_len, feature_co...  19.2 us
    dot_general x1, matrix products, local(): lax.dot_general(lax.all_gather(output_gradient, 'tensor', axis=1, tiled=T...  17 us
    scatter x1, local copies, waits for them, and re-layouts, local(): send_rows = jnp.zeros((gathered_blocks, block_len, feature_columns), jnp....  16.2 us
    dot_general x1, matrix products, local(): jnp.dot(comp_rows, key_weight_matrix, preferred_element_type=jnp.float32)  14.5 us
  transfers between devices with their start and end apart: 7, of which 5 were waited for; matrix products, arithmetic and copies ran while one was open for 15% of the time, Pallas kernels for 0%

commit v1 on v0

v1 whole, which is shorter than its diff:
```python
import functools

import jax
import jax.numpy as jnp
from jax import lax
from jax.experimental import pallas as pl
from jax.experimental.pallas import tpu as pltpu
from jax.sharding import PartitionSpec as P

ADAPTER_RANK = 16
SCALE = 2.0


def split2(v):
    high = lax.reduce_precision(v, 8, 7)
    return high.astype(jnp.bfloat16), (v - high).astype(jnp.bfloat16)


def dot32(a, b, dims):
    return lax.dot_general(a, b, (dims, ((), ())), preferred_element_type=jnp.float32)


def general(x, group, slot, job, w, a, b, dy):
    groups = lax.axis_size("dp")
    blocks = group.shape[0]
    rows, features = x.shape
    length = rows // blocks
    columns = dy.shape[1]
    cap = dy.shape[0] // length // groups
    jobs = a.shape[1] // ADAPTER_RANK
    index = group * cap + slot
    got = lax.all_to_all(
        dy.reshape(groups, cap * length, columns), "dp", split_axis=0, concat_axis=0, tiled=True
    )
    dy_home = got.reshape(groups * cap, length, columns)[index].reshape(rows, columns)
    hot = jnp.repeat(job, length)[:, None] == (
        jnp.arange(jobs * ADAPTER_RANK, dtype=jnp.int32) // ADAPTER_RANK
    )

    def of_job(terms):
        kept = jnp.where(hot, terms, 0.0).reshape(rows, jobs, ADAPTER_RANK)
        return jnp.sum(kept, axis=1).T

    def spread(sums):
        return jnp.where(hot, jnp.tile(sums.T, (1, jobs)), 0.0)

    parts = jnp.stack(
        (of_job(dot32(x, a, ((1,), (0,)))), of_job(SCALE * dot32(dy_home, b, ((1,), (1,)))))
    )
    sums = lax.psum(parts, "tensor")
    low, low_grad = spread(sums[0]), spread(sums[1])
    low_hi, low_lo = split2(low)
    grad_hi, grad_lo = split2(low_grad)
    base = lax.psum_scatter(dot32(x, w, ((1,), (0,))), "tensor", scatter_dimension=1, tiled=True)
    adapter = dot32(low_hi, b, ((1,), (0,))) + dot32(low_lo, b, ((1,), (0,)))
    out_home = (base + SCALE * adapter).astype(jnp.bfloat16)
    sent = (
        jnp.zeros((groups * cap, length, columns), jnp.bfloat16)
        .at[index]
        .set(out_home.reshape(blocks, length, columns))
    )
    output = lax.all_to_all(
        sent.reshape(groups, cap * length, columns), "dp", split_axis=0, concat_axis=0, tiled=True
    ).reshape(dy.shape)
    full = lax.all_gather(dy_home, "tensor", axis=1, tiled=True)
    grad_home = (
        dot32(full, w, ((1,), (1,)))
        + dot32(grad_hi, a, ((1,), (1,)))
        + dot32(grad_lo, a, ((1,), (1,)))
    ).astype(jnp.bfloat16)
    a_term = dot32(x, grad_hi, ((0,), (0,))) + dot32(x, grad_lo, ((0,), (0,)))
    b_term = SCALE * (dot32(low_hi, dy_home, ((0,), (0,))) + dot32(low_lo, dy_home, ((0,), (0,))))
    return (
        output,
        grad_home,
        lax.psum_scatter(a_term, "dp", scatter_dimension=1, tiled=True),
        lax.psum_scatter(b_term, "dp", scatter_dimension=0, tiled=True),
    )


def local(*args):
    return general(*args)


def solution(mesh):
    return jax.shard_map(
        local,
        mesh=mesh,
        in_specs=(
            P(("parts", "dp"), "tensor"),
            P(("parts", "dp")),
            P(("parts", "dp")),
            P(("parts", "dp")),
            P("tensor", None),
            P("tensor", None),
            P(None, "tensor"),
            P(("parts", "dp"), "tensor"),
        ),
        out_specs=(
            P(("parts", "dp"), "tensor"),
            P(("parts", "dp"), "tensor"),
            P("tensor", ("parts", "dp")),
            P(("parts", "dp"), "tensor"),
        ),
        check_vma=False,
    )
```

time: 579 us -> 460 us (0.79)
  waiting for transfers between devices: 427 us -> 342 us
  local copies, waits for them, and re-layouts: 37.2 us -> 12.7 us
  blocking collectives: 19.2 us -> 5.62 us
  starting transfers between devices: 10.7 us -> 4.11 us
  other arithmetic: 4.91 us -> 10.9 us
    reduce_scatter x3, waiting for transfers between devices: 247 us -> 185 us  [the longest x1 185 us: general(): lax.psum_scatter(dot32(x, w, ((1,), (0,))), 'tensor', scatter_dimension=1...]
    all_gather x1, waiting for transfers between devices: 102 us -> 83.6 us  [general(): full = lax.all_gather(dy_home, 'tensor', axis=1, tiled=True)]
    all_to_all x1, blocking collectives: 19.2 us -> 5.62 us  [general(): lax.all_to_all(sent.reshape(groups, cap * length, columns), 'dp', split_a...]
    scatter x2 -> x1, local copies, waits for them, and re-layouts: 17 us -> 3.5 us  [general(): sent = jnp.zeros((groups * cap, length, columns), jnp.bfloat16).at[index]...]
    gather x3 -> x1, local copies, waits for them, and re-layouts: 10.1 us -> 1.92 us  [general(): got.reshape(groups * cap, length, columns)[index].reshape(rows, columns)]
    all_to_all x2 -> x1, starting transfers between devices: 10.3 us -> 3.77 us  [general(): lax.all_to_all(dy.reshape(groups, cap * length, columns), 'dp', split_axi...]
    dot_general x10 -> x12, matrix products: 64.2 us -> 69.6 us  [dot32(): lax.dot_general(a, b, (dims, ((), ())), preferred_element_type=jnp.float32)]
  transfers between devices with their start and end apart: 7 -> 6, of which waited for: 5 -> 4; matrix products, arithmetic and copies ran while one was open for 15% -> 13% of each run, Pallas kernels for 0% -> 0%
where the time goes in v1:
time: 460 us; the launch traced here: 459 us
  waiting for transfers between devices  342 us (74%)
  matrix products  69.6 us (15%)
  between operations  14 us (3%)
  local copies, waits for them, and re-layouts  12.7 us (3%)
  other arithmetic  10.9 us (2%)
  blocking collectives  5.62 us (1%)
    reduce_scatter x1, waiting for transfers between devices, general(): lax.psum_scatter(dot32(x, w, ((1,), (0,))), 'tensor', scatter_dimension=1...  185 us
    all_gather x1, waiting for transfers between devices, general(): full = lax.all_gather(dy_home, 'tensor', axis=1, tiled=True)  83.6 us
    psum x1, waiting for transfers between devices, general(): sums = lax.psum(parts, 'tensor')  72.1 us
    dot_general x12, matrix products, dot32(): lax.dot_general(a, b, (dims, ((), ())), preferred_element_type=jnp.float32)  69.6 us
  transfers between devices with their start and end apart: 6, of which 4 were waited for; matrix products, arithmetic and copies ran while one was open for 13% of the time, Pallas kernels for 0%

profile of v1, /device:TPU:1, one launch (start us, length us, event | category | flops | bytes accessed | tf_op | source)
XLA Modules:
  0.0 458.8 jit_solution(16319457976040969084)
XLA Ops:
  7.2 0.0 copy-start
  7.2 3.8 all-to-all-start
  11.0 0.0 all-reduce.2.cloned.1.call-start
  11.0 0.7 compare_select_fusion.4
  11.7 0.7 broadcast_bitcast_fusion
  12.4 0.3 all-to-all-done
  12.7 1.0 copy-done.7
  13.7 1.9 gather_fusion
  15.6 0.0 copy-start.8
  15.6 2.2 compare_select_fusion.2
  17.9 2.7 reduce_sum.19
  20.6 0.0 copy-done.1
  20.6 6.3 %compare_select_fusion.3 = f32[3072,256]{0,1:T(8,128)} fusion(bf16[3072,1024]{1,0:T(8,128)(2,1)} %param.8, bf16[1024,256]{1,0:T(8,128)(2,1)S(1)} %copy-done.8, s32[3072]{0:T(1024)S(1)} %broadcast_bitcast_fusion, s32[256]{0:T(256)S(1)} %and_select_fusion), kind=kOutput, calls=%fused_computation.6 | convolution fusion | flops 1612185600 | bytes 9974784 | tf_op jit(solution)/shard_map/dot_general | solution.py:20
  26.9 2.1 reduce_sum.18
  29.0 0.8 pad_maximum_fusion
  29.8 0.0 all-reduce.2.cloned.1.call-update
  29.8 0.0 reduce-scatter.6.cloned.1.call-start
  29.9 72.1 %all-reduce.2.cloned.1.call-done = f32[2,16,3072]{2,1,0:T(8,128)} async-done(((f32[2,16,3072]{2,1,0:T(8,128)}), f32[2,16,3072]{2,1,0:T(8,128)}) %all-reduce.2.cloned.1.call-update) | async-done | bytes 393232 | tf_op jit(solution)/shard_map/psum | solution.py:50
  102.0 1.0 slice_bitcast_fusion
  103.0 0.0 copy-start.9
  103.0 0.0 slice-start
  103.0 3.0 fusion.4
  106.0 5.7 %fusion.13 = f32[256,1024]{1,0:T(8,128)S(1)} fusion(bf16[3072,256]{0,1:T(8,128)(2,1)S(1)} %get-tuple-element.13, bf16[3072,1024]{1,0:T(8,128)(2,1)} %param.8), kind=kOutput, calls=%fused_computation.44 | convolution fusion | flops 1610612736 | bytes 8912896 | tf_op jit(solution)/shard_map/dot_general | solution.py:20
  111.8 2.8 fusion.6
  114.6 0.0 reduce-scatter.6.cloned.1.call-update
  114.6 0.0 all-gather.2.cloned.1.call-start
  114.7 0.7 all-gather.2.cloned.1.call-update
  115.4 0.0 reduce-scatter.4.cloned.1.call-start
  115.4 12.4 %fusion.9 = f32[3072,1024]{1,0:T(8,128)} fusion(bf16[3072,1024]{1,0:T(8,128)(2,1)} %param.8, bf16[1024,1024]{1,0:T(8,128)(2,1)S(1)} %copy-done), kind=kOutput, calls=%fused_computation.40 | convolution fusion | flops 6442450944 | bytes 20971520 | tf_op jit(solution)/shard_map/dot_general | solution.py:20
  127.8 0.0 reduce-scatter.4.cloned.1.call-update
  127.8 0.2 reduce-scatter.8.cloned.1.call-start
  128.1 1.6 fusion.5
  129.7 0.6 fusion.14
  130.3 1.2 fusion.7
  131.5 3.3 fusion.10
  134.8 6.3 %fusion.12 = f32[3072,1024]{1,0:T(8,128)} fusion(bf16[3072,256]{0,1:T(8,128)(2,1)S(1)} %copy-done.4, bf16[1024,256]{1,0:T(8,128)(2,1)S(1)} %copy-done.8), kind=kOutput, calls=%fused_computation.43 | convolution fusion | flops 1610612736 | bytes 14680064 | tf_op jit(solution)/shard_map/dot_general | solution.py:20
  141.2 0.0 reduce-scatter.8.cloned.1.call-update
  141.2 0.0 reduce-scatter.6.cloned.1.call-done
  141.2 2.0 copy.12
  143.3 83.6 %all-gather.2.cloned.1.call-done = bf16[3072,1024]{1,0:T(8,128)(2,1)} async-done(((bf16[3072,128]{1,0:T(8,128)(2,1)}), bf16[3072,1024]{1,0:T(8,128)(2,1)}) %all-gather.2.cloned.1.call-update) | async-done | bytes 6291472 | tf_op jit(solution)/shard_map/all_gather | solution.py:65
  226.8 12.6 %fusion.11 = f32[3072,1024]{1,0:T(8,128)} fusion(bf16[3072,1024]{1,0:T(8,128)(2,1)} %all-gather.2.cloned.1.call-done, bf16[1024,1024]{1,0:T(8,128)(2,1)S(1)} %copy-done), kind=kOutput, calls=%fused_computation.42 | convolution fusion | flops 6442450944 | bytes 20971520 | tf_op jit(solution)/shard_map/dot_general | solution.py:20
  239.5 12.3 %add_convert_fusion = bf16[3072,1024]{1,0:T(8,128)(2,1)} fusion(f32[3072,1024]{1,0:T(8,128)} %fusion.11, f32[3072,1024]{1,0:T(8,128)} %fusion.12, bf16[3072,256]{0,1:T(8,128)(2,1)S(1)} %copy-done.6, bf16[1024,256]{1,0:T(8,128)(2,1)S(1)} %copy-done.8), kind=kOutput, calls=%fused_computation.2 | convolution fusion | flops 1620049920 | bytes 33554432 | tf_op jit(solution)/shard_map/dot_general | solution.py:20
  251.7 185.1 %reduce-scatter.4.cloned.1.call-done = f32[3072,128]{1,0:T(8,128)} async-done(((f32[3072,1024]{1,0:T(8,128)}), f32[3072,128]{1,0:T(8,128)}) %reduce-scatter.4.cloned.1.call-update) | async-done | bytes 1572880 | tf_op jit(solution)/shard_map/reduce_scatter | solution.py:54
  436.8 3.9 fusion.2
  440.7 0.2 broadcast_in_dim.20
  440.9 3.5 scatter_fusion
  444.4 5.6 %all_to_all.10 = bf16[2,2048,128]{2,1,0:T(8,128)(2,1)} all-to-all(bf16[2,2048,128]{2,1,0:T(8,128)(2,1)S(1)} %bitcast.69), channel_id=1, replica_groups=mesh['parts'=2,'dp'=2,'tensor'=8] {'dp'}, dimensions={0} | all-to-all | bytes 2097152 | tf_op jit(solution)/shard_map/all_to_all | solution.py:62
  450.0 2.3 copy.16
  (27 shorter events, 0.1 us)
Async XLA Ops:
  7.2 108.3 %copy-start = (bf16[1024,1024]{1,0:T(8,128)(2,1)S(1)}, bf16[1024,1024]{1,0:T(8,128)(2,1)}, u32[]{:S(2)}) copy-start(bf16[1024,1024]{1,0:T(8,128)(2,1)} %param.12) | copy-start | bytes 6291460
  7.2 8.4 %copy-start.11 = (bf16[256,128]{1,0:T(8,128)(2,1)S(1)}, bf16[256,128]{1,0:T(8,128)(2,1)}, u32[]{:S(2)}) copy-start(bf16[256,128]{1,0:T(8,128)(2,1)} %param.14) | copy-start | bytes 196612
  7.2 5.5 %all-to-all-start = ((bf16[2,2048,128]{2,1,0:T(8,128)(2,1)}), bf16[2,2048,128]{2,1,0:T(8,128)(2,1)S(1)}, u32[]{:S(2)}, u32[]{:S(2)}) async-start(bf16[2,2048,128]{2,1,0:T(8,128)(2,1)} %bitcast.76), calls=%async_computation.1 | async-start | bytes 2097152 | tf_op jit(solution)/shard_map/all_to_all | solution.py:32
  11.0 91.0 %all-reduce.2.cloned.1.call-start = ((), (), s32[]{:S(2)}) async-start(), calls=%async_computation.6 | async-start | bytes 786432 | tf_op jit(solution)/shard_map/psum | solution.py:50
  12.7 1.0 copy-start.7
  15.6 5.0 %copy-start.1 = (bf16[24,128,128]{2,1,0:T(8,128)(2,1)}, bf16[24,128,128]{2,1,0:T(8,128)(2,1)S(1)}, u32[]{:S(2)}) copy-start(bf16[24,128,128]{2,1,0:T(8,128)(2,1)S(1)} %gather_fusion) | copy-start | bytes 2359300
  15.6 5.0 %copy-start.8 = (bf16[1024,256]{1,0:T(8,128)(2,1)S(1)}, bf16[1024,256]{1,0:T(8,128)(2,1)}, u32[]{:S(2)}) copy-start(bf16[1024,256]{1,0:T(8,128)(2,1)} %param.13) | copy-start | bytes 1572868
  26.9 2.1 copy-start.10
  29.8 111.4 %reduce-scatter.6.cloned.1.call-start = ((), (), s32[]{:S(2)}) async-start(), calls=%async_computation.8 | async-start | bytes 1572864 | tf_op jit(solution)/shard_map/reduce_scatter | solution.py:76
  103.0 3.0 copy-start.9
  103.0 8.8 %slice-start = ((s8[6291456]{0:T(1024)(128)(4,1)}), s8[2097152]{0:T(1024)(128)(4,1)S(1)}, s32[]{:S(2)}) async-start(s8[6291456]{0:T(1024)(128)(4,1)} %bitcast.79), calls=%async_computation.10 | async-start | bytes 4194304
  106.0 5.8 %copy-start.3 = (bf16[3072,256]{0,1:T(8,128)(2,1)}, bf16[3072,256]{0,1:T(8,128)(2,1)S(1)}, u32[]{:S(2)}) copy-start(bf16[3072,256]{0,1:T(8,128)(2,1)S(1)} %get-tuple-element.13) | copy-start | bytes 4718596
  106.0 5.8 %copy-start.5 = (bf16[3072,256]{0,1:T(8,128)(2,1)}, bf16[3072,256]{0,1:T(8,128)(2,1)S(1)}, u32[]{:S(2)}) copy-start(bf16[3072,256]{0,1:T(8,128)(2,1)S(1)} %get-tuple-element.12) | copy-start | bytes 4718596
  106.0 5.8 %slice-start.1 = ((s8[6291456]{0:T(1024)(128)(4,1)}), s8[4194304]{0:T(1024)(128)(4,1)S(1)}, s32[]{:S(2)}) async-start(s8[6291456]{0:T(1024)(128)(4,1)} %bitcast.79), calls=%async_computation.11 | async-start | bytes 8388608
  114.6 112.2 %all-gather.2.cloned.1.call-start = ((), (), s32[]{:S(2)}) async-start(), calls=%async_computation.7 | async-start | bytes 7077888 | tf_op jit(solution)/shard_map/all_gather | solution.py:65
  115.4 321.4 %reduce-scatter.4.cloned.1.call-start = ((), (), s32[]{:S(2)}) async-start(), calls=%async_computation.5 | async-start | bytes 14155776 | tf_op jit(solution)/shard_map/reduce_scatter | solution.py:54
  127.8 1.9 copy-start.2
  127.8 322.2 %reduce-scatter.8.cloned.1.call-start = ((), (), s32[]{:S(2)}) async-start(), calls=%async_computation.9 | async-start | bytes 196608 | tf_op jit(solution)/shard_map/reduce_scatter | solution.py:77
  131.5 3.3 copy-start.4
  226.8 12.6 %copy-start.6 = (bf16[3072,256]{0,1:T(8,128)(2,1)S(1)}, bf16[3072,256]{0,1:T(8,128)(2,1)}, u32[]{:S(2)}) copy-start(bf16[3072,256]{0,1:T(8,128)(2,1)} %copy-done.5) | copy-start | bytes 4718596
Sparse Core Ops, SparseCore 0:
  29.9 71.9 all-reduce.1
  114.8 9.6 reduce-scatter.5
  126.5 100.2 all-gather.1
  230.3 206.4 reduce-scatter.3
  439.4 6.9 reduce-scatter.7

commit v2 on v1

--- a/solution.py
+++ b/solution.py
@@ -77,9 +77,425 @@
         lax.psum_scatter(b_term, "dp", scatter_dimension=0, tiled=True),
     )
 
+RANGE = 32766.0
+STEPS = 64.0
+PAD = 16
+VMEM_BYTES = 56 * 1024 * 1024
+
+
+def params():
+    return pltpu.CompilerParams(vmem_limit_bytes=VMEM_BYTES)
+
+
+def cost(flops, read):
+    return pl.CostEstimate(flops=flops, bytes_accessed=read, transcendentals=0)
+
+
+def halves(v):
+    high = v.astype(jnp.bfloat16)
+    return high, (v - high.astype(jnp.float32)).astype(jnp.bfloat16)
+
+
+def store_coded(out_ref, v):
+    rows = v.shape[0]
+    top = jnp.maximum(jnp.max(jnp.abs(v), axis=0, keepdims=True), 1e-30)
+    level = jnp.ceil(jnp.log2(top) * STEPS)
+    coded = jnp.round(v * (jnp.exp2(level * (-1.0 / STEPS)) * (RANGE * 0.9999)))
+    out_ref[0, pl.ds(0, rows), :] = coded.astype(jnp.int32).astype(jnp.int16)
+    out_ref[0, pl.ds(rows, PAD), :] = (
+        jnp.broadcast_to(level, (PAD, v.shape[1])).astype(jnp.int32).astype(jnp.int16)
+    )
+
+
+def load_coded(in_ref):
+    rows = in_ref.shape[1] - PAD
+    level = in_ref[0, pl.ds(rows, PAD), :].astype(jnp.int32).astype(jnp.float32)[0:1, :]
+    coded = in_ref[0, pl.ds(0, rows), :].astype(jnp.int32).astype(jnp.float32)
+    return coded * (jnp.exp2(level * (1.0 / STEPS)) * (1.0 / (RANGE * 0.9999)))
+
+
+def coded_spec(group_rows, columns):
+    return pl.BlockSpec((1, group_rows + PAD, columns), lambda g, *_: (g, 0, 0))
+
+
+def coded_shape(rows, group_rows, columns):
+    return jax.ShapeDtypeStruct((rows // group_rows, group_rows + PAD, columns), jnp.int16)
+
+
+def project(x, w, place, offsets, group_rows, columns, coded):
+    rows, features = x.shape
+    count = len(offsets)
+
+    def kernel(place_ref, x_ref, *refs):
+        weights = jnp.concatenate([r[...] for r in refs[:count]], axis=1)
+        product = dot32(x_ref[...], weights, ((1,), (0,)))
+        for i in range(count):
+            part = product[:, i * columns : (i + 1) * columns]
+            if coded:
+                store_coded(refs[count + i], part)
+            else:
+                refs[count + i][...] = part
+
+    def weight_spec(d):
+        return pl.BlockSpec((features, columns), lambda g, place_ref: (0, place_ref[d]))
+
+    if coded:
+        out_specs = [coded_spec(group_rows, columns)] * count
+        out_shape = [coded_shape(rows, group_rows, columns)] * count
+    else:
+        out_specs = [pl.BlockSpec((group_rows, columns), lambda g, place_ref: (g, 0))] * count
+        out_shape = [jax.ShapeDtypeStruct((rows, columns), jnp.float32)] * count
+    return pl.pallas_call(
+        kernel,
+        grid_spec=pltpu.PrefetchScalarGridSpec(
+            num_scalar_prefetch=1,
+            grid=(rows // group_rows,),
+            in_specs=[pl.BlockSpec((group_rows, features), lambda g, place_ref: (g, 0))]
+            + [weight_spec(d) for d in offsets],
+            out_specs=out_specs,
+        ),
+        out_shape=out_shape,
+        compiler_params=params(),
+        cost_estimate=cost(
+            2 * rows * features * columns * count, rows * features * 2 + rows * columns * 4 * count
+        ),
+        name="project",
+    )(place, x, *([w] * count))
+
+
+def add_coded(own, received, group_rows):
+    rows, columns = own.shape
+
+    def kernel(own_ref, received_ref, out_ref):
+        store_coded(out_ref, own_ref[...] + load_coded(received_ref))
+
+    return pl.pallas_call(
+        kernel,
+        grid=(rows // group_rows,),
+        in_specs=[
+            pl.BlockSpec((group_rows, columns), lambda g: (g, 0)),
+            coded_spec(group_rows, columns),
+        ],
+        out_specs=coded_spec(group_rows, columns),
+        out_shape=coded_shape(rows, group_rows, columns),
+        compiler_params=params(),
+        cost_estimate=cost(rows * columns, rows * columns * 8),
+        name="add_coded",
+    )(own, received)
+
+
+SMEM = pl.BlockSpec(memory_space=pltpu.SMEM)
+VMEM = pl.BlockSpec(memory_space=pltpu.VMEM)
+
+
+def home_gradient(kept, received, b, group, slot, job, me, length):
+    blocks = group.shape[0]
+    columns = b.shape[1]
+
+    def kernel(group_ref, slot_ref, job_ref, me_ref, kept_ref, received_ref, b_ref, dy_ref, low_ref):
+        mine = me_ref[0]
+        for n in range(blocks):
+            at = pl.ds(pl.multiple_of(slot_ref[n] * length, length), length)
+
+            @pl.when(group_ref[n] == mine)
+            def _():
+                dy_ref[pl.ds(n * length, length), :] = kept_ref[at, :]
+
+            @pl.when(group_ref[n] != mine)
+            def _():
+                dy_ref[pl.ds(n * length, length), :] = received_ref[at, :]
+
+            factor = b_ref[
+                pl.ds(pl.multiple_of(job_ref[n] * ADAPTER_RANK, ADAPTER_RANK), ADAPTER_RANK), :
+            ]
+            low_ref[n] = SCALE * dot32(
+                factor, dy_ref[pl.ds(n * length, length), :], ((1,), (1,))
+            )
+
+    return pl.pallas_call(
+        kernel,
+        in_specs=[SMEM] * 4 + [VMEM] * 3,
+        out_specs=[VMEM, VMEM],
+        out_shape=[
+            jax.ShapeDtypeStruct((blocks * length, columns), jnp.bfloat16),
+            jax.ShapeDtypeStruct((blocks, ADAPTER_RANK, length), jnp.float32),
+        ],
+        compiler_params=params(),
+        cost_estimate=cost(2 * blocks * length * columns * ADAPTER_RANK, 4 * kept.size * 2),
+        name="home_gradient",
+    )(group, slot, job, me, kept, received, b)
+
+
+def low_rank(x, a_t, job, length, step_blocks):
+    blocks = job.shape[0]
+    features = x.shape[1]
+
+    def kernel(job_ref, x_ref, a_ref, low_ref):
+        first = pl.program_id(0) * step_blocks
+        for i in range(step_blocks):
+            factor = a_ref[
+                pl.ds(
+                    pl.multiple_of(job_ref[first + i] * ADAPTER_RANK, ADAPTER_RANK), ADAPTER_RANK
+                ),
+                :,
+            ]
+            low_ref[i] = dot32(factor, x_ref[pl.ds(i * length, length), :], ((1,), (1,)))
+
+    return pl.pallas_call(
+        kernel,
+        grid_spec=pltpu.PrefetchScalarGridSpec(
+            num_scalar_prefetch=1,
+            grid=(blocks // step_blocks,),
+            in_specs=[
+                pl.BlockSpec((step_blocks * length, features), lambda g, job_ref: (g, 0)),
+                pl.BlockSpec(a_t.shape, lambda g, job_ref: (0, 0)),
+            ],
+            out_specs=pl.BlockSpec(
+                (step_blocks, ADAPTER_RANK, length), lambda g, job_ref: (g, 0, 0)
+            ),
+        ),
+        out_shape=jax.ShapeDtypeStruct((blocks, ADAPTER_RANK, length), jnp.float32),
+        compiler_params=params(),
+        cost_estimate=cost(2 * x.size * ADAPTER_RANK, x.size * 2),
+        name="low_rank",
+    )(job, x, a_t)
+
+
+def factor_gradients(x, dy_home, low, low_grad, job, jobs, length, step_blocks):
+    blocks = job.shape[0]
+    features = x.shape[1]
+    columns = dy_home.shape[1]
+
+    def kernel(job_ref, x_ref, dy_ref, low_ref, grad_ref, out_ref):
+        step = pl.program_id(0)
+
+        @pl.when(step == 0)
+        def _():
+            out_ref[...] = jnp.zeros_like(out_ref)
+
+        for i in range(step_blocks):
+            at = pl.ds(
+                pl.multiple_of(job_ref[step * step_blocks + i] * ADAPTER_RANK, ADAPTER_RANK),
+                ADAPTER_RANK,
+            )
+            here = pl.ds(i * length, length)
+            terms = dot32(
+                jnp.concatenate(halves(grad_ref[i]), axis=0), x_ref[here, :], ((1,), (0,))
+            )
+            out_ref[at, pl.ds(0, features)] += terms[:ADAPTER_RANK] + terms[ADAPTER_RANK:]
+            terms = dot32(
+                jnp.concatenate(halves(SCALE * low_ref[i]), axis=0), dy_ref[here, :], ((1,), (0,))
+            )
+            out_ref[at, pl.ds(features, columns)] += terms[:ADAPTER_RANK] + terms[ADAPTER_RANK:]
+
+    low_spec = pl.BlockSpec((step_blocks, ADAPTER_RANK, length), lambda g, job_ref: (g, 0, 0))
+    shape = (jobs * ADAPTER_RANK, features + columns)
+    return pl.pallas_call(
+        kernel,
+        grid_spec=pltpu.PrefetchScalarGridSpec(
+            num_scalar_prefetch=1,
+            grid=(blocks // step_blocks,),
+            in_specs=[
+                pl.BlockSpec((step_blocks * length, features), lambda g, job_ref: (g, 0)),
+                pl.BlockSpec((step_blocks * length, columns), lambda g, job_ref: (g, 0)),
+                low_spec,
+                low_spec,
+            ],
+            out_specs=pl.BlockSpec(shape, lambda g, job_ref: (0, 0)),
+        ),
+        out_shape=jax.ShapeDtypeStruct(shape, jnp.float32),
+        compiler_params=params(),
+        cost_estimate=cost(8 * x.size * ADAPTER_RANK, x.size * 2),
+        name="factor_gradients",
+    )(job, x, dy_home, low, low_grad)
+
+
+def place_output(own, from_left, from_right, low, b, group, slot, job, me, length, cap):
+    blocks = group.shape[0]
+    columns = b.shape[1]
+    group_rows = from_left.shape[1] - PAD
+    per_group = group_rows // length
+
+    def kernel(
+        group_ref, slot_ref, job_ref, me_ref, own_ref, left_ref, right_ref, low_ref, b_ref, out_ref
+    ):
+        out_ref[...] = jnp.zeros_like(out_ref)
+        for g in range(blocks // per_group):
+            scales = []
+            for ref in (left_ref, right_ref):
+                level = ref[g, pl.ds(group_rows, PAD), :].astype(jnp.int32).astype(jnp.float32)
+                scales.append(
+                    jnp.exp2(level[0:1, :] * (1.0 / STEPS)) * (1.0 / (RANGE * 0.9999))
+                )
+            for i in range(per_group):
+                n = g * per_group + i
+                total = own_ref[pl.ds(n * length, length), :]
+                for ref, scale in zip((left_ref, right_ref), scales):
+                    coded = ref[g, pl.ds(i * length, length), :].astype(jnp.int32)
+                    total = total + coded.astype(jnp.float32) * scale
+                factor = b_ref[
+                    pl.ds(pl.multiple_of(job_ref[n] * ADAPTER_RANK, ADAPTER_RANK), ADAPTER_RANK), :
+                ]
+                high, rest = halves((SCALE * low_ref[n]).T)
+                total = total + (
+                    dot32(high, factor, ((1,), (0,))) + dot32(rest, factor, ((1,), (0,)))
+                )
+                other = jnp.where(group_ref[n] == me_ref[0], 0, 1)
+                out_ref[other * cap + slot_ref[n]] = total.astype(jnp.bfloat16)
+
+    return pl.pallas_call(
+        kernel,
+        in_specs=[SMEM] * 4 + [VMEM] * 5,
+        out_specs=VMEM,
+        out_shape=jax.ShapeDtypeStruct((2 * cap, length, columns), jnp.bfloat16),
+        compiler_params=params(),
+        cost_estimate=cost(own.size * 64, own.size * 10),
+        name="place_output",
+    )(group, slot, job, me, own, from_left, from_right, low, b)
+
+
+def input_gradient(pieces, w_rows, low_grad, a_t, job, length, step_blocks):
+    blocks = job.shape[0]
+    columns = pieces[0].shape[1]
+    features = a_t.shape[1]
+    count = len(pieces)
+
+    def kernel(job_ref, *refs):
+        w_ref, grad_ref, a_ref, out_ref = refs[count:]
+        lhs = jnp.concatenate([r[...] for r in refs[:count]], axis=1)
+        total = dot32(lhs, w_ref[...], ((1,), (0,)))
+        for i in range(step_blocks):
+            n = pl.program_id(0) * step_blocks + i
+            factor = a_ref[
+                pl.ds(pl.multiple_of(job_ref[n] * ADAPTER_RANK, ADAPTER_RANK), ADAPTER_RANK), :
+            ]
+            high, rest = halves(grad_ref[i].T)
+            here = slice(i * length, (i + 1) * length)
+            out_ref[pl.ds(i * length, length), :] = (
+                total[here]
+                + (dot32(high, factor, ((1,), (0,))) + dot32(rest, factor, ((1,), (0,))))
+            ).astype(jnp.bfloat16)
+
+    rows = blocks * length
+    step_rows = step_blocks * length
+    return pl.pallas_call(
+        kernel,
+        grid_spec=pltpu.PrefetchScalarGridSpec(
+            num_scalar_prefetch=1,
+            grid=(blocks // step_blocks,),
+            in_specs=[pl.BlockSpec((step_rows, columns), lambda g, job_ref: (g, 0))] * count
+            + [
+                pl.BlockSpec(w_rows.shape, lambda g, job_ref: (0, 0)),
+                pl.BlockSpec(
+                    (step_blocks, ADAPTER_RANK, length), lambda g, job_ref: (g, 0, 0)
+                ),
+                pl.BlockSpec(a_t.shape, lambda g, job_ref: (0, 0)),
+            ],
+            out_specs=pl.BlockSpec((step_rows, features), lambda g, job_ref: (g, 0)),
+        ),
+        out_shape=jax.ShapeDtypeStruct((rows, features), jnp.bfloat16),
+        compiler_params=params(),
+        cost_estimate=cost(2 * rows * features * columns * count, rows * features * 4),
+        name="input_gradient",
+    )(job, *pieces, w_rows, low_grad, a_t)
+
+
+def ring(x, group, slot, job, w, a, b, dy):
+    size = lax.axis_size("tensor")
+    me = lax.axis_index("dp").astype(jnp.int32)
+    blocks = group.shape[0]
+    rows, features = x.shape
+    length = rows // blocks
+    columns = dy.shape[1]
+    half = dy.shape[0] // 2
+    cap = half // length
+    jobs = a.shape[1] // ADAPTER_RANK
+    step_blocks = 8
+    group_rows = step_blocks * length
+
+    order = [2 * r for r in range(size // 2)] + [2 * r + 1 for r in reversed(range(size // 2))]
+    place_of = [order.index(t) for t in range(size)]
+    here = jnp.asarray(place_of, jnp.int32)[lax.axis_index("tensor")]
+    place = jnp.asarray(order, jnp.int32)[(here + jnp.arange(size, dtype=jnp.int32)) % size]
+    ahead = [(order[r], order[(r + 1) % size]) for r in range(size)]
+    back = [(order[r], order[(r - 1) % size]) for r in range(size)]
+    swap = [(0, 1), (1, 0)]
+
+    def right(v):
+        return lax.ppermute(v, "tensor", ahead)
+
+    def left(v):
+        return lax.ppermute(v, "tensor", back)
+
+    mine = me[None]
+    kept = lax.dynamic_slice_in_dim(dy, me * half, half)
+    got = lax.ppermute(lax.dynamic_slice_in_dim(dy, (1 - me) * half, half), "dp", swap)
+
+    far, near = size // 2, size // 2 - 1
+    sums_r, sums_l = project(x, w, place, (far, size - near), group_rows, columns, True)
+    sums_r = right(sums_r)
+    sums_l = left(sums_l)
+    dy_home, low_grad = home_gradient(kept, got, b, group, slot, job, mine, length)
+    held_r = right(dy_home)
+    held_l = left(dy_home)
+    a_t = a.T
+    low = low_rank(x, a_t, job, length, step_blocks)
+    low, low_grad = lax.psum((low, low_grad), "tensor")
+
+    offsets = []
+    for d in range(1, far):
+        offsets += [far - d] + ([size - (near - d)] if near > d else [])
+    offsets += [0]
+    terms = dict(zip(offsets, project(x, w, place, tuple(offsets), group_rows, columns, False)))
+
+    pieces = {0: dy_home, size - 1: held_r, 1: held_l}
+    for d in range(1, far):
+        sums_r = right(add_coded(terms[far - d], sums_r, group_rows))
+        if near > d:
+            sums_l = left(add_coded(terms[size - (near - d)], sums_l, group_rows))
+        if d < near:
+            held_r = right(held_r)
+            pieces[size - 1 - d] = held_r
+        held_l = left(held_l)
+        pieces[1 + d] = held_l
+
+    factors = factor_gradients(x, dy_home, low, low_grad, job, jobs, length, step_blocks)
+    part = factors.shape[0] // 2
+    theirs = lax.ppermute(lax.dynamic_slice_in_dim(factors, (1 - me) * part, part), "dp", swap)
+    factors = lax.dynamic_slice_in_dim(factors, me * part, part) + theirs
+
+    placed = place_output(
+        terms[0], sums_r, sums_l, low, b, group, slot, job, mine, length, cap
+    ).reshape(2, half, columns)
+    theirs = lax.ppermute(placed[1], "dp", swap)
+    output = jnp.where(
+        me == 0,
+        jnp.concatenate((placed[0], theirs)),
+        jnp.concatenate((theirs, placed[0])),
+    )
+
+    w_rows = w.T.reshape(size, columns, features)[place].reshape(size * columns, features)
+    grad_home = input_gradient(
+        [pieces[d] for d in range(size)], w_rows, low_grad, a_t, job, length, step_blocks // 2
+    )
+    return output, grad_home, factors[:, :features].T, factors[:, features:]
+
 
 def local(*args):
-    return general(*args)
+    x, group, dy = args[0], args[1], args[7]
+    size = lax.axis_size("tensor")
+    blocks = group.shape[0]
+    length = x.shape[0] // blocks
+    fits = (
+        lax.axis_size("dp") == 2
+        and size % 2 == 0
+        and 4 <= size <= 8
+        and dy.shape[1] % 128 == 0
+        and x.shape[1] % 128 == 0
+        and length % 128 == 0
+        and blocks % 8 == 0
+    )
+    return ring(*args) if fits else general(*args)
 
 
 def solution(mesh):

time: 460 us -> 214 us (0.47)
  waiting for transfers between devices: 342 us -> 77.6 us
  Pallas kernels: 0 us -> 71.4 us
  matrix products: 69.6 us -> 0 us
  starting transfers between devices: 4.11 us -> 22.8 us
  local copies, waits for them, and re-layouts: 12.7 us -> 21.2 us
  other arithmetic: 10.9 us -> 3.06 us
  blocking collectives: 5.62 us -> 0 us
    reduce_scatter x3 -> x0, waiting for transfers between devices: 185 us -> none  [the longest x1 185 us: general(): lax.psum_scatter(dot32(x, w, ((1,), (0,))), 'tensor', scatter_dimension=1...]
    all_gather x1 -> x0, waiting for transfers between devices: 83.6 us -> none  [general(): full = lax.all_gather(dy_home, 'tensor', axis=1, tiled=True)]
    pallas_call x0 -> x12, Pallas kernels: none -> 71.4 us  [the longest x5 17.6 us: add_coded(): pl.pallas_call(kernel, grid=(rows // group_rows,), in_specs=[pl.BlockSpec...]
    dot_general x12 -> x0, matrix products: 69.6 us -> none  [dot32(): lax.dot_general(a, b, (dims, ((), ())), preferred_element_type=jnp.float32)]
    ppermute x0 -> x17, starting transfers between devices: none -> 22.8 us  [the longest x7 8.43 us: right(): return lax.ppermute(v, 'tensor', ahead)]
    ppermute x0 -> x17, waiting for transfers between devices: none -> 22.7 us  [the longest x7 18.5 us: left(): return lax.ppermute(v, 'tensor', back)]
    psum x1, waiting for transfers between devices: 72.1 us -> 54.8 us  [ring(): low, low_grad = lax.psum((low, low_grad), 'tensor')]
    all_to_all x1 -> x0, blocking collectives: 5.62 us -> none  [general(): lax.all_to_all(sent.reshape(groups, cap * length, columns), 'dp', split_a...]
  transfers between devices with their start and end apart: 6 -> 18, of which waited for: 4 -> 7; matrix products, arithmetic and copies ran while one was open for 13% -> 7% of each run, Pallas kernels for 0% -> 34%
where the time goes in v2:
time: 214 us; the launch traced here: 210 us
  waiting for transfers between devices  77.6 us (36%)
  Pallas kernels  71.4 us (33%)
  starting transfers between devices  22.8 us (11%)
  local copies, waits for them, and re-layouts  21.2 us (10%)
  between operations  14.2 us (7%)
  other arithmetic  3.06 us (1%)
    psum x1, waiting for transfers between devices, ring(): low, low_grad = lax.psum((low, low_grad), 'tensor')  54.8 us
    ppermute x7, waiting for transfers between devices, left(): return lax.ppermute(v, 'tensor', back)  18.5 us
    pallas_call x5, Pallas kernels, add_coded(): pl.pallas_call(kernel, grid=(rows // group_rows,), in_specs=[pl.BlockSpec...  17.6 us
    pallas_call x2, Pallas kernels, project(): pl.pallas_call(kernel, grid_spec=pltpu.PrefetchScalarGridSpec(num_scalar_...  17 us
    pallas_call x1, Pallas kernels, input_gradient(): pl.pallas_call(kernel, grid_spec=pltpu.PrefetchScalarGridSpec(num_scalar_...  14.9 us
    ppermute x7, starting transfers between devices, right(): return lax.ppermute(v, 'tensor', ahead)  8.43 us
    unnamed x30, local copies, waits for them, and re-layouts  7.98 us
    ppermute x1, starting transfers between devices, ring(): theirs = lax.ppermute(placed[1], 'dp', swap)  6.8 us
  transfers between devices with their start and end apart: 18, of which 7 were waited for; matrix products, arithmetic and copies ran while one was open for 7% of the time, Pallas kernels for 34%

profile of v2, /device:TPU:1, one launch (start us, length us, event | category | flops | bytes accessed | tf_op | source)
XLA Modules:
  0.0 210.2 jit_solution(9144288888954132774)
XLA Ops:
  7.2 2.1 constant_dynamic-slice_fusion.1
  9.4 0.6 dynamic_slice.15
  10.0 0.7 fusion.1
  10.6 1.2 gather_fusion
  11.8 6.6 %project.3 = (s16[3,1040,128]{2,1,0:T(8,128)(2,1)}, s16[3,1040,128]{2,1,0:T(8,128)(2,1)}) custom-call(s32[8]{0:T(128)} %gather_fusion, bf16[3072,1024]{1,0:T(8,128)(2,1)} %x_ref.7, bf16[1024,1024]{1,0:T(8,128)(2,1)} %refs_1_.3, bf16[1024,1024]{1,0:T(8,128)(2,1)} %refs_1_.3), custom_call_target="tpu_custom_call" | custom-call | flops 1610612736 | bytes 9437184 | tf_op jit(solution)/shard_map/project/pallas_call | solution.py:148
  18.3 2.7 %collective-permute-start = (s16[3,1040,128]{2,1,0:T(8,128)(2,1)}, s16[3,1040,128]{2,1,0:T(8,128)(2,1)S(1)}, u32[]{:S(2)}, u32[]{:S(2)}) collective-permute-start(s16[3,1040,128]{2,1,0:T(8,128)(2,1)} %get-tuple-element.18), channel_id=1, source_target_pairs={{0,2},{2,4},{4,6},{6,7},{7,5},{5,3},{3,1},{1,0},{8,10},{10,12},{12... | collective-permute-start | bytes 2396168 | tf_op jit(solution)/shard_map/ppermute | solution.py:425
  21.1 0.8 copy-done.10
  21.9 5.7 %home_gradient.1 = (bf16[3072,128]{1,0:T(8,128)(2,1)}, f32[24,16,128]{2,1,0:T(8,128)}) custom-call(s32[24]{0:T(128)} %group_ref.3, s32[24]{0:T(128)} %slot_ref.3, s32[24]{0:T(128)} %job_ref.9, s32[1]{0:T(128)} %bitcast.me_ref, bf16[2048,128]{1,0:T(8,128)(2,1)} %get-tuple-element.37.kept_ref, bf16[2048,128]{1,0:T(8,128)(2,1)} %copy-done.10, ...), custom_call_target="tpu_custom_call" | custom-call | flops 12582912 | bytes 2097152 | tf_op jit(solution)/shard_map/home_gradient/pallas_call | solution.py:215
  27.6 1.4 collective-permute-start.4
  29.0 10.5 %project.2 = (f32[3072,128]{1,0:T(8,128)}, f32[3072,128]{1,0:T(8,128)}, f32[3072,128]{1,0:T(8,128)}, f32[3072,128]{1,0:T(8,128)}, f32[3072,128]{1,0:T(8,128)}, /*index=5*/f32[3072,128]{1,0:T(8,128)}) custom-call(s32[8]{0:T(128)} %gather_fusion, bf16[3072,1024]{1,0:T(8,128)(2,1)} %x_ref.7, bf16[1024,1024]{1,0:T(8,128)(2,1)} %refs_1_.3, ...), custom_call_target="tpu_custom_call" | custom-call | flops 4831838208 | bytes 15728640 | tf_op jit(solution)/shard_map/project/pallas_call | solution.py:148
  39.5 0.9 copy-done.7
  40.4 3.5 %add_coded.5 = s16[3,1040,128]{2,1,0:T(8,128)(2,1)} custom-call(f32[3072,128]{1,0:T(8,128)} %get-tuple-element.17.own_ref, s16[3,1040,128]{2,1,0:T(8,128)(2,1)} %copy-done.7), custom_call_target="tpu_custom_call" | custom-call | flops 393216 | bytes 3145728 | tf_op jit(solution)/shard_map/add_coded/pallas_call | solution.py:172
  43.9 1.3 collective-permute-start.1
  45.2 1.3 collective-permute-start.13
  47.0 1.0 copy.16
  48.0 5.9 %low_rank.1 = f32[24,16,128]{2,1,0:T(8,128)} custom-call(s32[24]{0:T(128)} %job_ref.9, bf16[3072,1024]{1,0:T(8,128)(2,1)} %x_ref.7, bf16[256,1024]{1,0:T(8,128)(2,1)} %bitcast.20), custom_call_target="tpu_custom_call" | custom-call | flops 100663296 | bytes 6291456 | tf_op jit(solution)/shard_map/low_rank/pallas_call | solution.py:244
  53.9 9.7 %collective-permute-done.4.received_ref = s16[3,1040,128]{2,1,0:T(8,128)(2,1)S(1)} collective-permute-done((s16[3,1040,128]{2,1,0:T(8,128)(2,1)}, s16[3,1040,128]{2,1,0:T(8,128)(2,1)S(1)}, u32[]{:S(2)}, u32[]{:S(2)}) %collective-permute-start.4) | collective-permute-done | bytes 798752 | tf_op jit(solution)/shard_map/ppermute | solution.py:428
  63.7 0.9 copy-done.5
  64.6 3.5 %add_coded.8 = s16[3,1040,128]{2,1,0:T(8,128)(2,1)} custom-call(f32[3072,128]{1,0:T(8,128)} %get-tuple-element.20.own_ref, s16[3,1040,128]{2,1,0:T(8,128)(2,1)} %copy-done.5), custom_call_target="tpu_custom_call" | custom-call | flops 393216 | bytes 3145728 | tf_op jit(solution)/shard_map/add_coded/pallas_call | solution.py:172
  68.4 0.9 copy-done.6
  69.3 3.5 %add_coded.6 = s16[3,1040,128]{2,1,0:T(8,128)(2,1)} custom-call(f32[3072,128]{1,0:T(8,128)} %get-tuple-element.16.own_ref, s16[3,1040,128]{2,1,0:T(8,128)(2,1)} %copy-done.6), custom_call_target="tpu_custom_call" | custom-call | flops 393216 | bytes 3145728 | tf_op jit(solution)/shard_map/add_coded/pallas_call | solution.py:172
  72.8 1.1 collective-permute-start.2
  73.9 54.8 %all-reduce.3.cloned.1.call-done = (f32[24,16,128]{2,1,0:T(8,128)}, f32[24,16,128]{2,1,0:T(8,128)}) async-done(((f32[24,16,128]{2,1,0:T(8,128)}, f32[24,16,128]{2,1,0:T(8,128)}), (f32[24,16,128]{2,1,0:T(8,128)}, f32[24,16,128]{2,1,0:T(8,128)})) %all-reduce.3.cloned.1.call-update) | async-done | bytes 393232 | tf_op jit(solution)/shard_map/psum | solution.py:443
  128.8 6.3 %factor_gradients.1 = f32[256,1152]{1,0:T(8,128)} custom-call(s32[24]{0:T(128)} %job_ref.9, bf16[3072,1024]{1,0:T(8,128)(2,1)} %x_ref.7, bf16[3072,128]{1,0:T(8,128)(2,1)} %get-tuple-element.22.refs_0_.dy_ref, f32[24,16,128]{2,1,0:T(8,128)} %get-tuple-element.32.low_ref, f32[24,16,128]{2,1,0:T(8,128)} %get-tuple-element.33.refs_9_.grad_ref), custom_call_target="tpu_custom_call" | custom-call | flops 402653184 | bytes 6291456 | tf_op jit(solution)/shard_map/factor_gradients/pallas_call | solution.py:293
  135.1 0.5 collective-permute-start.14
  135.6 1.0 collective-permute-start.11
  136.6 1.1 constant_dynamic-slice_fusion
  137.7 3.1 %collective-permute-start.16 = (f32[128,1152]{1,0:T(8,128)S(1)}, f32[128,1152]{1,0:T(8,128)}, u32[]{:S(2)}, u32[]{:S(2)}) collective-permute-start(f32[128,1152]{1,0:T(8,128)S(1)} %constant_dynamic-slice_fusion), channel_id=1, source_target_pairs={{0,8},{8,0},{1,9},{9,1},{2,10},{10,2},{3,11},{11,3},{4,12},{12,4},... | collective-permute-start | bytes 1769480 | tf_op jit(solution)/shard_map/ppermute | solution.py:464
  140.8 0.9 copy-done.4
  141.7 3.5 %add_coded.9 = s16[3,1040,128]{2,1,0:T(8,128)(2,1)} custom-call(f32[3072,128]{1,0:T(8,128)} %get-tuple-element.19.own_ref, s16[3,1040,128]{2,1,0:T(8,128)(2,1)} %copy-done.4), custom_call_target="tpu_custom_call" | custom-call | flops 393216 | bytes 3145728 | tf_op jit(solution)/shard_map/add_coded/pallas_call | solution.py:172
  145.6 3.6 %add_coded.7 = s16[3,1040,128]{2,1,0:T(8,128)(2,1)} custom-call(f32[3072,128]{1,0:T(8,128)} %get-tuple-element.15.own_ref, s16[3,1040,128]{2,1,0:T(8,128)(2,1)} %collective-permute-done.2.received_ref), custom_call_target="tpu_custom_call" | custom-call | flops 393216 | bytes 3145728 | tf_op jit(solution)/shard_map/add_coded/pallas_call | solution.py:172
  149.3 0.8 collective-permute-start.3
  150.1 2.6 %copy.17 = bf16[1024,1024]{1,0:T(8,128)(2,1)} copy(bf16[1024,1024]{0,1:T(8,128)(2,1)S(1)} %bitcast.16) | data formatting | bytes 4194304 | tf_op jit(solution)/shard_map/transpose | solution.py:477
  152.7 3.8 %gather_fusion.1 = bf16[8,128,1024]{2,1,0:T(8,128)(2,1)} fusion(bf16[8,128,1024]{2,1,0:T(8,128)(2,1)} %bitcast.17, s32[1024]{0:T(1024)S(1)} %pad_clamp_fusion), kind=kCustom, calls=%fused_computation.1 | custom fusion | bytes 4194336 | tf_op jit(solution)/shard_map/gather | solution.py:477
  156.5 0.6 collective-permute-start.15
  157.1 0.9 collective-permute-start.12
  157.9 1.1 dynamic-slice_add_fusion
  159.1 0.6 slice.26
  159.8 1.0 copy.18
  160.8 8.6 %collective-permute-done.6.right_ref = s16[3,1040,128]{2,1,0:T(8,128)(2,1)S(1)} collective-permute-done((s16[3,1040,128]{2,1,0:T(8,128)(2,1)}, s16[3,1040,128]{2,1,0:T(8,128)(2,1)S(1)}, u32[]{:S(2)}, u32[]{:S(2)}) %collective-permute-start.6) | collective-permute-done | bytes 798752 | tf_op jit(solution)/shard_map/ppermute | solution.py:428
  169.5 0.8 copy-done.3
  170.2 4.0 %place_output.1 = bf16[32,128,128]{2,1,0:T(8,128)(2,1)} custom-call(s32[24]{0:T(128)} %group_ref.3, s32[24]{0:T(128)} %slot_ref.3, s32[24]{0:T(128)} %job_ref.9, s32[1]{0:T(128)} %bitcast.me_ref, f32[3072,128]{1,0:T(8,128)} %get-tuple-element.14.own_ref, s16[3,1040,128]{2,1,0:T(8,128)(2,1)} %collective-permute-done.3.left_ref, ...), custom_call_target="tpu_custom_call" | custom-call | flops 25165824 | bytes 3932160 | tf_op jit(solution)/shard_map/place_output/pallas_call | solution.py:346
  174.2 1.3 fusion.3
  175.5 6.8 %collective-permute-start.7 = (bf16[2048,128]{1,0:T(8,128)(2,1)S(1)}, bf16[2048,128]{1,0:T(8,128)(2,1)S(1)}, u32[]{:S(2)}, u32[]{:S(2)}) collective-permute-start(bf16[2048,128]{1,0:T(8,128)(2,1)S(1)} %bitcast.22), channel_id=1, source_target_pairs={{0,8},{8,0},{1,9},{9,1},{2,10},{10,2},{3,11},{11,3},{4,12},{12,4},... | collective-permute-start | bytes 1572872 | tf_op jit(solution)/shard_map/ppermute | solution.py:470
  182.3 4.0 %collective-permute-done.15.refs_5_ = bf16[3072,128]{1,0:T(8,128)(2,1)S(1)} collective-permute-done((bf16[3072,128]{1,0:T(8,128)(2,1)}, bf16[3072,128]{1,0:T(8,128)(2,1)S(1)}, u32[]{:S(2)}, u32[]{:S(2)}) %collective-permute-start.15) | collective-permute-done | bytes 786464 | tf_op jit(solution)/shard_map/ppermute | solution.py:425
  186.3 0.9 copy-done.12
  187.2 14.9 %input_gradient.1 = bf16[3072,1024]{1,0:T(8,128)(2,1)} custom-call(s32[24]{0:T(128)} %job_ref.9, bf16[3072,128]{1,0:T(8,128)(2,1)} %get-tuple-element.22.refs_0_.dy_ref, bf16[3072,128]{1,0:T(8,128)(2,1)} %collective-permute-done.9.refs_1_, bf16[3072,128]{1,0:T(8,128)(2,1)} %collective-permute-done.10.refs_2_, ...), custom_call_target="tpu_custom_call" | custom-call | flops 6442450944 | bytes 12582912 | tf_op jit(solution)/shard_map/input_gradient/pallas_call | solution.py:381
  202.1 1.2 maximum_select_fusion
  (46 shorter events, 1.7 us)
Async XLA Ops:
  7.2 2.2 %copy-start.13 = (s32[8]{0:T(128)S(1)}, s32[8]{0:T(128)}, u32[]{:S(2)}) copy-start(s32[8]{0:T(128)} %constant.41.clone) | copy-start | bytes 100
  7.2 3.5 %copy-start = (s32[8]{0:T(128)S(1)}, s32[8]{0:T(128)}, u32[]{:S(2)}) copy-start(s32[8]{0:T(128)} %constant.42.clone) | copy-start | bytes 100
  7.2 121.6 %all-reduce.3.cloned.1.call-start = ((), (), s32[]{:S(2)}) async-start(), calls=%async_computation | async-start | bytes 786432 | tf_op jit(solution)/shard_map/psum | solution.py:443
  9.3 11.8 %collective-permute-start.8 = (bf16[2048,128]{1,0:T(8,128)(2,1)S(1)}, bf16[2048,128]{1,0:T(8,128)(2,1)S(1)}, u32[]{:S(2)}, u32[]{:S(2)}) collective-permute-start(bf16[2048,128]{1,0:T(8,128)(2,1)S(1)} %get-tuple-element.36), channel_id=1, source_target_pairs={{0,8},{8,0},{1,9},{9,1},{2,10},{10,2},{3,11},{11,3},{4,12},{12,4},... | collective-permute-start | bytes 1572872 | tf_op jit(solution)/shard_map/ppermute | solution.py:432
  18.3 21.2 %collective-permute-start = (s16[3,1040,128]{2,1,0:T(8,128)(2,1)}, s16[3,1040,128]{2,1,0:T(8,128)(2,1)S(1)}, u32[]{:S(2)}, u32[]{:S(2)}) collective-permute-start(s16[3,1040,128]{2,1,0:T(8,128)(2,1)} %get-tuple-element.18), channel_id=1, source_target_pairs={{0,2},{2,4},{4,6},{6,7},{7,5},{5,3},{3,1},{1,0},{8,10},{10,12},{12... | collective-permute-start | bytes 2396168 | tf_op jit(solution)/shard_map/ppermute | solution.py:425
  21.1 0.8 copy-start.10
  27.6 19.1 %collective-permute-start.9 = (bf16[3072,128]{1,0:T(8,128)(2,1)}, bf16[3072,128]{1,0:T(8,128)(2,1)}, u32[]{:S(2)}, u32[]{:S(2)}) collective-permute-start(bf16[3072,128]{1,0:T(8,128)(2,1)} %get-tuple-element.22.refs_0_.dy_ref), channel_id=1, source_target_pairs={{0,1},{2,0},{4,2},{6,4},{7,6},{5,7},{3,5},{1,3},{8,9},{10,8},{12,1... | collective-permute-start | bytes 2359304 | tf_op jit(solution)/shard_map/ppermute | solution.py:428
  27.6 36.1 %collective-permute-start.4 = (s16[3,1040,128]{2,1,0:T(8,128)(2,1)}, s16[3,1040,128]{2,1,0:T(8,128)(2,1)S(1)}, u32[]{:S(2)}, u32[]{:S(2)}) collective-permute-start(s16[3,1040,128]{2,1,0:T(8,128)(2,1)} %get-tuple-element.21), channel_id=1, source_target_pairs={{0,1},{2,0},{4,2},{6,4},{7,6},{5,7},{3,5},{1,3},{8,9},{10,8},{12,1... | collective-permute-start | bytes 2396168 | tf_op jit(solution)/shard_map/ppermute | solution.py:428
  39.4 5.8 %copy-start.8 = (bf16[3072,128]{1,0:T(8,128)(2,1)S(1)}, bf16[3072,128]{1,0:T(8,128)(2,1)}, u32[]{:S(2)}) copy-start(bf16[3072,128]{1,0:T(8,128)(2,1)} %get-tuple-element.22.refs_0_.dy_ref) | copy-start | bytes 2359300
  39.4 7.6 %copy-start.9 = (bf16[1024,256]{1,0:T(8,128)(2,1)S(1)}, bf16[1024,256]{1,0:T(8,128)(2,1)}, u32[]{:S(2)}) copy-start(bf16[1024,256]{1,0:T(8,128)(2,1)} %param.15) | copy-start | bytes 1572868
  39.5 0.9 copy-start.7
  43.9 24.5 %collective-permute-start.1 = (s16[3,1040,128]{2,1,0:T(8,128)(2,1)}, s16[3,1040,128]{2,1,0:T(8,128)(2,1)S(1)}, u32[]{:S(2)}, u32[]{:S(2)}) collective-permute-start(s16[3,1040,128]{2,1,0:T(8,128)(2,1)} %add_coded.5), channel_id=1, source_target_pairs={{0,2},{2,4},{4,6},{6,7},{7,5},{5,3},{3,1},{1,0},{8,10},{10,12},{12... | collective-permute-start | bytes 2396168 | tf_op jit(solution)/shard_map/ppermute | solution.py:425
  45.2 89.9 %collective-permute-start.13 = (bf16[3072,128]{1,0:T(8,128)(2,1)S(1)}, bf16[3072,128]{1,0:T(8,128)(2,1)}, u32[]{:S(2)}, u32[]{:S(2)}) collective-permute-start(bf16[3072,128]{1,0:T(8,128)(2,1)S(1)} %copy-done.8), channel_id=1, source_target_pairs={{0,2},{2,4},{4,6},{6,7},{7,5},{5,3},{3,1},{1,0},{8,10},{10,12},{12... | collective-permute-start | bytes 2359304 | tf_op jit(solution)/shard_map/ppermute | solution.py:425
  46.7 88.9 %collective-permute-start.10 = (bf16[3072,128]{1,0:T(8,128)(2,1)}, bf16[3072,128]{1,0:T(8,128)(2,1)}, u32[]{:S(2)}, u32[]{:S(2)}) collective-permute-start(bf16[3072,128]{1,0:T(8,128)(2,1)} %collective-permute-done.9.refs_1_), channel_id=1, source_target_pairs={{0,1},{2,0},{4,2},{6,4},{7,6},{5,7},{3,5},{1,3},{8,9},{10,8},{12,1... | collective-permute-start | bytes 2359304 | tf_op jit(solution)/shard_map/ppermute | solution.py:428
  63.7 0.9 copy-start.5
  68.1 72.7 %collective-permute-start.5 = (s16[3,1040,128]{2,1,0:T(8,128)(2,1)}, s16[3,1040,128]{2,1,0:T(8,128)(2,1)S(1)}, u32[]{:S(2)}, u32[]{:S(2)}) collective-permute-start(s16[3,1040,128]{2,1,0:T(8,128)(2,1)} %add_coded.8), channel_id=1, source_target_pairs={{0,1},{2,0},{4,2},{6,4},{7,6},{5,7},{3,5},{1,3},{8,9},{10,8},{12,1... | collective-permute-start | bytes 2396168 | tf_op jit(solution)/shard_map/ppermute | solution.py:428
  68.4 0.9 copy-start.6
  72.8 72.9 %collective-permute-start.2 = (s16[3,1040,128]{2,1,0:T(8,128)(2,1)}, s16[3,1040,128]{2,1,0:T(8,128)(2,1)}, u32[]{:S(2)}, u32[]{:S(2)}) collective-permute-start(s16[3,1040,128]{2,1,0:T(8,128)(2,1)} %add_coded.6), channel_id=1, source_target_pairs={{0,2},{2,4},{4,6},{6,7},{7,5},{5,3},{3,1},{1,0},{8,10},{10,12},{12... | collective-permute-start | bytes 2396168 | tf_op jit(solution)/shard_map/ppermute | solution.py:425
  128.8 12.0 %copy-start.11 = (s32[8]{0:T(128)S(1)}, s32[8]{0:T(128)}, u32[]{:S(2)}) copy-start(s32[8]{0:T(128)} %gather_fusion) | copy-start | bytes 100
  135.1 21.4 %collective-permute-start.14 = (bf16[3072,128]{1,0:T(8,128)(2,1)}, bf16[3072,128]{1,0:T(8,128)(2,1)}, u32[]{:S(2)}, u32[]{:S(2)}) collective-permute-start(bf16[3072,128]{1,0:T(8,128)(2,1)} %collective-permute-done.13.refs_7_), channel_id=1, source_target_pairs={{0,2},{2,4},{4,6},{6,7},{7,5},{5,3},{3,1},{1,0},{8,10},{10,12},{12... | collective-permute-start | bytes 2359304 | tf_op jit(solution)/shard_map/ppermute | solution.py:425
  135.6 21.5 %collective-permute-start.11 = (bf16[3072,128]{1,0:T(8,128)(2,1)}, bf16[3072,128]{1,0:T(8,128)(2,1)}, u32[]{:S(2)}, u32[]{:S(2)}) collective-permute-start(bf16[3072,128]{1,0:T(8,128)(2,1)} %collective-permute-done.10.refs_2_), channel_id=1, source_target_pairs={{0,1},{2,0},{4,2},{6,4},{7,6},{5,7},{3,5},{1,3},{8,9},{10,8},{12,1... | collective-permute-start | bytes 2359304 | tf_op jit(solution)/shard_map/ppermute | solution.py:428
  137.7 20.3 %collective-permute-start.16 = (f32[128,1152]{1,0:T(8,128)S(1)}, f32[128,1152]{1,0:T(8,128)}, u32[]{:S(2)}, u32[]{:S(2)}) collective-permute-start(f32[128,1152]{1,0:T(8,128)S(1)} %constant_dynamic-slice_fusion), channel_id=1, source_target_pairs={{0,8},{8,0},{1,9},{9,1},{2,10},{10,2},{3,11},{11,3},{4,12},{12,4},... | collective-permute-start | bytes 1769480 | tf_op jit(solution)/shard_map/ppermute | solution.py:464
  140.8 0.9 copy-start.4
  145.2 5.0 %copy-start.1 = (bf16[1024,1024]{1,0:T(8,128)(2,1)S(1)}, bf16[1024,1024]{1,0:T(8,128)(2,1)}, u32[]{:S(2)}) copy-start(bf16[1024,1024]{1,0:T(8,128)(2,1)} %refs_1_.3) | copy-start | bytes 6291460
  145.2 24.2 %collective-permute-start.6 = (s16[3,1040,128]{2,1,0:T(8,128)(2,1)}, s16[3,1040,128]{2,1,0:T(8,128)(2,1)S(1)}, u32[]{:S(2)}, u32[]{:S(2)}) collective-permute-start(s16[3,1040,128]{2,1,0:T(8,128)(2,1)} %add_coded.9), channel_id=1, source_target_pairs={{0,1},{2,0},{4,2},{6,4},{7,6},{5,7},{3,5},{1,3},{8,9},{10,8},{12,1... | collective-permute-start | bytes 2396168 | tf_op jit(solution)/shard_map/ppermute | solution.py:428
  149.3 20.2 %collective-permute-start.3 = (s16[3,1040,128]{2,1,0:T(8,128)(2,1)}, s16[3,1040,128]{2,1,0:T(8,128)(2,1)}, u32[]{:S(2)}, u32[]{:S(2)}) collective-permute-start(s16[3,1040,128]{2,1,0:T(8,128)(2,1)} %add_coded.7), channel_id=1, source_target_pairs={{0,2},{2,4},{4,6},{6,7},{7,5},{5,3},{3,1},{1,0},{8,10},{10,12},{12... | collective-permute-start | bytes 2396168 | tf_op jit(solution)/shard_map/ppermute | solution.py:425
  152.7 5.2 %copy-start.2 = (f32[256,1152]{1,0:T(8,128)S(1)}, f32[256,1152]{1,0:T(8,128)}, u32[]{:S(2)}) copy-start(f32[256,1152]{1,0:T(8,128)} %factor_gradients.1) | copy-start | bytes 3538948
  156.5 29.9 %collective-permute-start.15 = (bf16[3072,128]{1,0:T(8,128)(2,1)}, bf16[3072,128]{1,0:T(8,128)(2,1)S(1)}, u32[]{:S(2)}, u32[]{:S(2)}) collective-permute-start(bf16[3072,128]{1,0:T(8,128)(2,1)} %collective-permute-done.14.refs_6_), channel_id=1, source_target_pairs={{0,2},{2,4},{4,6},{6,7},{7,5},{5,3},{3,1},{1,0},{8,10},{10,12},{12... | collective-permute-start | bytes 2359304 | tf_op jit(solution)/shard_map/ppermute | solution.py:425
  157.1 29.3 %collective-permute-start.12 = (bf16[3072,128]{1,0:T(8,128)(2,1)}, bf16[3072,128]{1,0:T(8,128)(2,1)}, u32[]{:S(2)}, u32[]{:S(2)}) collective-permute-start(bf16[3072,128]{1,0:T(8,128)(2,1)} %collective-permute-done.11.refs_3_), channel_id=1, source_target_pairs={{0,1},{2,0},{4,2},{6,4},{7,6},{5,7},{3,5},{1,3},{8,9},{10,8},{12,1... | collective-permute-start | bytes 2359304 | tf_op jit(solution)/shard_map/ppermute | solution.py:428
  169.4 0.9 copy-start.3
  175.5 26.6 %collective-permute-start.7 = (bf16[2048,128]{1,0:T(8,128)(2,1)S(1)}, bf16[2048,128]{1,0:T(8,128)(2,1)S(1)}, u32[]{:S(2)}, u32[]{:S(2)}) collective-permute-start(bf16[2048,128]{1,0:T(8,128)(2,1)S(1)} %bitcast.22), channel_id=1, source_target_pairs={{0,8},{8,0},{1,9},{9,1},{2,10},{10,2},{3,11},{11,3},{4,12},{12,4},... | collective-permute-start | bytes 1572872 | tf_op jit(solution)/shard_map/ppermute | solution.py:470
  186.3 0.9 copy-start.12
Sparse Core Ops, SparseCore 0:
  54.1 74.6 all-reduce.2

commit v3 on v1

--- a/solution.py
+++ b/solution.py
@@ -77,9 +77,540 @@
         lax.psum_scatter(b_term, "dp", scatter_dimension=0, tiled=True),
     )
 
+RANGE = 32766.0
+STEPS = 64.0
+PAD = 16
+VMEM_BYTES = 63 * 1024 * 1024
+
+
+SMEM = pl.BlockSpec(memory_space=pltpu.SMEM)
+VMEM = pl.BlockSpec(memory_space=pltpu.VMEM)
+ANY = pl.BlockSpec(memory_space=pl.ANY)
+
+
+def params():
+    return pltpu.CompilerParams(vmem_limit_bytes=VMEM_BYTES)
+
+
+def cost():
+    return pl.CostEstimate(flops=1, bytes_accessed=1, transcendentals=0)
+
+
+def halves(v):
+    high = v.astype(jnp.bfloat16)
+    return high, (v - high.astype(jnp.float32)).astype(jnp.bfloat16)
+
+
+def store_coded(out_ref, at, v):
+    rows = v.shape[0]
+    top = jnp.maximum(jnp.max(jnp.abs(v), axis=0, keepdims=True), 1e-30)
+    level = jnp.ceil(jnp.log2(top) * STEPS)
+    coded = jnp.round(v * (jnp.exp2(level * (-1.0 / STEPS)) * (RANGE * 0.9999)))
+    out_ref[at, pl.ds(0, rows), :] = coded.astype(jnp.int32).astype(jnp.int16)
+    out_ref[at, pl.ds(rows, PAD), :] = (
+        jnp.broadcast_to(level, (PAD, v.shape[1])).astype(jnp.int32).astype(jnp.int16)
+    )
+
+
+def load_coded(in_ref, at, first=0, rows=None):
+    total = in_ref.shape[1] - PAD
+    level = in_ref[at, pl.ds(total, PAD), :].astype(jnp.int32).astype(jnp.float32)[0:1, :]
+    coded = in_ref[at, pl.ds(first, rows or total), :].astype(jnp.int32).astype(jnp.float32)
+    return coded * (jnp.exp2(level * (1.0 / STEPS)) * (1.0 / (RANGE * 0.9999)))
+
+
+LANES = 128
+PACKED = LANES // ADAPTER_RANK
+
+
+def lane_slot(shape):
+    return lax.broadcasted_iota(jnp.int32, shape, len(shape) - 1) // ADAPTER_RANK
+
+
+def pack(tile, i, values, job):
+    kept = values[:, :LANES]
+    for h in range(1, values.shape[1] // LANES):
+        kept = jnp.where(job // PACKED == h, values[:, h * LANES : (h + 1) * LANES], kept)
+    shift = lax.rem((i - lax.rem(job, PACKED) + PACKED) * ADAPTER_RANK, LANES)
+    return jnp.where(lane_slot(tile.shape) == i, pltpu.roll(kept, shift, 1), tile)
+
+
+def expand(tile, i, job, columns):
+    place = lax.rem(job, PACKED)
+    shift = lax.rem((place - i + PACKED) * ADAPTER_RANK, LANES)
+    rolled = pltpu.roll(tile, shift, 1)
+    rolled = jnp.where(lane_slot(tile.shape) == place, rolled, 0.0)
+    return jnp.concatenate(
+        [jnp.where(job // PACKED == h, rolled, 0.0) for h in range(columns // LANES)], axis=1
+    )
+
+
+def coded_spec(group_rows, columns):
+    return pl.BlockSpec((1, group_rows + PAD, columns), lambda g, *_: (g, 0, 0))
+
+
+def coded_shape(rows, group_rows, columns):
+    return jax.ShapeDtypeStruct((rows // group_rows, group_rows + PAD, columns), jnp.int16)
+
+
+def project(x, first, rows, w, place, offsets, group_rows, columns, coded, after=()):
+    features = x.shape[1]
+    count = len(offsets)
+    start = first // group_rows
+
+    def kernel(place_ref, x_ref, *refs):
+        weight_ref = refs[-1]
+        refs = refs[:count] + refs[count + len(after) : -1]
+
+        @pl.when(pl.program_id(0) == 0)
+        def _():
+            for i in range(count):
+                weight_ref[:, i * columns : (i + 1) * columns] = refs[i][...]
+
+        product = dot32(x_ref[...], weight_ref[...], ((1,), (0,)))
+        for i in range(count):
+            part = product[:, i * columns : (i + 1) * columns]
+            if coded:
+                store_coded(refs[count + i], 0, part)
+            else:
+                refs[count + i][...] = part
+
+    def weight_spec(d):
+        return pl.BlockSpec((features, columns), lambda g, place_ref: (0, place_ref[d]))
+
+    if coded:
+        out_specs = [coded_spec(group_rows, columns)] * count
+        out_shape = [coded_shape(rows, group_rows, columns)] * count
+    else:
+        out_specs = [pl.BlockSpec((group_rows, columns), lambda g, place_ref: (g, 0))] * count
+        out_shape = [jax.ShapeDtypeStruct((rows, columns), jnp.float32)] * count
+    return pl.pallas_call(
+        kernel,
+        grid_spec=pltpu.PrefetchScalarGridSpec(
+            num_scalar_prefetch=1,
+            grid=(rows // group_rows,),
+            in_specs=[pl.BlockSpec((group_rows, features), lambda g, place_ref: (g + start, 0))]
+            + [weight_spec(d) for d in offsets]
+            + [ANY] * len(after),
+            out_specs=out_specs,
+            scratch_shapes=[pltpu.VMEM((features, count * columns), jnp.bfloat16)],
+        ),
+        out_shape=out_shape,
+        compiler_params=params(),
+        cost_estimate=cost(),
+        name="project",
+    )(place, x, *([w] * count), *after)
+
+
+def add_coded(pairs, group_rows, after, sums=False, coded=True, groups=1):
+    rows, columns = pairs[0][0].shape
+    count = len(pairs)
+
+    def kernel(*refs):
+        outs = refs[2 * count + len(after) :]
+        for p in range(count):
+            for g in range(groups):
+                here = pl.ds(g * group_rows, group_rows)
+                total = refs[2 * p][here, :] + load_coded(refs[2 * p + 1], g)
+                if sums:
+                    outs[p][here, :] = total
+                if coded:
+                    store_coded(outs[count * sums + p], g, total)
+
+    block = pl.BlockSpec((groups * group_rows, columns), lambda g: (g, 0))
+    coded_block = pl.BlockSpec((groups, group_rows + PAD, columns), lambda g: (g, 0, 0))
+    return pl.pallas_call(
+        kernel,
+        grid=(rows // group_rows // groups,),
+        in_specs=[block, coded_block] * count + [ANY] * len(after),
+        out_specs=[block] * (count * sums) + [coded_block] * (count * coded),
+        out_shape=[jax.ShapeDtypeStruct((rows, columns), jnp.float32)] * (count * sums)
+        + [coded_shape(rows, group_rows, columns)] * (count * coded),
+        compiler_params=params(),
+        cost_estimate=cost(),
+        name="add_coded",
+    )(*[v for pair in pairs for v in pair], *after)
+
+
+def home_gradient(dy, received, group, slot, me, length, streams, after):
+    blocks = group.shape[0]
+    columns = dy.shape[1]
+    half = received.shape[0]
+    per = blocks // streams
+
+    def kernel(group_ref, slot_ref, me_ref, dy_ref, received_ref, *refs):
+        outs = refs[len(after) :]
+        mine = me_ref[0]
+
+        def put(n, value):
+            outs[0][pl.ds(n * length, length), :] = value
+            outs[1 + n // per][pl.ds(n % per * length, length), :] = value
+
+        for n in range(blocks):
+            at = slot_ref[n] * length
+
+            @pl.when(group_ref[n] == mine)
+            def _():
+                put(n, dy_ref[pl.ds(pl.multiple_of(mine * half + at, length), length), :])
+
+            @pl.when(group_ref[n] != mine)
+            def _():
+                put(n, received_ref[pl.ds(pl.multiple_of(at, length), length), :])
+
+    return pl.pallas_call(
+        kernel,
+        in_specs=[SMEM] * 3 + [VMEM] * 2 + [ANY] * len(after),
+        out_specs=[VMEM] * (1 + streams),
+        out_shape=[jax.ShapeDtypeStruct((blocks * length, columns), jnp.bfloat16)]
+        + [jax.ShapeDtypeStruct((per * length, columns), jnp.bfloat16)] * streams,
+        compiler_params=params(),
+        cost_estimate=cost(),
+        name="home_gradient",
+    )(group, slot, me, dy, received, *after)
+
+
+def low_rank(x, a, dy_home, b_t, job, length, after):
+    blocks = job.shape[0]
+    features = x.shape[1]
+    columns = dy_home.shape[1]
+
+    def kernel(job_ref, x_ref, a_ref, dy_ref, b_ref, *refs):
+        low_ref, coded_ref = refs[-2:]
+        first = pl.program_id(0) * PACKED
+        products = (
+            dot32(x_ref[...], a_ref[...], ((1,), (0,))),
+            SCALE * dot32(dy_ref[...], b_ref[...], ((1,), (0,))),
+        )
+        for kind, product in enumerate(products):
+            tile = jnp.zeros((length, LANES), jnp.float32)
+            for i in range(PACKED):
+                tile = pack(tile, i, product[i * length : (i + 1) * length], job_ref[first + i])
+            low_ref[pl.ds(kind * length, length), :] = tile
+            store_coded(coded_ref, kind, tile)
+
+    rows = PACKED * length
+    return pl.pallas_call(
+        kernel,
+        grid_spec=pltpu.PrefetchScalarGridSpec(
+            num_scalar_prefetch=1,
+            grid=(blocks // PACKED,),
+            in_specs=[
+                pl.BlockSpec((rows, features), lambda g, job_ref: (g, 0)),
+                pl.BlockSpec(a.shape, lambda g, job_ref: (0, 0)),
+                pl.BlockSpec((rows, columns), lambda g, job_ref: (g, 0)),
+                pl.BlockSpec(b_t.shape, lambda g, job_ref: (0, 0)),
+            ]
+            + [ANY] * len(after),
+            out_specs=[
+                pl.BlockSpec((2 * length, LANES), lambda g, job_ref: (g, 0)),
+                pl.BlockSpec((2, length + PAD, LANES), lambda g, job_ref: (g, 0, 0)),
+            ],
+        ),
+        out_shape=[
+            jax.ShapeDtypeStruct((blocks // PACKED * 2 * length, LANES), jnp.float32),
+            coded_shape(blocks // PACKED * 2 * length, length, LANES),
+        ],
+        compiler_params=params(),
+        cost_estimate=cost(),
+        name="low_rank",
+    )(job, x, a, dy_home, b_t, *after)
+
+
+def factor_gradients(x, dy_home, low, job, ranks, length, after):
+    blocks = job.shape[0]
+    features = x.shape[1]
+    columns = dy_home.shape[1]
+
+    def kernel(job_ref, x_ref, dy_ref, low_ref, *refs):
+        out_ref = refs[-1]
+        step = pl.program_id(0)
+        spread = []
+        for kind in range(2):
+            tile = low_ref[pl.ds(kind * length, length), :]
+            wide = jnp.concatenate(
+                [expand(tile, i, job_ref[step * PACKED + i], ranks) for i in range(PACKED)], axis=0
+            )
+            spread.append(jnp.concatenate(halves(wide), axis=1))
+        down = dot32(spread[1], x_ref[...], ((0,), (0,)))
+        up = SCALE * dot32(spread[0], dy_ref[...], ((0,), (0,)))
+
+        @pl.when(step == 0)
+        def _():
+            out_ref[...] = jnp.zeros_like(out_ref)
+
+        out_ref[:, pl.ds(0, features)] += down[:ranks] + down[ranks:]
+        out_ref[:, pl.ds(features, columns)] += up[:ranks] + up[ranks:]
+
+    rows = PACKED * length
+    shape = (ranks, features + columns)
+    return pl.pallas_call(
+        kernel,
+        grid_spec=pltpu.PrefetchScalarGridSpec(
+            num_scalar_prefetch=1,
+            grid=(blocks // PACKED,),
+            in_specs=[
+                pl.BlockSpec((rows, features), lambda g, job_ref: (g, 0)),
+                pl.BlockSpec((rows, columns), lambda g, job_ref: (g, 0)),
+                pl.BlockSpec((2 * length, LANES), lambda g, job_ref: (g, 0)),
+            ]
+            + [ANY] * len(after),
+            out_specs=pl.BlockSpec(shape, lambda g, job_ref: (0, 0)),
+        ),
+        out_shape=jax.ShapeDtypeStruct(shape, jnp.float32),
+        compiler_params=params(),
+        cost_estimate=cost(),
+        name="factor_gradients",
+    )(job, x, dy_home, low, *after)
+
+
+def place_output(own, from_left, from_right, low, b, group, slot, job, me, length, cap, after):
+    blocks = group.shape[0]
+    ranks, columns = b.shape
+    per_group = (from_left[0].shape[1] - PAD) // length
+    count = len(own)
+    per_stream = blocks // count
+
+    def kernel(group_ref, slot_ref, job_ref, me_ref, low_ref, b_ref, *refs):
+        out_ref = refs[-1]
+        out_ref[...] = jnp.zeros_like(out_ref)
+        factors = jnp.concatenate((b_ref[...], b_ref[...]), axis=0)
+        for n in range(blocks):
+            own_ref, left_ref, right_ref = refs[3 * (n // per_stream) :][:3]
+            m = n % per_stream
+            g, i = m // per_group, m % per_group
+            total = (
+                own_ref[pl.ds(m * length, length), :]
+                + load_coded(left_ref, g, i * length, length)
+                + load_coded(right_ref, g, i * length, length)
+            )
+            tile = low_ref[pl.ds(n // PACKED * 2 * length, length), :]
+            wide = jnp.concatenate(
+                halves(expand(SCALE * tile, n % PACKED, job_ref[n], ranks)), axis=1
+            )
+            total = total + dot32(wide, factors, ((1,), (0,)))
+            other = jnp.where(group_ref[n] == me_ref[0], 0, 1)
+            out_ref[other * cap + slot_ref[n]] = total.astype(jnp.bfloat16)
+
+    sums = [v for k in range(count) for v in (own[k], from_left[k], from_right[k])]
+    return pl.pallas_call(
+        kernel,
+        in_specs=[SMEM] * 4 + [VMEM] * (2 + len(sums)) + [ANY] * len(after),
+        out_specs=VMEM,
+        out_shape=jax.ShapeDtypeStruct((2 * cap, length, columns), jnp.bfloat16),
+        compiler_params=params(),
+        cost_estimate=cost(),
+        name="place_output",
+    )(group, slot, job, me, low, b, *sums, *after)
+
+
+def input_gradient(pieces, w_t, place, low, a_t, job, length, step_blocks, stream, made, after):
+    blocks = job.shape[0]
+    count = len(pieces)
+    stream_rows, columns = pieces[0].shape
+    ranks, features = a_t.shape
+    depth = count * columns + 2 * ranks
+    steps = stream_rows // (step_blocks * length)
+    start = stream * steps
+    held = () if made is None else (made,)
+
+    def kernel(job_ref, place_ref, *refs):
+        weights, parts = refs[:count], refs[count : 2 * count]
+        low_ref, a_ref = refs[2 * count : 2 * count + 2]
+        out_ref, factor_ref = refs[-2:]
+
+        @pl.when(pl.program_id(0) == 0)
+        def _():
+            for i in range(count):
+                factor_ref[pl.ds(i * columns, columns), :] = weights[i][...]
+            for i in range(2):
+                factor_ref[pl.ds(count * columns + i * ranks, ranks), :] = a_ref[...]
+
+        wide = []
+        for i in range(step_blocks):
+            n = (pl.program_id(0) + start) * step_blocks + i
+            first = pl.multiple_of((2 * (n // PACKED) + 1) * length, length)
+            tile = low_ref[pl.ds(first, length), :]
+            wide.append(expand(tile, lax.rem(n, PACKED), job_ref[n], ranks))
+        lhs = [r[...] for r in parts] + list(halves(jnp.concatenate(wide, axis=0)))
+        out_ref[...] = dot32(
+            jnp.concatenate(lhs, axis=1), factor_ref[...], ((1,), (0,))
+        ).astype(jnp.bfloat16)
+
+    step_rows = step_blocks * length
+
+    def weight_spec(d):
+        return pl.BlockSpec((columns, features), lambda g, job_ref, place_ref: (place_ref[d], 0))
+
+    def whole_spec(v):
+        return pl.BlockSpec(v.shape, lambda g, job_ref, place_ref: (0, 0))
+
+    return pl.pallas_call(
+        kernel,
+        grid_spec=pltpu.PrefetchScalarGridSpec(
+            num_scalar_prefetch=2,
+            grid=(steps,),
+            in_specs=[weight_spec(d) for d in range(count)]
+            + [pl.BlockSpec((step_rows, columns), lambda g, job_ref, place_ref: (g, 0))] * count
+            + [whole_spec(low), whole_spec(a_t)]
+            + [ANY] * (len(held) + len(after)),
+            out_specs=pl.BlockSpec(
+                (step_rows, features), lambda g, job_ref, place_ref: (g + start, 0)
+            ),
+            scratch_shapes=[pltpu.VMEM((depth, features), jnp.bfloat16)],
+        ),
+        out_shape=jax.ShapeDtypeStruct((blocks * length, features), jnp.bfloat16),
+        input_output_aliases={2 + 2 * count + 2: 0} if held else {},
+        compiler_params=params(),
+        cost_estimate=cost(),
+        name="input_gradient",
+    )(job, place, *([w_t] * count), *[pieces[d] for d in range(count)], low, a_t, *held, *after)
+
+
+def ring(x, group, slot, job, w, a, b, dy):
+    size = lax.axis_size("tensor")
+    me = lax.axis_index("dp").astype(jnp.int32)
+    blocks = group.shape[0]
+    rows, features = x.shape
+    length = rows // blocks
+    columns = dy.shape[1]
+    half = dy.shape[0] // 2
+    cap = half // length
+    streams = 2
+    part_rows = rows // streams
+    step_blocks = blocks // streams // 2
+    group_rows = step_blocks * length
+
+    order = [2 * r for r in range(size // 2)] + [2 * r + 1 for r in reversed(range(size // 2))]
+    me_tensor = lax.axis_index("tensor").astype(jnp.int32)
+    here = jnp.where(me_tensor % 2 == 0, me_tensor // 2, size - 1 - me_tensor // 2)
+    there = (here + jnp.arange(size, dtype=jnp.int32)) % size
+    place = jnp.where(there < size // 2, 2 * there, 2 * (size - 1 - there) + 1)
+    ahead = [(order[r], order[(r + 1) % size]) for r in range(size)]
+    back = [(order[r], order[(r - 1) % size]) for r in range(size)]
+    swap = [(0, 1), (1, 0)]
+
+    def right(v):
+        return lax.ppermute(v, "tensor", ahead)
+
+    def left(v):
+        return lax.ppermute(v, "tensor", back)
+
+    def exchange(v, bit):
+        return lax.ppermute(v, "tensor", [(t, t ^ bit) for t in range(size)])
+
+    mine = me[None]
+    got = lax.ppermute(lax.dynamic_slice_in_dim(dy, (1 - me) * half, half), "dp", swap)
+
+    far, near = size // 2, size // 2 - 1
+    both = range(streams)
+    sums_r, sums_l, held_r, held_l, terms, pieces = [], [], [], [], [], []
+    last = ()
+
+    def first(k):
+        nonlocal last
+        r, l = project(
+            x, k * part_rows, part_rows, w, place, (far, size - near), group_rows, columns, True, last
+        )
+        last = (r,)
+        sums_r.append(right(r))
+        sums_l.append(left(l))
+
+    first(0)
+    dy_home, *parts = home_gradient(dy, got, group, slot, mine, length, streams, last)
+    for k in both:
+        held_r.append(right(parts[k]))
+        held_l.append(left(parts[k]))
+        pieces.append({0: parts[k], size - 1: held_r[k], 1: held_l[k]})
+    last = (dy_home,)
+    for k in both[1:]:
+        first(k)
+    low, coded = low_rank(x, a, dy_home, b.T, job, length, last)
+    last = (coded,)
+    bit = 1
+    swapped = exchange(coded, bit)
+
+    offsets = []
+    for d in range(1, far):
+        offsets += [far - d] + ([size - (near - d)] if near > d else [])
+    offsets += [0]
+    for k in both:
+        made = project(
+            x, k * part_rows, part_rows, w, place, tuple(offsets), group_rows, columns, False, last
+        )
+        terms.append(dict(zip(offsets, made)))
+        last = (made[0],)
+
+    def low_step():
+        nonlocal low, swapped, bit, last
+        more = 2 * bit < size
+        got = add_coded([(low, swapped)], length, last, True, more, low.shape[0] // length)
+        low = got[0]
+        last = (low,)
+        bit *= 2
+        if more:
+            swapped = exchange(got[1], bit)
+
+    low_step()
+    for d in range(1, far):
+        for k in both:
+            pairs = [(terms[k][far - d], sums_r[k])]
+            if near > d:
+                pairs.append((terms[k][size - (near - d)], sums_l[k]))
+            turns = add_coded(pairs, group_rows, last)
+            sums_r[k] = right(turns[0])
+            if near > d:
+                sums_l[k] = left(turns[1])
+            last = (turns[0], held_l[k])
+            if d < near:
+                last += (held_r[k],)
+                held_r[k] = right(held_r[k])
+                pieces[k][size - 1 - d] = held_r[k]
+            held_l[k] = left(held_l[k])
+            pieces[k][1 + d] = held_l[k]
+        if bit < size:
+            low_step()
+
+    ranks = a.shape[1]
+    factors = factor_gradients(x, dy_home, low, job, ranks, length, last)
+    part = ranks // 2
+    theirs = lax.ppermute(lax.dynamic_slice_in_dim(factors, (1 - me) * part, part), "dp", swap)
+    w_t, a_t = w.T, a.T
+    placed = place_output(
+        [terms[k][0] for k in both], sums_r, sums_l, low, b, group, slot, job, mine, length, cap,
+        (factors, w_t),
+    )
+    last = (placed,)
+    placed = placed.reshape(2, half, columns)
+    other = lax.ppermute(placed[1], "dp", swap)
+    factors = lax.dynamic_slice_in_dim(factors, me * part, part) + theirs
+    output = jnp.where(
+        me == 0, jnp.concatenate((placed[0], other)), jnp.concatenate((other, placed[0]))
+    )
+    grad_home = None
+    for k in both:
+        grad_home = input_gradient(
+            pieces[k], w_t, place, low, a_t, job, length, step_blocks // 2, k, grad_home, last
+        )
+        last = (output,)
+    return output, grad_home, factors[:, :features].T, factors[:, features:]
+
 
 def local(*args):
-    return general(*args)
+    x, group, dy = args[0], args[1], args[7]
+    size = lax.axis_size("tensor")
+    blocks = group.shape[0]
+    length = x.shape[0] // blocks
+    fits = (
+        lax.axis_size("dp") == 2
+        and size % 2 == 0
+        and size in (4, 8)
+        and dy.shape[1] % 128 == 0
+        and x.shape[1] % 128 == 0
+        and length == LANES
+        and args[5].shape[1] % (2 * LANES) == 0
+        and blocks % 8 == 0
+    )
+    return ring(*args) if fits else general(*args)
 
 
 def solution(mesh):

time: 460 us -> 187 us (0.41)
  waiting for transfers between devices: 342 us -> 35.7 us
  Pallas kernels: 0 us -> 86.2 us
  matrix products: 69.6 us -> 0 us
  starting transfers between devices: 4.11 us -> 43.9 us
  between operations: 14 us -> 0.93 us
  other arithmetic: 10.9 us -> 4.34 us
  blocking collectives: 5.62 us -> 0 us
    reduce_scatter x3 -> x0, waiting for transfers between devices: 185 us -> none  [the longest x1 185 us: general(): lax.psum_scatter(dot32(x, w, ((1,), (0,))), 'tensor', scatter_dimension=1...]
    pallas_call x0 -> x19, Pallas kernels: none -> 86.2 us  [the longest x4 22.5 us: project(): pl.pallas_call(kernel, grid_spec=pltpu.PrefetchScalarGridSpec(num_scalar_...]
    all_gather x1 -> x0, waiting for transfers between devices: 83.6 us -> none  [general(): full = lax.all_gather(dy_home, 'tensor', axis=1, tiled=True)]
    psum x1 -> x0, waiting for transfers between devices: 72.1 us -> none  [general(): sums = lax.psum(parts, 'tensor')]
    dot_general x12 -> x0, matrix products: 69.6 us -> none  [dot32(): lax.dot_general(a, b, (dims, ((), ())), preferred_element_type=jnp.float32)]
    ppermute x0 -> x34, starting transfers between devices: none -> 43.9 us  [the longest x14 23.6 us: left(): return lax.ppermute(v, 'tensor', back)]
    ppermute x0 -> x34, waiting for transfers between devices: none -> 35.7 us  [the longest x3 16 us: exchange(): return lax.ppermute(v, 'tensor', [(t, t ^ bit) for t in range(size)])]
    all_to_all x1 -> x0, blocking collectives: 5.62 us -> none  [general(): lax.all_to_all(sent.reshape(groups, cap * length, columns), 'dp', split_a...]
  transfers between devices with their start and end apart: 6 -> 34, of which waited for: 4 -> 7; matrix products, arithmetic and copies ran while one was open for 13% -> 9% of each run, Pallas kernels for 0% -> 41%
where the time goes in v3:
time: 187 us; the launch traced here: 186 us
  Pallas kernels  86.2 us (46%)
  starting transfers between devices  43.9 us (23%)
  waiting for transfers between devices  35.7 us (19%)
  local copies, waits for them, and re-layouts  14.9 us (8%)
  other arithmetic  4.34 us (2%)
    ppermute x14, starting transfers between devices, left(): return lax.ppermute(v, 'tensor', back)  23.6 us
    pallas_call x4, Pallas kernels, project(): pl.pallas_call(kernel, grid_spec=pltpu.PrefetchScalarGridSpec(num_scalar_...  22.5 us
    pallas_call x9, Pallas kernels, add_coded(): pl.pallas_call(kernel, grid=(rows // group_rows // groups,), in_specs=[bl...  20.3 us
    pallas_call x2, Pallas kernels, input_gradient(): pl.pallas_call(kernel, grid_spec=pltpu.PrefetchScalarGridSpec(num_scalar_...  19.8 us
    ppermute x3, waiting for transfers between devices, exchange(): return lax.ppermute(v, 'tensor', [(t, t ^ bit) for t in range(size)])  16 us
    ppermute x14, waiting for transfers between devices, right(): return lax.ppermute(v, 'tensor', ahead)  13.1 us
    ppermute x14, starting transfers between devices, right(): return lax.ppermute(v, 'tensor', ahead)  12 us
    pallas_call x1, Pallas kernels, factor_gradients(): pl.pallas_call(kernel, grid_spec=pltpu.PrefetchScalarGridSpec(num_scalar_...  9.25 us
  transfers between devices with their start and end apart: 34, of which 7 were waited for; matrix products, arithmetic and copies ran while one was open for 9% of the time, Pallas kernels for 41%

profile of v3, /device:TPU:1, one launch (start us, length us, event | category | flops | bytes accessed | tf_op | source)
XLA Modules:
  0.0 185.9 jit_solution(2234376860036872282)
XLA Ops:
  2.4 4.4 %project.4 = (s16[2,784,128]{2,1,0:T(8,128)(2,1)}, s16[2,784,128]{2,1,0:T(8,128)(2,1)}) custom-call(s32[8]{0:T(128)} %compare_select_fusion.2.place_ref, bf16[3072,1024]{1,0:T(8,128)(2,1)} %x_ref.11, bf16[1024,1024]{1,0:T(8,128)(2,1)} %refs_5_.3, bf16[1024,1024]{1,0:T(8,128)(2,1)} %refs_5_.3), custom_call_target="tpu_custom_call" | custom-call | flops 1 | bytes 1 | tf_op jit(solution)/shard_map/project/pallas_call | solution.py:187
  6.8 2.7 %collective-permute-start.5 = (s16[2,784,128]{2,1,0:T(8,128)(2,1)}, s16[2,784,128]{2,1,0:T(8,128)(2,1)S(1)}, u32[]{:S(2)}, u32[]{:S(2)}) collective-permute-start(s16[2,784,128]{2,1,0:T(8,128)(2,1)} %get-tuple-element.37.refs_0_), channel_id=1, source_target_pairs={{0,2},{2,4},{4,6},{6,7},{7,5},{5,3},{3,1},{1,0},{8,10},{10,12},{12... | collective-permute-start | bytes 1204232 | tf_op jit(solution)/shard_map/ppermute | solution.py:493
  9.6 1.6 copy.13
  11.2 3.1 %home_gradient.1 = (bf16[3072,128]{1,0:T(8,128)(2,1)}, bf16[1536,128]{1,0:T(8,128)(2,1)}, bf16[1536,128]{1,0:T(8,128)(2,1)}) custom-call(s32[24]{0:T(128)} %group_ref.3, s32[24]{0:T(128)} %slot_ref.3, s32[1]{0:T(128)} %bitcast.me_ref, bf16[4096,128]{1,0:T(8,128)(2,1)} %dy_ref.1, bf16[2048,128]{1,0:T(8,128)(2,1)} %collective-permute-done.received_ref, ...), custom_call_target="tpu_custom_call" | custom-call | flops 1 | bytes 1 | tf_op jit(solution)/shard_map/home_gradient/pallas_call | solution.py:260
  14.3 4.4 %project.5 = (s16[2,784,128]{2,1,0:T(8,128)(2,1)}, s16[2,784,128]{2,1,0:T(8,128)(2,1)}) custom-call(s32[8]{0:T(128)} %compare_select_fusion.2.place_ref, bf16[3072,1024]{1,0:T(8,128)(2,1)} %x_ref.11, bf16[1024,1024]{1,0:T(8,128)(2,1)} %refs_5_.3, bf16[1024,1024]{1,0:T(8,128)(2,1)} %refs_5_.3, bf16[3072,128]{1,0:T(8,128)(2,1)} %get-tuple-element.38.refs_2_.dy_ref), custom_call_target="tpu_custom_call" | custom-call | flops 1 | bytes 1 | tf_op jit(solution)/shard_map/project/pallas_call | solution.py:187
  18.7 6.6 %low_rank.1 = (f32[768,128]{1,0:T(8,128)}, s16[6,144,128]{2,1,0:T(8,128)(2,1)}) custom-call(s32[24]{0:T(128)} %job_ref.9, bf16[3072,1024]{1,0:T(8,128)(2,1)} %x_ref.11, bf16[1024,256]{1,0:T(8,128)(2,1)} %a_ref.1, bf16[3072,128]{1,0:T(8,128)(2,1)} %get-tuple-element.38.refs_2_.dy_ref, bf16[128,256]{1,0:T(8,128)(2,1)} %bitcast.28, ...), custom_call_target="tpu_custom_call" | custom-call | flops 1 | bytes 1 | tf_op jit(solution)/shard_map/low_rank/pallas_call | solution.py:292
  25.3 1.4 collective-permute-start.1
  26.8 1.4 collective-permute-start.8
  29.0 1.3 collective-permute-start.10
  30.3 1.3 collective-permute-start.3
  33.4 6.8 %project.6 = (f32[1536,128]{1,0:T(8,128)}, f32[1536,128]{1,0:T(8,128)}, f32[1536,128]{1,0:T(8,128)}, f32[1536,128]{1,0:T(8,128)}, f32[1536,128]{1,0:T(8,128)}, /*index=5*/f32[1536,128]{1,0:T(8,128)}) custom-call(s32[8]{0:T(128)} %compare_select_fusion.2.place_ref, bf16[3072,1024]{1,0:T(8,128)(2,1)} %x_ref.11, bf16[1024,1024]{1,0:T(8,128)(2,1)} %refs_5_.3, ...), custom_call_target="tpu_custom_call" | custom-call | flops 1 | bytes 1 | tf_op jit(solution)/shard_map/project/pallas_call | solution.py:187
  40.3 6.9 %project.7 = (f32[1536,128]{1,0:T(8,128)}, f32[1536,128]{1,0:T(8,128)}, f32[1536,128]{1,0:T(8,128)}, f32[1536,128]{1,0:T(8,128)}, f32[1536,128]{1,0:T(8,128)}, /*index=5*/f32[1536,128]{1,0:T(8,128)}) custom-call(s32[8]{0:T(128)} %compare_select_fusion.2.place_ref, bf16[3072,1024]{1,0:T(8,128)(2,1)} %x_ref.11, bf16[1024,1024]{1,0:T(8,128)(2,1)} %refs_5_.3, ...), custom_call_target="tpu_custom_call" | custom-call | flops 1 | bytes 1 | tf_op jit(solution)/shard_map/project/pallas_call | solution.py:187
  47.1 2.0 %add_coded.9 = (f32[768,128]{1,0:T(8,128)}, s16[6,144,128]{2,1,0:T(8,128)(2,1)}) custom-call(f32[768,128]{1,0:T(8,128)} %get-tuple-element.40.refs_0_, s16[6,144,128]{2,1,0:T(8,128)(2,1)} %copy-done.8, f32[1536,128]{1,0:T(8,128)} %get-tuple-element.43.refs_2_.refs_0_), custom_call_target="tpu_custom_call" | custom-call | flops 1 | bytes 1 | tf_op jit(solution)/shard_map/add_coded/pallas_call | solution.py:222
  49.1 2.6 %add_coded.10 = (s16[2,784,128]{2,1,0:T(8,128)(2,1)}, s16[2,784,128]{2,1,0:T(8,128)(2,1)}) custom-call(f32[1536,128]{1,0:T(8,128)} %get-tuple-element.42.refs_6_.refs_0_, s16[2,784,128]{2,1,0:T(8,128)(2,1)} %copy-done.6, f32[1536,128]{1,0:T(8,128)} %get-tuple-element.48.refs_2_, s16[2,784,128]{2,1,0:T(8,128)(2,1)} %collective-permute-done.6.refs_3_, ...), custom_call_target="tpu_custom_call" | custom-call | flops 1 | bytes 1 | tf_op jit(solution)/shard_map/add_coded/pallas_call | solution.py:222
  51.7 1.3 collective-permute-start.9
  53.2 1.3 collective-permute-start.15
  54.5 3.3 %collective-permute-done.3.refs_1_ = s16[2,784,128]{2,1,0:T(8,128)(2,1)} collective-permute-done((s16[2,784,128]{2,1,0:T(8,128)(2,1)}, s16[2,784,128]{2,1,0:T(8,128)(2,1)}, u32[]{:S(2)}, u32[]{:S(2)}) %collective-permute-start.3) | collective-permute-done | bytes 401440 | tf_op jit(solution)/shard_map/ppermute | solution.py:493
  57.8 2.6 %add_coded.11 = (s16[2,784,128]{2,1,0:T(8,128)(2,1)}, s16[2,784,128]{2,1,0:T(8,128)(2,1)}) custom-call(f32[1536,128]{1,0:T(8,128)} %get-tuple-element.43.refs_2_.refs_0_, s16[2,784,128]{2,1,0:T(8,128)(2,1)} %collective-permute-done.3.refs_1_, f32[1536,128]{1,0:T(8,128)} %get-tuple-element.46.refs_2_, s16[2,784,128]{2,1,0:T(8,128)(2,1)} %collective-permute-done.4.refs_3_, ...), custom_call_target="tpu_custom_call" | custom-call | flops 1 | bytes 1 | tf_op jit(solution)/shard_map/add_coded/pallas_call | solution.py:222
  60.5 1.5 collective-permute-start.12
  62.0 11.4 %collective-permute-done.2.refs_1_ = s16[6,144,128]{2,1,0:T(8,128)(2,1)} collective-permute-done((s16[6,144,128]{2,1,0:T(8,128)(2,1)}, s16[6,144,128]{2,1,0:T(8,128)(2,1)}, u32[]{:S(2)}, u32[]{:S(2)}) %collective-permute-start.2) | collective-permute-done | bytes 221216 | tf_op jit(solution)/shard_map/ppermute | solution.py:499
  73.3 1.5 collective-permute-start.13
  74.8 2.3 %collective-permute-start.18 = (bf16[1536,128]{1,0:T(8,128)(2,1)S(1)}, bf16[1536,128]{1,0:T(8,128)(2,1)}, u32[]{:S(2)}, u32[]{:S(2)}) collective-permute-start(bf16[1536,128]{1,0:T(8,128)(2,1)S(1)} %collective-permute-done.9.refs_3_.refs_9_), channel_id=1, source_target_pairs={{0,1},{2,0},{4,2},{6,4},{7,6},{5,7},{3,5},{1,3},{8,9},{10,8},{12,1... | collective-permute-start | bytes 1179656 | tf_op jit(solution)/shard_map/ppermute | solution.py:496
  77.1 2.0 %add_coded.12 = (f32[768,128]{1,0:T(8,128)}, s16[6,144,128]{2,1,0:T(8,128)(2,1)}) custom-call(f32[768,128]{1,0:T(8,128)} %get-tuple-element.44.refs_4_.refs_0_, s16[6,144,128]{2,1,0:T(8,128)(2,1)} %collective-permute-done.2.refs_1_, s16[2,784,128]{2,1,0:T(8,128)(2,1)} %get-tuple-element.52.refs_2_, bf16[1536,128]{1,0:T(8,128)(2,1)} %copy-done.5, ...), custom_call_target="tpu_custom_call" | custom-call | flops 1 | bytes 1 | tf_op jit(solution)/shard_map/add_coded/pallas_call | solution.py:222
  79.1 2.7 %collective-permute-done.16.refs_5_.refs_10_ = bf16[1536,128]{1,0:T(8,128)(2,1)} collective-permute-done((bf16[1536,128]{1,0:T(8,128)(2,1)}, bf16[1536,128]{1,0:T(8,128)(2,1)}, u32[]{:S(2)}, u32[]{:S(2)}) %collective-permute-start.16) | collective-permute-done | bytes 393248 | tf_op jit(solution)/shard_map/ppermute | solution.py:496
  81.8 2.1 %collective-permute-start.11 = (s16[6,144,128]{2,1,0:T(8,128)(2,1)}, s16[6,144,128]{2,1,0:T(8,128)(2,1)}, u32[]{:S(2)}, u32[]{:S(2)}) collective-permute-start(s16[6,144,128]{2,1,0:T(8,128)(2,1)} %get-tuple-element.55), channel_id=1, source_target_pairs={{0,4},{1,5},{2,6},{3,7},{4,0},{5,1},{6,2},{7,3},{8,12},{9,13},{10,... | collective-permute-start | bytes 663560 | tf_op jit(solution)/shard_map/ppermute | solution.py:499
  83.9 2.6 %add_coded.13 = (s16[2,784,128]{2,1,0:T(8,128)(2,1)}, s16[2,784,128]{2,1,0:T(8,128)(2,1)}) custom-call(f32[1536,128]{1,0:T(8,128)} %get-tuple-element.59.refs_0_, s16[2,784,128]{2,1,0:T(8,128)(2,1)} %collective-permute-done.14.refs_1_, f32[1536,128]{1,0:T(8,128)} %get-tuple-element.60.refs_2_, s16[2,784,128]{2,1,0:T(8,128)(2,1)} %collective-permute-done.15.refs_3_, ...), custom_call_target="tpu_custom_call" | custom-call | flops 1 | bytes 1 | tf_op jit(solution)/shard_map/add_coded/pallas_call | solution.py:222
  86.6 3.8 %collective-permute-done.13.refs_3_ = s16[2,784,128]{2,1,0:T(8,128)(2,1)} collective-permute-done((s16[2,784,128]{2,1,0:T(8,128)(2,1)}, s16[2,784,128]{2,1,0:T(8,128)(2,1)}, u32[]{:S(2)}, u32[]{:S(2)}) %collective-permute-start.13) | collective-permute-done | bytes 401440 | tf_op jit(solution)/shard_map/ppermute | solution.py:496
  90.4 2.6 %add_coded.14 = (s16[2,784,128]{2,1,0:T(8,128)(2,1)}, s16[2,784,128]{2,1,0:T(8,128)(2,1)}) custom-call(f32[1536,128]{1,0:T(8,128)} %get-tuple-element.56.refs_0_, s16[2,784,128]{2,1,0:T(8,128)(2,1)} %collective-permute-done.12.refs_1_, f32[1536,128]{1,0:T(8,128)} %get-tuple-element.57.refs_2_, s16[2,784,128]{2,1,0:T(8,128)(2,1)} %collective-permute-done.13.refs_3_, ...), custom_call_target="tpu_custom_call" | custom-call | flops 1 | bytes 1 | tf_op jit(solution)/shard_map/add_coded/pallas_call | solution.py:222
  93.0 2.4 %collective-permute-start.19 = (bf16[1536,128]{1,0:T(8,128)(2,1)S(1)}, bf16[1536,128]{1,0:T(8,128)(2,1)}, u32[]{:S(2)}, u32[]{:S(2)}) collective-permute-start(bf16[1536,128]{1,0:T(8,128)(2,1)S(1)} %copy-done.4), channel_id=1, source_target_pairs={{0,2},{2,4},{4,6},{6,7},{7,5},{5,3},{3,1},{1,0},{8,10},{10,12},{12... | collective-permute-start | bytes 1179656 | tf_op jit(solution)/shard_map/ppermute | solution.py:493
  95.4 3.9 %collective-permute-done.11.refs_1_ = s16[6,144,128]{2,1,0:T(8,128)(2,1)} collective-permute-done((s16[6,144,128]{2,1,0:T(8,128)(2,1)}, s16[6,144,128]{2,1,0:T(8,128)(2,1)}, u32[]{:S(2)}, u32[]{:S(2)}) %collective-permute-start.11) | collective-permute-done | bytes 221216 | tf_op jit(solution)/shard_map/ppermute | solution.py:499
  99.3 5.7 %collective-permute-start.24 = (bf16[1536,128]{1,0:T(8,128)(2,1)}, bf16[1536,128]{1,0:T(8,128)(2,1)}, u32[]{:S(2)}, u32[]{:S(2)}) collective-permute-start(bf16[1536,128]{1,0:T(8,128)(2,1)} %collective-permute-done.16.refs_5_.refs_10_), channel_id=1, source_target_pairs={{0,1},{2,0},{4,2},{6,4},{7,6},{5,7},{3,5},{1,3},{8,9},{10,8},{12,1... | collective-permute-start | bytes 1179656 | tf_op jit(solution)/shard_map/ppermute | solution.py:496
  105.0 9.8 %collective-permute-done.19.refs_4_.refs_14_ = bf16[1536,128]{1,0:T(8,128)(2,1)} collective-permute-done((bf16[1536,128]{1,0:T(8,128)(2,1)S(1)}, bf16[1536,128]{1,0:T(8,128)(2,1)}, u32[]{:S(2)}, u32[]{:S(2)}) %collective-permute-start.19) | collective-permute-done | bytes 393248 | tf_op jit(solution)/shard_map/ppermute | solution.py:493
  114.8 1.6 collective-permute-start.22
  116.4 1.9 add_coded.15.refs_2_.low_ref.refs_16_
  118.2 6.2 %collective-permute-start.26 = (s16[2,784,128]{2,1,0:T(8,128)(2,1)}, s16[2,784,128]{2,1,0:T(8,128)(2,1)}, u32[]{:S(2)}, u32[]{:S(2)}) collective-permute-start(s16[2,784,128]{2,1,0:T(8,128)(2,1)} %get-tuple-element.69), channel_id=1, source_target_pairs={{0,1},{2,0},{4,2},{6,4},{7,6},{5,7},{3,5},{1,3},{8,9},{10,8},{12,1... | collective-permute-start | bytes 1204232 | tf_op jit(solution)/shard_map/ppermute | solution.py:496
  124.4 2.1 %add_coded.16.refs_2_ = s16[2,784,128]{2,1,0:T(8,128)(2,1)} custom-call(f32[1536,128]{1,0:T(8,128)} %get-tuple-element.65.refs_0_, s16[2,784,128]{2,1,0:T(8,128)(2,1)} %collective-permute-done.20.refs_1_, f32[768,128]{1,0:T(8,128)} %add_coded.15.refs_2_.low_ref.refs_16_), custom_call_target="tpu_custom_call" | custom-call | flops 1 | bytes 1 | tf_op jit(solution)/shard_map/add_coded/pallas_call | solution.py:222
  126.5 2.1 %add_coded.17.refs_0_ = s16[2,784,128]{2,1,0:T(8,128)(2,1)} custom-call(f32[1536,128]{1,0:T(8,128)} %get-tuple-element.68.refs_0_, s16[2,784,128]{2,1,0:T(8,128)(2,1)} %collective-permute-done.23.refs_1_, s16[2,784,128]{2,1,0:T(8,128)(2,1)} %add_coded.16.refs_2_, bf16[1536,128]{1,0:T(8,128)(2,1)} %collective-permute-done.24.refs_3_.refs_11_), custom_call_target="tpu_custom_call" | custom-call | flops 1 | bytes 1 | tf_op jit(solution)/shard_map/add_coded/pallas_call | solution.py:222
  129.4 9.2 %factor_gradients.1.refs_6_ = f32[256,1152]{1,0:T(8,128)} custom-call(s32[24]{0:T(128)} %job_ref.9, bf16[3072,1024]{1,0:T(8,128)(2,1)} %x_ref.11, bf16[3072,128]{1,0:T(8,128)(2,1)} %get-tuple-element.38.refs_2_.dy_ref, f32[768,128]{1,0:T(8,128)} %add_coded.15.refs_2_.low_ref.refs_16_, s16[2,784,128]{2,1,0:T(8,128)(2,1)} %add_coded.17.refs_0_, ...), custom_call_target="tpu_custom_call" | custom-call | flops 1 | bytes 1 | tf_op jit(solution)/shard_map/factor_gradients/pallas_call | solution.py:346
  138.6 1.9 %constant_dynamic-slice_fusion = f32[128,1152]{1,0:T(8,128)} fusion(f32[256,1152]{1,0:T(8,128)} %factor_gradients.1.refs_6_, s32[]{:T(128)S(6)} %select_n.51), kind=kLoop, calls=%fused_computation.7 | loop fusion | bytes 1179652 | tf_op jit(solution)/shard_map/dynamic_slice | solution.py:576
  140.6 4.0 %collective-permute-start.33 = (f32[128,1152]{1,0:T(8,128)}, f32[128,1152]{1,0:T(8,128)}, u32[]{:S(2)}, u32[]{:S(2)}) collective-permute-start(f32[128,1152]{1,0:T(8,128)} %constant_dynamic-slice_fusion), channel_id=1, source_target_pairs={{0,8},{8,0},{1,9},{9,1},{2,10},{10,2},{3,11},{11,3},{4,12},{12,4},... | collective-permute-start | bytes 1769480 | tf_op jit(solution)/shard_map/ppermute | solution.py:576
  146.4 4.0 %copy.14 = bf16[1024,1024]{0,1:T(8,128)(2,1)} copy(bf16[1024,1024]{1,0:T(8,128)(2,1)} %refs_5_.3) | data formatting | bytes 4194304 | tf_op args[4]
  151.9 1.3 collective-permute-start.29
  153.2 4.5 %place_output.1.refs_18_ = bf16[32,128,128]{2,1,0:T(8,128)(2,1)} custom-call(s32[24]{0:T(128)} %group_ref.3, s32[24]{0:T(128)} %slot_ref.3, s32[24]{0:T(128)} %job_ref.9, s32[1]{0:T(128)} %bitcast.me_ref, f32[768,128]{1,0:T(8,128)} %add_coded.15.refs_2_.low_ref.refs_16_, bf16[256,128]{1,0:T(8,128)(2,1)} %b_ref.1, f32[1536,128]{1,0:T(8,128)} %get-tuple-element.64.refs_0_, ...), custom_call_target="tpu_custom_call" | custom-call | flops 1 | bytes 1 | tf_op jit(solution)/shard_map/place_output/pallas_call | solution.py:395
  157.7 2.1 %fusion.1 = (bf16[16,128,128]{2,1,0:T(8,128)(2,1)S(1)}, bf16[16,128,128]{2,1,0:T(8,128)(2,1)}) fusion(bf16[32,128,128]{2,1,0:T(8,128)(2,1)} %place_output.1.refs_18_), kind=kLoop, calls=%fused_computation.10 | loop fusion | bytes 2097152 | tf_op jit(solution)/shard_map/slice | solution.py:587
  160.5 9.9 %input_gradient.2.refs_18_ = bf16[3072,1024]{1,0:T(8,128)(2,1)} custom-call(s32[24]{0:T(128)} %job_ref.9, s32[8]{0:T(128)} %compare_select_fusion.2.place_ref, bf16[1024,1024]{1,0:T(8,128)(2,1)} %bitcast.9, bf16[1024,1024]{1,0:T(8,128)(2,1)} %bitcast.10, bf16[1024,1024]{1,0:T(8,128)(2,1)} %bitcast.11, bf16[1024,1024]{1,0:T(8,128)(2,1)} %bitcast.12, ...), custom_call_target="tpu_custom_call" | custom-call | flops 1 | bytes 1 | tf_op jit(solution)/shard_map/input_gradient/pallas_call | solution.py:447
  170.4 1.3 dynamic-slice_add_fusion
  173.4 2.5 %maximum_select_fusion.refs_19_ = bf16[4096,128]{1,0:T(8,128)(2,1)} fusion(bf16[2048,128]{1,0:T(8,128)(2,1)} %collective-permute-done.28, bf16[2048,128]{1,0:T(8,128)(2,1)S(1)} %bitcast.27, pred[]{:T(512)S(6)} %eq.10), kind=kLoop, calls=%fused_computation | loop fusion | flops 4718592 | bytes 2097153 | tf_op jit(solution)/shard_map/jit(_where)/select_n | solution.py:586
  175.9 9.9 %input_gradient.3 = bf16[3072,1024]{1,0:T(8,128)(2,1)} custom-call(s32[24]{0:T(128)} %job_ref.9, s32[8]{0:T(128)} %compare_select_fusion.2.place_ref, bf16[1024,1024]{1,0:T(8,128)(2,1)} %bitcast.17, bf16[1024,1024]{1,0:T(8,128)(2,1)} %bitcast.18, bf16[1024,1024]{1,0:T(8,128)(2,1)} %bitcast.19, ...), custom_call_target="tpu_custom_call", output_to_operand_aliasing={{}: (20, {})} | custom-call | flops 1 | bytes 1 | tf_op jit(solution)/shard_map/input_gradient/pallas_call | solution.py:447
  (69 shorter events, 11.2 us)
Async XLA Ops:
  1.7 9.4 %collective-permute-start = (bf16[2048,128]{1,0:T(8,128)(2,1)S(1)}, bf16[2048,128]{1,0:T(8,128)(2,1)}, u32[]{:S(2)}, u32[]{:S(2)}) collective-permute-start(bf16[2048,128]{1,0:T(8,128)(2,1)S(1)} %constant_dynamic-slice_fusion.1), channel_id=1, source_target_pairs={{0,8},{8,0},{1,9},{9,1},{2,10},{10,2},{3,11},{11,3},{4,12},{12,4},... | collective-permute-start | bytes 1572872 | tf_op jit(solution)/shard_map/ppermute | solution.py:502
  6.8 21.4 %collective-permute-start.5 = (s16[2,784,128]{2,1,0:T(8,128)(2,1)}, s16[2,784,128]{2,1,0:T(8,128)(2,1)S(1)}, u32[]{:S(2)}, u32[]{:S(2)}) collective-permute-start(s16[2,784,128]{2,1,0:T(8,128)(2,1)} %get-tuple-element.37.refs_0_), channel_id=1, source_target_pairs={{0,2},{2,4},{4,6},{6,7},{7,5},{5,3},{3,1},{1,0},{8,10},{10,12},{12... | collective-permute-start | bytes 1204232 | tf_op jit(solution)/shard_map/ppermute | solution.py:493
  9.6 20.7 %collective-permute-start.6 = (s16[2,784,128]{2,1,0:T(8,128)(2,1)}, s16[2,784,128]{2,1,0:T(8,128)(2,1)}, u32[]{:S(2)}, u32[]{:S(2)}) collective-permute-start(s16[2,784,128]{2,1,0:T(8,128)(2,1)} %get-tuple-element.49), channel_id=1, source_target_pairs={{0,1},{2,0},{4,2},{6,4},{7,6},{5,7},{3,5},{1,3},{8,9},{10,8},{12,1... | collective-permute-start | bytes 1204232 | tf_op jit(solution)/shard_map/ppermute | solution.py:496
  25.3 7.0 %collective-permute-start.1 = (s16[6,144,128]{2,1,0:T(8,128)(2,1)}, s16[6,144,128]{2,1,0:T(8,128)(2,1)S(1)}, u32[]{:S(2)}, u32[]{:S(2)}) collective-permute-start(s16[6,144,128]{2,1,0:T(8,128)(2,1)} %get-tuple-element.41.refs_6_), channel_id=1, source_target_pairs={{0,1},{1,0},{2,3},{3,2},{4,5},{5,4},{6,7},{7,6},{8,9},{9,8},{10,11... | collective-permute-start | bytes 663560 | tf_op jit(solution)/shard_map/ppermute | solution.py:499
  26.7 25.0 %collective-permute-start.7 = (bf16[1536,128]{1,0:T(8,128)(2,1)}, bf16[1536,128]{1,0:T(8,128)(2,1)}, u32[]{:S(2)}, u32[]{:S(2)}) collective-permute-start(bf16[1536,128]{1,0:T(8,128)(2,1)} %get-tuple-element.51.refs_8_), channel_id=1, source_target_pairs={{0,1},{2,0},{4,2},{6,4},{7,6},{5,7},{3,5},{1,3},{8,9},{10,8},{12,1... | collective-permute-start | bytes 1179656 | tf_op jit(solution)/shard_map/ppermute | solution.py:496
  26.8 26.3 %collective-permute-start.8 = (bf16[1536,128]{1,0:T(8,128)(2,1)}, bf16[1536,128]{1,0:T(8,128)(2,1)}, u32[]{:S(2)}, u32[]{:S(2)}) collective-permute-start(bf16[1536,128]{1,0:T(8,128)(2,1)} %get-tuple-element.51.refs_8_), channel_id=1, source_target_pairs={{0,2},{2,4},{4,6},{6,7},{7,5},{5,3},{3,1},{1,0},{8,10},{10,12},{12... | collective-permute-start | bytes 1179656 | tf_op jit(solution)/shard_map/ppermute | solution.py:493
  28.2 0.7 copy-start.6
  29.0 24.3 %collective-permute-start.10 = (bf16[1536,128]{1,0:T(8,128)(2,1)}, bf16[1536,128]{1,0:T(8,128)(2,1)S(1)}, u32[]{:S(2)}, u32[]{:S(2)}) collective-permute-start(bf16[1536,128]{1,0:T(8,128)(2,1)} %get-tuple-element.53.refs_8_), channel_id=1, source_target_pairs={{0,2},{2,4},{4,6},{6,7},{7,5},{5,3},{3,1},{1,0},{8,10},{10,12},{12... | collective-permute-start | bytes 1179656 | tf_op jit(solution)/shard_map/ppermute | solution.py:493
  30.3 27.6 %collective-permute-start.3 = (s16[2,784,128]{2,1,0:T(8,128)(2,1)}, s16[2,784,128]{2,1,0:T(8,128)(2,1)}, u32[]{:S(2)}, u32[]{:S(2)}) collective-permute-start(s16[2,784,128]{2,1,0:T(8,128)(2,1)} %get-tuple-element.39.refs_0_), channel_id=1, source_target_pairs={{0,2},{2,4},{4,6},{6,7},{7,5},{5,3},{3,1},{1,0},{8,10},{10,12},{12... | collective-permute-start | bytes 1204232 | tf_op jit(solution)/shard_map/ppermute | solution.py:493
  32.4 7.9 %copy-start.8 = (s16[6,144,128]{2,1,0:T(8,128)(2,1)}, s16[6,144,128]{2,1,0:T(8,128)(2,1)S(1)}, u32[]{:S(2)}) copy-start(s16[6,144,128]{2,1,0:T(8,128)(2,1)S(1)} %collective-permute-done.1.refs_1_) | copy-start | bytes 663556
  32.4 25.5 %collective-permute-start.4 = (s16[2,784,128]{2,1,0:T(8,128)(2,1)}, s16[2,784,128]{2,1,0:T(8,128)(2,1)}, u32[]{:S(2)}, u32[]{:S(2)}) collective-permute-start(s16[2,784,128]{2,1,0:T(8,128)(2,1)} %get-tuple-element.47), channel_id=1, source_target_pairs={{0,1},{2,0},{4,2},{6,4},{7,6},{5,7},{3,5},{1,3},{8,9},{10,8},{12,1... | collective-permute-start | bytes 1204232 | tf_op jit(solution)/shard_map/ppermute | solution.py:496
  51.7 8.7 %collective-permute-start.9 = (bf16[1536,128]{1,0:T(8,128)(2,1)}, bf16[1536,128]{1,0:T(8,128)(2,1)S(1)}, u32[]{:S(2)}, u32[]{:S(2)}) collective-permute-start(bf16[1536,128]{1,0:T(8,128)(2,1)} %get-tuple-element.53.refs_8_), channel_id=1, source_target_pairs={{0,1},{2,0},{4,2},{6,4},{7,6},{5,7},{3,5},{1,3},{8,9},{10,8},{12,1... | collective-permute-start | bytes 1179656 | tf_op jit(solution)/shard_map/ppermute | solution.py:496
  53.1 21.7 %collective-permute-start.14 = (s16[2,784,128]{2,1,0:T(8,128)(2,1)}, s16[2,784,128]{2,1,0:T(8,128)(2,1)}, u32[]{:S(2)}, u32[]{:S(2)}) collective-permute-start(s16[2,784,128]{2,1,0:T(8,128)(2,1)} %get-tuple-element.50.refs_4_), channel_id=1, source_target_pairs={{0,2},{2,4},{4,6},{6,7},{7,5},{5,3},{3,1},{1,0},{8,10},{10,12},{12... | collective-permute-start | bytes 1204232 | tf_op jit(solution)/shard_map/ppermute | solution.py:493
  53.2 23.8 %copy-start.3 = (bf16[1536,128]{1,0:T(8,128)(2,1)}, bf16[1536,128]{1,0:T(8,128)(2,1)S(1)}, u32[]{:S(2)}) copy-start(bf16[1536,128]{1,0:T(8,128)(2,1)S(1)} %collective-permute-done.10.refs_4_.refs_15_) | copy-start | bytes 1179652
  53.2 21.6 %collective-permute-start.15 = (s16[2,784,128]{2,1,0:T(8,128)(2,1)}, s16[2,784,128]{2,1,0:T(8,128)(2,1)}, u32[]{:S(2)}, u32[]{:S(2)}) collective-permute-start(s16[2,784,128]{2,1,0:T(8,128)(2,1)} %get-tuple-element.61), channel_id=1, source_target_pairs={{0,1},{2,0},{4,2},{6,4},{7,6},{5,7},{3,5},{1,3},{8,9},{10,8},{12,1... | collective-permute-start | bytes 1204232 | tf_op jit(solution)/shard_map/ppermute | solution.py:496
  57.8 15.5 %collective-permute-start.2 = (s16[6,144,128]{2,1,0:T(8,128)(2,1)}, s16[6,144,128]{2,1,0:T(8,128)(2,1)}, u32[]{:S(2)}, u32[]{:S(2)}) collective-permute-start(s16[6,144,128]{2,1,0:T(8,128)(2,1)} %get-tuple-element.45), channel_id=1, source_target_pairs={{0,2},{1,3},{2,0},{3,1},{4,6},{5,7},{6,4},{7,5},{8,10},{9,11},{10,... | collective-permute-start | bytes 663560 | tf_op jit(solution)/shard_map/ppermute | solution.py:499
  57.8 23.9 %collective-permute-start.16 = (bf16[1536,128]{1,0:T(8,128)(2,1)}, bf16[1536,128]{1,0:T(8,128)(2,1)}, u32[]{:S(2)}, u32[]{:S(2)}) collective-permute-start(bf16[1536,128]{1,0:T(8,128)(2,1)} %collective-permute-done.7.refs_5_.refs_9_), channel_id=1, source_target_pairs={{0,1},{2,0},{4,2},{6,4},{7,6},{5,7},{3,5},{1,3},{8,9},{10,8},{12,1... | collective-permute-start | bytes 1179656 | tf_op jit(solution)/shard_map/ppermute | solution.py:496
  60.4 16.6 %copy-start.5 = (bf16[1536,128]{1,0:T(8,128)(2,1)}, bf16[1536,128]{1,0:T(8,128)(2,1)S(1)}, u32[]{:S(2)}) copy-start(bf16[1536,128]{1,0:T(8,128)(2,1)S(1)} %collective-permute-done.9.refs_3_.refs_9_) | copy-start | bytes 1179652
  60.5 26.1 %collective-permute-start.12 = (s16[2,784,128]{2,1,0:T(8,128)(2,1)}, s16[2,784,128]{2,1,0:T(8,128)(2,1)}, u32[]{:S(2)}, u32[]{:S(2)}) collective-permute-start(s16[2,784,128]{2,1,0:T(8,128)(2,1)} %get-tuple-element.52.refs_2_), channel_id=1, source_target_pairs={{0,2},{2,4},{4,6},{6,7},{7,5},{5,3},{3,1},{1,0},{8,10},{10,12},{12... | collective-permute-start | bytes 1204232 | tf_op jit(solution)/shard_map/ppermute | solution.py:493
  73.3 17.0 %collective-permute-start.13 = (s16[2,784,128]{2,1,0:T(8,128)(2,1)}, s16[2,784,128]{2,1,0:T(8,128)(2,1)}, u32[]{:S(2)}, u32[]{:S(2)}) collective-permute-start(s16[2,784,128]{2,1,0:T(8,128)(2,1)} %get-tuple-element.58), channel_id=1, source_target_pairs={{0,1},{2,0},{4,2},{6,4},{7,6},{5,7},{3,5},{1,3},{8,9},{10,8},{12,1... | collective-permute-start | bytes 1204232 | tf_op jit(solution)/shard_map/ppermute | solution.py:496
  74.8 11.7 %collective-permute-start.17 = (bf16[1536,128]{1,0:T(8,128)(2,1)}, bf16[1536,128]{1,0:T(8,128)(2,1)}, u32[]{:S(2)}, u32[]{:S(2)}) collective-permute-start(bf16[1536,128]{1,0:T(8,128)(2,1)} %collective-permute-done.8.refs_6_.refs_15_), channel_id=1, source_target_pairs={{0,2},{2,4},{4,6},{6,7},{7,5},{5,3},{3,1},{1,0},{8,10},{10,12},{12... | collective-permute-start | bytes 1179656 | tf_op jit(solution)/shard_map/ppermute | solution.py:493
  74.8 30.2 %collective-permute-start.18 = (bf16[1536,128]{1,0:T(8,128)(2,1)S(1)}, bf16[1536,128]{1,0:T(8,128)(2,1)}, u32[]{:S(2)}, u32[]{:S(2)}) collective-permute-start(bf16[1536,128]{1,0:T(8,128)(2,1)S(1)} %collective-permute-done.9.refs_3_.refs_9_), channel_id=1, source_target_pairs={{0,1},{2,0},{4,2},{6,4},{7,6},{5,7},{3,5},{1,3},{8,9},{10,8},{12,1... | collective-permute-start | bytes 1179656 | tf_op jit(solution)/shard_map/ppermute | solution.py:496
  81.8 17.5 %collective-permute-start.11 = (s16[6,144,128]{2,1,0:T(8,128)(2,1)}, s16[6,144,128]{2,1,0:T(8,128)(2,1)}, u32[]{:S(2)}, u32[]{:S(2)}) collective-permute-start(s16[6,144,128]{2,1,0:T(8,128)(2,1)} %get-tuple-element.55), channel_id=1, source_target_pairs={{0,4},{1,5},{2,6},{3,7},{4,0},{5,1},{6,2},{7,3},{8,12},{9,13},{10,... | collective-permute-start | bytes 663560 | tf_op jit(solution)/shard_map/ppermute | solution.py:499
  86.5 6.5 %copy-start.4 = (bf16[1536,128]{1,0:T(8,128)(2,1)S(1)}, bf16[1536,128]{1,0:T(8,128)(2,1)}, u32[]{:S(2)}) copy-start(bf16[1536,128]{1,0:T(8,128)(2,1)} %copy-done.3) | copy-start | bytes 1179652
  86.5 31.7 %collective-permute-start.20 = (s16[2,784,128]{2,1,0:T(8,128)(2,1)}, s16[2,784,128]{2,1,0:T(8,128)(2,1)}, u32[]{:S(2)}, u32[]{:S(2)}) collective-permute-start(s16[2,784,128]{2,1,0:T(8,128)(2,1)} %get-tuple-element.62.refs_4_), channel_id=1, source_target_pairs={{0,2},{2,4},{4,6},{6,7},{7,5},{5,3},{3,1},{1,0},{8,10},{10,12},{12... | collective-permute-start | bytes 1204232 | tf_op jit(solution)/shard_map/ppermute | solution.py:493
  93.0 33.6 %collective-permute-start.23 = (s16[2,784,128]{2,1,0:T(8,128)(2,1)}, s16[2,784,128]{2,1,0:T(8,128)(2,1)}, u32[]{:S(2)}, u32[]{:S(2)}) collective-permute-start(s16[2,784,128]{2,1,0:T(8,128)(2,1)} %get-tuple-element.63.refs_2_), channel_id=1, source_target_pairs={{0,2},{2,4},{4,6},{6,7},{7,5},{5,3},{3,1},{1,0},{8,10},{10,12},{12... | collective-permute-start | bytes 1204232 | tf_op jit(solution)/shard_map/ppermute | solution.py:493
  93.0 21.8 %collective-permute-start.19 = (bf16[1536,128]{1,0:T(8,128)(2,1)S(1)}, bf16[1536,128]{1,0:T(8,128)(2,1)}, u32[]{:S(2)}, u32[]{:S(2)}) collective-permute-start(bf16[1536,128]{1,0:T(8,128)(2,1)S(1)} %copy-done.4), channel_id=1, source_target_pairs={{0,2},{2,4},{4,6},{6,7},{7,5},{5,3},{3,1},{1,0},{8,10},{10,12},{12... | collective-permute-start | bytes 1179656 | tf_op jit(solution)/shard_map/ppermute | solution.py:493
  99.3 27.3 %collective-permute-start.24 = (bf16[1536,128]{1,0:T(8,128)(2,1)}, bf16[1536,128]{1,0:T(8,128)(2,1)}, u32[]{:S(2)}, u32[]{:S(2)}) collective-permute-start(bf16[1536,128]{1,0:T(8,128)(2,1)} %collective-permute-done.16.refs_5_.refs_10_), channel_id=1, source_target_pairs={{0,1},{2,0},{4,2},{6,4},{7,6},{5,7},{3,5},{1,3},{8,9},{10,8},{12,1... | collective-permute-start | bytes 1179656 | tf_op jit(solution)/shard_map/ppermute | solution.py:496
  105.0 23.6 %collective-permute-start.27 = (bf16[1536,128]{1,0:T(8,128)(2,1)}, bf16[1536,128]{1,0:T(8,128)(2,1)S(1)}, u32[]{:S(2)}, u32[]{:S(2)}) collective-permute-start(bf16[1536,128]{1,0:T(8,128)(2,1)} %collective-permute-done.18.refs_3_.refs_10_), channel_id=1, source_target_pairs={{0,1},{2,0},{4,2},{6,4},{7,6},{5,7},{3,5},{1,3},{8,9},{10,8},{12,1... | collective-permute-start | bytes 1179656 | tf_op jit(solution)/shard_map/ppermute | solution.py:496
  114.8 29.8 %collective-permute-start.22 = (s16[2,784,128]{2,1,0:T(8,128)(2,1)}, s16[2,784,128]{2,1,0:T(8,128)(2,1)S(1)}, u32[]{:S(2)}, u32[]{:S(2)}) collective-permute-start(s16[2,784,128]{2,1,0:T(8,128)(2,1)} %get-tuple-element.66), channel_id=1, source_target_pairs={{0,1},{2,0},{4,2},{6,4},{7,6},{5,7},{3,5},{1,3},{8,9},{10,8},{12,1... | collective-permute-start | bytes 1204232 | tf_op jit(solution)/shard_map/ppermute | solution.py:496
  118.2 26.9 %collective-permute-start.26 = (s16[2,784,128]{2,1,0:T(8,128)(2,1)}, s16[2,784,128]{2,1,0:T(8,128)(2,1)}, u32[]{:S(2)}, u32[]{:S(2)}) collective-permute-start(s16[2,784,128]{2,1,0:T(8,128)(2,1)} %get-tuple-element.69), channel_id=1, source_target_pairs={{0,1},{2,0},{4,2},{6,4},{7,6},{5,7},{3,5},{1,3},{8,9},{10,8},{12,1... | collective-permute-start | bytes 1204232 | tf_op jit(solution)/shard_map/ppermute | solution.py:496
  126.5 24.9 %collective-permute-start.21 = (s16[2,784,128]{2,1,0:T(8,128)(2,1)}, s16[2,784,128]{2,1,0:T(8,128)(2,1)}, u32[]{:S(2)}, u32[]{:S(2)}) collective-permute-start(s16[2,784,128]{2,1,0:T(8,128)(2,1)} %add_coded.16.refs_2_), channel_id=1, source_target_pairs={{0,2},{2,4},{4,6},{6,7},{7,5},{5,3},{3,1},{1,0},{8,10},{10,12},{12... | collective-permute-start | bytes 1204232 | tf_op jit(solution)/shard_map/ppermute | solution.py:493
  128.6 23.3 %collective-permute-start.25 = (s16[2,784,128]{2,1,0:T(8,128)(2,1)}, s16[2,784,128]{2,1,0:T(8,128)(2,1)}, u32[]{:S(2)}, u32[]{:S(2)}) collective-permute-start(s16[2,784,128]{2,1,0:T(8,128)(2,1)} %add_coded.17.refs_0_), channel_id=1, source_target_pairs={{0,2},{2,4},{4,6},{6,7},{7,5},{5,3},{3,1},{1,0},{8,10},{10,12},{12... | collective-permute-start | bytes 1204232 | tf_op jit(solution)/shard_map/ppermute | solution.py:493
  128.6 0.7 copy-start.1
  140.6 29.8 %collective-permute-start.33 = (f32[128,1152]{1,0:T(8,128)}, f32[128,1152]{1,0:T(8,128)}, u32[]{:S(2)}, u32[]{:S(2)}) collective-permute-start(f32[128,1152]{1,0:T(8,128)} %constant_dynamic-slice_fusion), channel_id=1, source_target_pairs={{0,8},{8,0},{1,9},{9,1},{2,10},{10,2},{3,11},{11,3},{4,12},{12,4},... | collective-permute-start | bytes 1769480 | tf_op jit(solution)/shard_map/ppermute | solution.py:576
  144.6 5.8 %copy-start.7 = (s16[2,784,128]{2,1,0:T(8,128)(2,1)}, s16[2,784,128]{2,1,0:T(8,128)(2,1)S(1)}, u32[]{:S(2)}) copy-start(s16[2,784,128]{2,1,0:T(8,128)(2,1)S(1)} %collective-permute-done.22.refs_2_) | copy-start | bytes 1204228
  144.6 15.2 %collective-permute-start.32 = (bf16[1536,128]{1,0:T(8,128)(2,1)}, bf16[1536,128]{1,0:T(8,128)(2,1)}, u32[]{:S(2)}, u32[]{:S(2)}) collective-permute-start(bf16[1536,128]{1,0:T(8,128)(2,1)} %collective-permute-done.17.refs_6_.refs_14_), channel_id=1, source_target_pairs={{0,2},{2,4},{4,6},{6,7},{7,5},{5,3},{3,1},{1,0},{8,10},{10,12},{12... | collective-permute-start | bytes 1179656 | tf_op jit(solution)/shard_map/ppermute | solution.py:493
  145.1 15.3 %collective-permute-start.31 = (bf16[1536,128]{1,0:T(8,128)(2,1)}, bf16[1536,128]{1,0:T(8,128)(2,1)}, u32[]{:S(2)}, u32[]{:S(2)}) collective-permute-start(bf16[1536,128]{1,0:T(8,128)(2,1)} %collective-permute-done.24.refs_3_.refs_11_), channel_id=1, source_target_pairs={{0,1},{2,0},{4,2},{6,4},{7,6},{5,7},{3,5},{1,3},{8,9},{10,8},{12,1... | collective-permute-start | bytes 1179656 | tf_op jit(solution)/shard_map/ppermute | solution.py:496
  146.4 4.0 %copy-start = (bf16[1024,256]{1,0:T(8,128)(2,1)S(1)}, bf16[1024,256]{1,0:T(8,128)(2,1)}, u32[]{:S(2)}) copy-start(bf16[1024,256]{1,0:T(8,128)(2,1)} %a_ref.1) | copy-start | bytes 1572868
  146.4 5.5 %copy-start.2 = (bf16[1536,128]{1,0:T(8,128)(2,1)S(1)}, bf16[1536,128]{1,0:T(8,128)(2,1)}, u32[]{:S(2)}) copy-start(bf16[1536,128]{1,0:T(8,128)(2,1)} %copy-done.1) | copy-start | bytes 1179652
  151.4 24.4 %collective-permute-start.30 = (bf16[1536,128]{1,0:T(8,128)(2,1)}, bf16[1536,128]{1,0:T(8,128)(2,1)}, u32[]{:S(2)}, u32[]{:S(2)}) collective-permute-start(bf16[1536,128]{1,0:T(8,128)(2,1)} %collective-permute-done.19.refs_4_.refs_14_), channel_id=1, source_target_pairs={{0,2},{2,4},{4,6},{6,7},{7,5},{5,3},{3,1},{1,0},{8,10},{10,12},{12... | collective-permute-start | bytes 1179656 | tf_op jit(solution)/shard_map/ppermute | solution.py:493
  151.9 23.9 %collective-permute-start.29 = (bf16[1536,128]{1,0:T(8,128)(2,1)S(1)}, bf16[1536,128]{1,0:T(8,128)(2,1)}, u32[]{:S(2)}, u32[]{:S(2)}) collective-permute-start(bf16[1536,128]{1,0:T(8,128)(2,1)S(1)} %copy-done.2), channel_id=1, source_target_pairs={{0,1},{2,0},{4,2},{6,4},{7,6},{5,7},{3,5},{1,3},{8,9},{10,8},{12,1... | collective-permute-start | bytes 1179656 | tf_op jit(solution)/shard_map/ppermute | solution.py:496
  159.8 13.6 %collective-permute-start.28 = (bf16[2048,128]{1,0:T(8,128)(2,1)}, bf16[2048,128]{1,0:T(8,128)(2,1)}, u32[]{:S(2)}, u32[]{:S(2)}) collective-permute-start(bf16[2048,128]{1,0:T(8,128)(2,1)} %bitcast.4), channel_id=1, source_target_pairs={{0,8},{8,0},{1,9},{9,1},{2,10},{10,2},{3,11},{11,3},{4,12},{12,4},... | collective-permute-start | bytes 1572872 | tf_op jit(solution)/shard_map/ppermute | solution.py:584

commit v4 on v3

--- a/solution.py
+++ b/solution.py
@@ -153,14 +153,13 @@
     return jax.ShapeDtypeStruct((rows // group_rows, group_rows + PAD, columns), jnp.int16)
 
 
-def project(x, first, rows, w, place, offsets, group_rows, columns, coded, after=()):
+def project(x, first, rows, w, place, offsets, received, plain, group_rows, columns, after):
     features = x.shape[1]
     count = len(offsets)
     start = first // group_rows
 
     def kernel(place_ref, x_ref, *refs):
-        weight_ref = refs[-1]
-        refs = refs[:count] + refs[count + len(after) : -1]
+        weight_ref, outs = refs[-1], refs[-1 - count : -1]
 
         @pl.when(pl.program_id(0) == 0)
         def _():
@@ -170,20 +169,17 @@
         product = dot32(x_ref[...], weight_ref[...], ((1,), (0,)))
         for i in range(count):
             part = product[:, i * columns : (i + 1) * columns]
-            if coded:
-                store_coded(refs[count + i], 0, part)
+            if i < len(received):
+                part = part + load_coded(refs[count + i], 0)
+            if plain and i == count - 1:
+                outs[i][...] = part
             else:
-                refs[count + i][...] = part
+                store_coded(outs[i], 0, part)
 
     def weight_spec(d):
         return pl.BlockSpec((features, columns), lambda g, place_ref: (0, place_ref[d]))
 
-    if coded:
-        out_specs = [coded_spec(group_rows, columns)] * count
-        out_shape = [coded_shape(rows, group_rows, columns)] * count
-    else:
-        out_specs = [pl.BlockSpec((group_rows, columns), lambda g, place_ref: (g, 0))] * count
-        out_shape = [jax.ShapeDtypeStruct((rows, columns), jnp.float32)] * count
+    coded = count - plain
     return pl.pallas_call(
         kernel,
         grid_spec=pltpu.PrefetchScalarGridSpec(
@@ -191,15 +187,18 @@
             grid=(rows // group_rows,),
             in_specs=[pl.BlockSpec((group_rows, features), lambda g, place_ref: (g + start, 0))]
             + [weight_spec(d) for d in offsets]
+            + [coded_spec(group_rows, columns)] * len(received)
             + [ANY] * len(after),
-            out_specs=out_specs,
+            out_specs=[coded_spec(group_rows, columns)] * coded
+            + [pl.BlockSpec((group_rows, columns), lambda g, place_ref: (g, 0))] * plain,
             scratch_shapes=[pltpu.VMEM((features, count * columns), jnp.bfloat16)],
         ),
-        out_shape=out_shape,
+        out_shape=[coded_shape(rows, group_rows, columns)] * coded
+        + [jax.ShapeDtypeStruct((rows, columns), jnp.float32)] * plain,
         compiler_params=params(),
         cost_estimate=cost(),
         name="project",
-    )(place, x, *([w] * count), *after)
+    )(place, x, *([w] * count), *received, *after)
 
 
 def add_coded(pairs, group_rows, after, sums=False, coded=True, groups=1):
@@ -316,13 +315,15 @@
     )(job, x, a, dy_home, b_t, *after)
 
 
-def factor_gradients(x, dy_home, low, job, ranks, length, after):
+def factor_gradients(x, dy_home, low, job, me, ranks, length, after):
     blocks = job.shape[0]
     features = x.shape[1]
     columns = dy_home.shape[1]
 
-    def kernel(job_ref, x_ref, dy_ref, low_ref, *refs):
-        out_ref = refs[-1]
+    part = ranks // 2
+
+    def kernel(job_ref, me_ref, x_ref, dy_ref, low_ref, *refs):
+        kept_ref, sent_ref, out_ref = refs[-3:]
         step = pl.program_id(0)
         spread = []
         for kind in range(2):
@@ -341,26 +342,32 @@
         out_ref[:, pl.ds(0, features)] += down[:ranks] + down[ranks:]
         out_ref[:, pl.ds(features, columns)] += up[:ranks] + up[ranks:]
 
+        @pl.when(step == blocks // PACKED - 1)
+        def _():
+            kept_ref[...] = out_ref[pl.ds(pl.multiple_of(me_ref[0] * part, part), part), :]
+            sent_ref[...] = out_ref[pl.ds(pl.multiple_of((1 - me_ref[0]) * part, part), part), :]
+
     rows = PACKED * length
-    shape = (ranks, features + columns)
+    shape = (part, features + columns)
     return pl.pallas_call(
         kernel,
         grid_spec=pltpu.PrefetchScalarGridSpec(
-            num_scalar_prefetch=1,
+            num_scalar_prefetch=2,
             grid=(blocks // PACKED,),
             in_specs=[
-                pl.BlockSpec((rows, features), lambda g, job_ref: (g, 0)),
-                pl.BlockSpec((rows, columns), lambda g, job_ref: (g, 0)),
-                pl.BlockSpec((2 * length, LANES), lambda g, job_ref: (g, 0)),
+                pl.BlockSpec((rows, features), lambda g, *_: (g, 0)),
+                pl.BlockSpec((rows, columns), lambda g, *_: (g, 0)),
+                pl.BlockSpec((2 * length, LANES), lambda g, *_: (g, 0)),
             ]
             + [ANY] * len(after),
-            out_specs=pl.BlockSpec(shape, lambda g, job_ref: (0, 0)),
+            out_specs=[pl.BlockSpec(shape, lambda g, *_: (0, 0))] * 2,
+            scratch_shapes=[pltpu.VMEM((ranks, features + columns), jnp.float32)],
         ),
-        out_shape=jax.ShapeDtypeStruct(shape, jnp.float32),
+        out_shape=[jax.ShapeDtypeStruct(shape, jnp.float32)] * 2,
         compiler_params=params(),
         cost_estimate=cost(),
         name="factor_gradients",
-    )(job, x, dy_home, low, *after)
+    )(job, me, x, dy_home, low, *after)
 
 
 def place_output(own, from_left, from_right, low, b, group, slot, job, me, length, cap, after):
@@ -371,8 +378,9 @@
     per_stream = blocks // count
 
     def kernel(group_ref, slot_ref, job_ref, me_ref, low_ref, b_ref, *refs):
-        out_ref = refs[-1]
-        out_ref[...] = jnp.zeros_like(out_ref)
+        kept_ref, sent_ref = refs[-2:]
+        mine = me_ref[0]
+        kept_ref[...] = jnp.zeros_like(kept_ref)
         factors = jnp.concatenate((b_ref[...], b_ref[...]), axis=0)
         for n in range(blocks):
             own_ref, left_ref, right_ref = refs[3 * (n // per_stream) :][:3]
@@ -388,30 +396,52 @@
                 halves(expand(SCALE * tile, n % PACKED, job_ref[n], ranks)), axis=1
             )
             total = total + dot32(wide, factors, ((1,), (0,)))
-            other = jnp.where(group_ref[n] == me_ref[0], 0, 1)
-            out_ref[other * cap + slot_ref[n]] = total.astype(jnp.bfloat16)
+            kept_ref[group_ref[n] * cap + slot_ref[n]] = total.astype(jnp.bfloat16)
+        sent_ref[...] = kept_ref[pl.ds((1 - mine) * cap, cap)]
 
     sums = [v for k in range(count) for v in (own[k], from_left[k], from_right[k])]
     return pl.pallas_call(
         kernel,
         in_specs=[SMEM] * 4 + [VMEM] * (2 + len(sums)) + [ANY] * len(after),
-        out_specs=VMEM,
-        out_shape=jax.ShapeDtypeStruct((2 * cap, length, columns), jnp.bfloat16),
+        out_specs=[VMEM, VMEM],
+        out_shape=[
+            jax.ShapeDtypeStruct((2 * cap, length, columns), jnp.bfloat16),
+            jax.ShapeDtypeStruct((cap, length, columns), jnp.bfloat16),
+        ],
         compiler_params=params(),
         cost_estimate=cost(),
         name="place_output",
     )(group, slot, job, me, low, b, *sums, *after)
 
 
-def input_gradient(pieces, w_t, place, low, a_t, job, length, step_blocks, stream, made, after):
-    blocks = job.shape[0]
-    count = len(pieces)
+def complete(kept, received, me):
+    def kernel(me_ref, received_ref, kept_ref, out_ref):
+        out_ref[...] = received_ref[...]
+
+    return pl.pallas_call(
+        kernel,
+        grid_spec=pltpu.PrefetchScalarGridSpec(
+            num_scalar_prefetch=1,
+            grid=(1,),
+            in_specs=[pl.BlockSpec(received.shape, lambda g, me_ref: (0, 0, 0)), ANY],
+            out_specs=pl.BlockSpec(received.shape, lambda g, me_ref: (1 - me_ref[0], 0, 0)),
+        ),
+        out_shape=jax.ShapeDtypeStruct(kept.shape, kept.dtype),
+        input_output_aliases={2: 0},
+        compiler_params=params(),
+        cost_estimate=cost(),
+        name="complete",
+    )(me, received, kept)
+
+
+def input_gradient(pieces, w_t, place, low, a_t, job, length, step_blocks, stream, after):
+    offsets = sorted(pieces)
+    count = len(offsets)
     stream_rows, columns = pieces[0].shape
     ranks, features = a_t.shape
     depth = count * columns + 2 * ranks
     steps = stream_rows // (step_blocks * length)
     start = stream * steps
-    held = () if made is None else (made,)
 
     def kernel(job_ref, place_ref, *refs):
         weights, parts = refs[:count], refs[count : 2 * count]
@@ -432,9 +462,7 @@
             tile = low_ref[pl.ds(first, length), :]
             wide.append(expand(tile, lax.rem(n, PACKED), job_ref[n], ranks))
         lhs = [r[...] for r in parts] + list(halves(jnp.concatenate(wide, axis=0)))
-        out_ref[...] = dot32(
-            jnp.concatenate(lhs, axis=1), factor_ref[...], ((1,), (0,))
-        ).astype(jnp.bfloat16)
+        out_ref[...] = dot32(jnp.concatenate(lhs, axis=1), factor_ref[...], ((1,), (0,)))
 
     step_rows = step_blocks * length
 
@@ -443,27 +471,81 @@
 
     def whole_spec(v):
         return pl.BlockSpec(v.shape, lambda g, job_ref, place_ref: (0, 0))
+
+    def row_spec(width):
+        return pl.BlockSpec((step_rows, width), lambda g, job_ref, place_ref: (g, 0))
 
     return pl.pallas_call(
         kernel,
         grid_spec=pltpu.PrefetchScalarGridSpec(
             num_scalar_prefetch=2,
             grid=(steps,),
-            in_specs=[weight_spec(d) for d in range(count)]
-            + [pl.BlockSpec((step_rows, columns), lambda g, job_ref, place_ref: (g, 0))] * count
+            in_specs=[weight_spec(d) for d in offsets]
+            + [row_spec(columns)] * count
             + [whole_spec(low), whole_spec(a_t)]
-            + [ANY] * (len(held) + len(after)),
-            out_specs=pl.BlockSpec(
-                (step_rows, features), lambda g, job_ref, place_ref: (g + start, 0)
-            ),
+            + [ANY] * len(after),
+            out_specs=row_spec(features),
             scratch_shapes=[pltpu.VMEM((depth, features), jnp.bfloat16)],
         ),
-        out_shape=jax.ShapeDtypeStruct((blocks * length, features), jnp.bfloat16),
-        input_output_aliases={2 + 2 * count + 2: 0} if held else {},
+        out_shape=jax.ShapeDtypeStruct((stream_rows, features), jnp.float32),
         compiler_params=params(),
         cost_estimate=cost(),
         name="input_gradient",
-    )(job, place, *([w_t] * count), *[pieces[d] for d in range(count)], low, a_t, *held, *after)
+    )(job, place, *([w_t] * count), *[pieces[d] for d in offsets], low, a_t, *after)
+
+
+def add_pieces(pieces, early, w_t, place, steps, after):
+    streams = len(pieces)
+    offsets = sorted(pieces[0])
+    count = len(offsets)
+    stream_rows, columns = early[0].shape[0], pieces[0][offsets[0]].shape[1]
+    features = w_t.shape[1]
+    step_rows = stream_rows // steps
+
+    def kernel(place_ref, *refs):
+        weights, parts = refs[:count], refs[count : count * (1 + streams)]
+        held = refs[count * (1 + streams) :][:streams]
+        out_ref, factor_ref = refs[-2:]
+
+        @pl.when(pl.program_id(0) == 0)
+        def _():
+            for i in range(count):
+                factor_ref[pl.ds(i * columns, columns), :] = weights[i][...]
+
+        for k in range(streams):
+
+            @pl.when(pl.program_id(0) // steps == k)
+            def _():
+                lhs = jnp.concatenate([r[...] for r in parts[k * count : (k + 1) * count]], axis=1)
+                out_ref[...] = (
+                    dot32(lhs, factor_ref[...], ((1,), (0,))) + held[k][...]
+                ).astype(jnp.bfloat16)
+
+    def weight_spec(d):
+        return pl.BlockSpec((columns, features), lambda g, place_ref: (place_ref[d], 0))
+
+    def row_spec(k, width):
+        return pl.BlockSpec(
+            (step_rows, width), lambda g, place_ref: (jnp.clip(g - k * steps, 0, steps - 1), 0)
+        )
+
+    return pl.pallas_call(
+        kernel,
+        grid_spec=pltpu.PrefetchScalarGridSpec(
+            num_scalar_prefetch=1,
+            grid=(streams * steps,),
+            in_specs=[weight_spec(d) for d in offsets]
+            + [row_spec(k, columns) for k in range(streams) for _ in offsets]
+            + [row_spec(k, features) for k in range(streams)]
+            + [ANY] * len(after),
+            out_specs=pl.BlockSpec((step_rows, features), lambda g, place_ref: (g, 0)),
+            scratch_shapes=[pltpu.VMEM((count * columns, features), jnp.bfloat16)],
+        ),
+        out_shape=jax.ShapeDtypeStruct((streams * stream_rows, features), jnp.bfloat16),
+        compiler_params=params(),
+        cost_estimate=cost(),
+        name="add_pieces",
+    )(place, *([w_t] * count), *[p[d] for p in pieces for d in offsets], *early, *after)
 
 
 def ring(x, group, slot, job, w, a, b, dy):
@@ -503,45 +585,36 @@
 
     far, near = size // 2, size // 2 - 1
     both = range(streams)
-    sums_r, sums_l, held_r, held_l, terms, pieces = [], [], [], [], [], []
-    last = ()
-
-    def first(k):
-        nonlocal last
-        r, l = project(
-            x, k * part_rows, part_rows, w, place, (far, size - near), group_rows, columns, True, last
+    ranks = a.shape[1]
+    sums_r, sums_l, held_r, held_l, own, pieces = [], [], [], [], [], []
+
+    def terms(k, offsets, received, plain, after):
+        return project(
+            x, k * part_rows, part_rows, w, place, offsets, received, plain, group_rows, columns, after
         )
-        last = (r,)
+
+    def first(k, after):
+        r, l = terms(k, (far, size - near), (), False, after)
         sums_r.append(right(r))
         sums_l.append(left(l))
-
-    first(0)
+        return (r,)
+
+    last = first(0, ())
     dy_home, *parts = home_gradient(dy, got, group, slot, mine, length, streams, last)
     for k in both:
         held_r.append(right(parts[k]))
         held_l.append(left(parts[k]))
         pieces.append({0: parts[k], size - 1: held_r[k], 1: held_l[k]})
-    last = (dy_home,)
-    for k in both[1:]:
-        first(k)
+    last = first(1, (dy_home,))
     low, coded = low_rank(x, a, dy_home, b.T, job, length, last)
     last = (coded,)
     bit = 1
     swapped = exchange(coded, bit)
 
-    offsets = []
-    for d in range(1, far):
-        offsets += [far - d] + ([size - (near - d)] if near > d else [])
-    offsets += [0]
-    for k in both:
-        made = project(
-            x, k * part_rows, part_rows, w, place, tuple(offsets), group_rows, columns, False, last
-        )
-        terms.append(dict(zip(offsets, made)))
-        last = (made[0],)
-
     def low_step():
         nonlocal low, swapped, bit, last
+        if bit >= size:
+            return
         more = 2 * bit < size
         got = add_coded([(low, swapped)], length, last, True, more, low.shape[0] // length)
         low = got[0]
@@ -550,49 +623,54 @@
         if more:
             swapped = exchange(got[1], bit)
 
-    low_step()
+    w_t, a_t = w.T, a.T
+    kept = sent = None
     for d in range(1, far):
+        if d == far - 1:
+            low_step()
+            kept, sent = factor_gradients(
+                x, dy_home, low, job, mine, ranks, length, last + (w_t, a_t)
+            )
+            last = (kept,)
         for k in both:
-            pairs = [(terms[k][far - d], sums_r[k])]
             if near > d:
-                pairs.append((terms[k][size - (near - d)], sums_l[k]))
-            turns = add_coded(pairs, group_rows, last)
-            sums_r[k] = right(turns[0])
-            if near > d:
-                sums_l[k] = left(turns[1])
-            last = (turns[0], held_l[k])
+                turn_r, turn_l = terms(
+                    k, (far - d, size - (near - d)), (sums_r[k], sums_l[k]), False, last
+                )
+                sums_l[k] = left(turn_l)
+            else:
+                turn_r, term = terms(k, (far - d, 0), (sums_r[k],), True, last)
+                own.append(term)
+            sums_r[k] = right(turn_r)
+            last = (turn_r, held_l[k])
             if d < near:
                 last += (held_r[k],)
                 held_r[k] = right(held_r[k])
                 pieces[k][size - 1 - d] = held_r[k]
             held_l[k] = left(held_l[k])
             pieces[k][1 + d] = held_l[k]
-        if bit < size:
-            low_step()
-
-    ranks = a.shape[1]
-    factors = factor_gradients(x, dy_home, low, job, ranks, length, last)
-    part = ranks // 2
-    theirs = lax.ppermute(lax.dynamic_slice_in_dim(factors, (1 - me) * part, part), "dp", swap)
-    w_t, a_t = w.T, a.T
-    placed = place_output(
-        [terms[k][0] for k in both], sums_r, sums_l, low, b, group, slot, job, mine, length, cap,
-        (factors, w_t),
-    )
-    last = (placed,)
-    placed = placed.reshape(2, half, columns)
-    other = lax.ppermute(placed[1], "dp", swap)
-    factors = lax.dynamic_slice_in_dim(factors, me * part, part) + theirs
-    output = jnp.where(
-        me == 0, jnp.concatenate((placed[0], other)), jnp.concatenate((other, placed[0]))
-    )
-    grad_home = None
+            if d == 1:
+                low_step()
+
+    factors = kept + lax.ppermute(sent, "dp", swap)
+    grad_a, grad_b = factors[:, :features].T, factors[:, features:]
+
+    late = (far - 1, far)
+    last = last[:1] + tuple(pieces[k][far - 1] for k in both)
+    early = []
     for k in both:
-        grad_home = input_gradient(
-            pieces[k], w_t, place, low, a_t, job, length, step_blocks // 2, k, grad_home, last
+        ready = {d: v for d, v in pieces[k].items() if d not in late}
+        early.append(
+            input_gradient(ready, w_t, place, low, a_t, job, length, step_blocks // 2, k, last)
         )
-        last = (output,)
-    return output, grad_home, factors[:, :features].T, factors[:, features:]
+        last = (early[k], grad_a, grad_b)
+    final = [{d: pieces[k][d] for d in late} for k in both]
+    placed, sent = place_output(
+        own, sums_r, sums_l, low, b, group, slot, job, mine, length, cap, last + tuple(pieces[k][far] for k in both)
+    )
+    grad_home = add_pieces(final, early, w_t, place, 2, (placed,))
+    output = complete(placed, lax.ppermute(sent, "dp", swap), mine)
+    return output.reshape(dy.shape), grad_home, grad_a, grad_b
 
 
 def local(*args):

time: 187 us -> 178 us (0.952)
  Pallas kernels: 86.2 us -> 97.6 us
  starting transfers between devices: 43.9 us -> 33.5 us
  local copies, waits for them, and re-layouts: 14.9 us -> 9.99 us
  other arithmetic: 4.34 us -> 1.67 us
  waiting for transfers between devices: 35.7 us -> 33.6 us
    ppermute x14, waiting for transfers between devices: 6.54 us -> 22.3 us  [left(): return lax.ppermute(v, 'tensor', back)]
    pallas_call x9 -> x3, Pallas kernels: 20.3 us -> 5.97 us  [add_coded(): pl.pallas_call(kernel, grid=(rows // group_rows // groups,), in_specs=[bl...]
    pallas_call x4 -> x8, Pallas kernels: 22.5 us -> 36.5 us  [project(): pl.pallas_call(kernel, grid_spec=pltpu.PrefetchScalarGridSpec(num_scalar_...]
    pallas_call x0 -> x2, Pallas kernels: none -> 12.5 us  [the longest x1 10.6 us: add_pieces(): pl.pallas_call(kernel, grid_spec=pltpu.PrefetchScalarGridSpec(num_scalar_...]
    ppermute x3, waiting for transfers between devices: 16 us -> 4.62 us  [exchange(): return lax.ppermute(v, 'tensor', [(t, t ^ bit) for t in range(size)])]
    ppermute x14, starting transfers between devices: 23.6 us -> 16.4 us  [left(): return lax.ppermute(v, 'tensor', back)]
    ppermute x14, waiting for transfers between devices: 13.1 us -> 6.66 us  [right(): return lax.ppermute(v, 'tensor', ahead)]
    select_n x1 -> x0, other arithmetic: 2.45 us -> none  [ring(): jnp.where(me == 0, jnp.concatenate((placed[0], other)), jnp.concatenate((...]
  transfers between devices with their start and end apart: 34 -> 34, of which waited for: 7 -> 10; matrix products, arithmetic and copies ran while one was open for 9% -> 5% of each run, Pallas kernels for 41% -> 51%
where the time goes in v4:
time: 178 us; the launch traced here: 177 us
  Pallas kernels  97.6 us (55%)
  waiting for transfers between devices  33.6 us (19%)
  starting transfers between devices  33.5 us (19%)
  local copies, waits for them, and re-layouts  9.99 us (6%)
    pallas_call x8, Pallas kernels, project(): pl.pallas_call(kernel, grid_spec=pltpu.PrefetchScalarGridSpec(num_scalar_...  36.5 us
    ppermute x14, waiting for transfers between devices, left(): return lax.ppermute(v, 'tensor', back)  22.3 us
    pallas_call x2, Pallas kernels, input_gradient(): pl.pallas_call(kernel, grid_spec=pltpu.PrefetchScalarGridSpec(num_scalar_...  18.8 us
    ppermute x14, starting transfers between devices, left(): return lax.ppermute(v, 'tensor', back)  16.4 us
    pallas_call x1, Pallas kernels, add_pieces(): pl.pallas_call(kernel, grid_spec=pltpu.PrefetchScalarGridSpec(num_scalar_...  10.6 us
    ppermute x14, starting transfers between devices, right(): return lax.ppermute(v, 'tensor', ahead)  10.2 us
    pallas_call x1, Pallas kernels, factor_gradients(): pl.pallas_call(kernel, grid_spec=pltpu.PrefetchScalarGridSpec(num_scalar_...  9.39 us
    unnamed x25, local copies, waits for them, and re-layouts  7.2 us
  transfers between devices with their start and end apart: 34, of which 10 were waited for; matrix products, arithmetic and copies ran while one was open for 5% of the time, Pallas kernels for 51%

profile of v4, /device:TPU:1, one launch (start us, length us, event | category | flops | bytes accessed | tf_op | source)
XLA Modules:
  0.0 177.1 jit_solution(10450163168936315510)
XLA Ops:
  2.4 4.4 %project.8 = (s16[2,784,128]{2,1,0:T(8,128)(2,1)}, s16[2,784,128]{2,1,0:T(8,128)(2,1)}) custom-call(s32[8]{0:T(128)} %compare_select_fusion.2.place_ref, bf16[3072,1024]{1,0:T(8,128)(2,1)} %x_ref.19, bf16[1024,1024]{1,0:T(8,128)(2,1)} %refs_1_.15, bf16[1024,1024]{1,0:T(8,128)(2,1)} %refs_1_.15), custom_call_target="tpu_custom_call" | custom-call | flops 1 | bytes 1 | tf_op jit(solution)/shard_map/project/pallas_call | solution.py:183
  6.8 2.7 %collective-permute-start.3 = (s16[2,784,128]{2,1,0:T(8,128)(2,1)}, s16[2,784,128]{2,1,0:T(8,128)(2,1)}, u32[]{:S(2)}, u32[]{:S(2)}) collective-permute-start(s16[2,784,128]{2,1,0:T(8,128)(2,1)} %get-tuple-element.38), channel_id=1, source_target_pairs={{0,1},{2,0},{4,2},{6,4},{7,6},{5,7},{3,5},{1,3},{8,9},{10,8},{12,1... | collective-permute-start | bytes 1204232 | tf_op jit(solution)/shard_map/ppermute | solution.py:578
  10.3 3.1 %home_gradient.1 = (bf16[3072,128]{1,0:T(8,128)(2,1)}, bf16[1536,128]{1,0:T(8,128)(2,1)}, bf16[1536,128]{1,0:T(8,128)(2,1)}) custom-call(s32[24]{0:T(128)} %group_ref.3, s32[24]{0:T(128)} %slot_ref.3, s32[1]{0:T(128)} %bitcast.me_ref, bf16[4096,128]{1,0:T(8,128)(2,1)} %dy_ref.1, bf16[2048,128]{1,0:T(8,128)(2,1)} %collective-permute-done.received_ref, ...), custom_call_target="tpu_custom_call" | custom-call | flops 1 | bytes 1 | tf_op jit(solution)/shard_map/home_gradient/pallas_call | solution.py:259
  13.4 1.4 collective-permute-start.5
  14.9 4.4 %project.9 = (s16[2,784,128]{2,1,0:T(8,128)(2,1)}, s16[2,784,128]{2,1,0:T(8,128)(2,1)}) custom-call(s32[8]{0:T(128)} %compare_select_fusion.2.place_ref, bf16[3072,1024]{1,0:T(8,128)(2,1)} %x_ref.19, bf16[1024,1024]{1,0:T(8,128)(2,1)} %refs_1_.15, bf16[1024,1024]{1,0:T(8,128)(2,1)} %refs_1_.15, bf16[3072,128]{1,0:T(8,128)(2,1)} %get-tuple-element.34.refs_2_.dy_ref), custom_call_target="tpu_custom_call" | custom-call | flops 1 | bytes 1 | tf_op jit(solution)/shard_map/project/pallas_call | solution.py:183
  19.3 6.7 %low_rank.1 = (f32[768,128]{1,0:T(8,128)}, s16[6,144,128]{2,1,0:T(8,128)(2,1)}) custom-call(s32[24]{0:T(128)} %job_ref.9, bf16[3072,1024]{1,0:T(8,128)(2,1)} %x_ref.19, bf16[1024,256]{1,0:T(8,128)(2,1)} %a_ref.1, bf16[3072,128]{1,0:T(8,128)(2,1)} %get-tuple-element.34.refs_2_.dy_ref, bf16[128,256]{1,0:T(8,128)(2,1)} %bitcast.26, ...), custom_call_target="tpu_custom_call" | custom-call | flops 1 | bytes 1 | tf_op jit(solution)/shard_map/low_rank/pallas_call | solution.py:291
  26.0 1.4 collective-permute-start.4
  27.5 1.4 collective-permute-start.9
  28.9 4.6 %collective-permute-done.1.refs_1_ = s16[6,144,128]{2,1,0:T(8,128)(2,1)S(1)} collective-permute-done((s16[6,144,128]{2,1,0:T(8,128)(2,1)}, s16[6,144,128]{2,1,0:T(8,128)(2,1)S(1)}, u32[]{:S(2)}, u32[]{:S(2)}) %collective-permute-start.1) | collective-permute-done | bytes 221216 | tf_op jit(solution)/shard_map/ppermute | solution.py:581
  35.0 4.7 %project.10 = (s16[2,784,128]{2,1,0:T(8,128)(2,1)}, s16[2,784,128]{2,1,0:T(8,128)(2,1)}) custom-call(s32[8]{0:T(128)} %compare_select_fusion.2.place_ref, bf16[3072,1024]{1,0:T(8,128)(2,1)} %x_ref.19, bf16[1024,1024]{1,0:T(8,128)(2,1)} %refs_1_.15, bf16[1024,1024]{1,0:T(8,128)(2,1)} %refs_1_.15, s16[2,784,128]{2,1,0:T(8,128)(2,1)} %collective-permute-done.2.refs_2_, ...), custom_call_target="tpu_custom_call" | custom-call | flops 1 | bytes 1 | tf_op jit(solution)/shard_map/project/pallas_call | solution.py:183
  39.7 1.4 collective-permute-start.15
  42.0 2.1 %add_coded.3 = (f32[768,128]{1,0:T(8,128)}, s16[6,144,128]{2,1,0:T(8,128)(2,1)}) custom-call(f32[768,128]{1,0:T(8,128)} %get-tuple-element.36.refs_0_, s16[6,144,128]{2,1,0:T(8,128)(2,1)} %copy-done.10, s16[2,784,128]{2,1,0:T(8,128)(2,1)} %get-tuple-element.39.refs_2_, bf16[1536,128]{1,0:T(8,128)(2,1)} %collective-permute-done.4.refs_3_.refs_7_, ...), custom_call_target="tpu_custom_call" | custom-call | flops 1 | bytes 1 | tf_op jit(solution)/shard_map/add_coded/pallas_call | solution.py:221
  44.1 3.3 %collective-permute-done.9.refs_3_.refs_7_ = bf16[1536,128]{1,0:T(8,128)(2,1)} collective-permute-done((bf16[1536,128]{1,0:T(8,128)(2,1)}, bf16[1536,128]{1,0:T(8,128)(2,1)}, u32[]{:S(2)}, u32[]{:S(2)}) %collective-permute-start.9) | collective-permute-done | bytes 393248 | tf_op jit(solution)/shard_map/ppermute | solution.py:578
  47.3 8.6 %collective-permute-done.8.refs_3_ = s16[2,784,128]{2,1,0:T(8,128)(2,1)} collective-permute-done((s16[2,784,128]{2,1,0:T(8,128)(2,1)}, s16[2,784,128]{2,1,0:T(8,128)(2,1)}, u32[]{:S(2)}, u32[]{:S(2)}) %collective-permute-start.8) | collective-permute-done | bytes 401440 | tf_op jit(solution)/shard_map/ppermute | solution.py:578
  55.9 2.2 %collective-permute-start.16 = (bf16[1536,128]{1,0:T(8,128)(2,1)}, bf16[1536,128]{1,0:T(8,128)(2,1)}, u32[]{:S(2)}, u32[]{:S(2)}) collective-permute-start(bf16[1536,128]{1,0:T(8,128)(2,1)} %collective-permute-done.4.refs_3_.refs_7_), channel_id=1, source_target_pairs={{0,1},{2,0},{4,2},{6,4},{7,6},{5,7},{3,5},{1,3},{8,9},{10,8},{12,1... | collective-permute-start | bytes 1179656 | tf_op jit(solution)/shard_map/ppermute | solution.py:578
  58.1 4.7 %project.11 = (s16[2,784,128]{2,1,0:T(8,128)(2,1)}, s16[2,784,128]{2,1,0:T(8,128)(2,1)}) custom-call(s32[8]{0:T(128)} %compare_select_fusion.2.place_ref, bf16[3072,1024]{1,0:T(8,128)(2,1)} %x_ref.19, bf16[1024,1024]{1,0:T(8,128)(2,1)} %refs_1_.15, bf16[1024,1024]{1,0:T(8,128)(2,1)} %refs_1_.15, s16[2,784,128]{2,1,0:T(8,128)(2,1)} %collective-permute-done.7.refs_2_, ...), custom_call_target="tpu_custom_call" | custom-call | flops 1 | bytes 1 | tf_op jit(solution)/shard_map/project/pallas_call | solution.py:183
  62.9 1.7 collective-permute-done.15.refs_3_
  64.5 2.2 %collective-permute-start.13 = (s16[2,784,128]{2,1,0:T(8,128)(2,1)}, s16[2,784,128]{2,1,0:T(8,128)(2,1)}, u32[]{:S(2)}, u32[]{:S(2)}) collective-permute-start(s16[2,784,128]{2,1,0:T(8,128)(2,1)} %get-tuple-element.48), channel_id=1, source_target_pairs={{0,1},{2,0},{4,2},{6,4},{7,6},{5,7},{3,5},{1,3},{8,9},{10,8},{12,1... | collective-permute-start | bytes 1204232 | tf_op jit(solution)/shard_map/ppermute | solution.py:578
  66.9 1.6 collective-permute-start.18
  68.5 2.0 %add_coded.4 = (f32[768,128]{1,0:T(8,128)}, s16[6,144,128]{2,1,0:T(8,128)(2,1)}) custom-call(f32[768,128]{1,0:T(8,128)} %get-tuple-element.41.refs_4_.refs_0_, s16[6,144,128]{2,1,0:T(8,128)(2,1)} %collective-permute-done.6.refs_1_, s16[2,784,128]{2,1,0:T(8,128)(2,1)} %get-tuple-element.44.refs_2_, bf16[1536,128]{1,0:T(8,128)(2,1)} %collective-permute-done.9.refs_3_.refs_7_, ...), custom_call_target="tpu_custom_call" | custom-call | flops 1 | bytes 1 | tf_op jit(solution)/shard_map/add_coded/pallas_call | solution.py:221
  70.5 4.4 %collective-permute-done.16.refs_5_.refs_8_ = bf16[1536,128]{1,0:T(8,128)(2,1)} collective-permute-done((bf16[1536,128]{1,0:T(8,128)(2,1)}, bf16[1536,128]{1,0:T(8,128)(2,1)}, u32[]{:S(2)}, u32[]{:S(2)}) %collective-permute-start.16) | collective-permute-done | bytes 393248 | tf_op jit(solution)/shard_map/ppermute | solution.py:578
  74.9 2.1 %collective-permute-start.11 = (s16[6,144,128]{2,1,0:T(8,128)(2,1)}, s16[6,144,128]{2,1,0:T(8,128)(2,1)}, u32[]{:S(2)}, u32[]{:S(2)}) collective-permute-start(s16[6,144,128]{2,1,0:T(8,128)(2,1)} %get-tuple-element.47), channel_id=1, source_target_pairs={{0,4},{1,5},{2,6},{3,7},{4,0},{5,1},{6,2},{7,3},{8,12},{9,13},{10,... | collective-permute-start | bytes 663560 | tf_op jit(solution)/shard_map/ppermute | solution.py:581
  77.0 4.7 %project.12 = (s16[2,784,128]{2,1,0:T(8,128)(2,1)}, s16[2,784,128]{2,1,0:T(8,128)(2,1)}) custom-call(s32[8]{0:T(128)} %compare_select_fusion.2.place_ref, bf16[3072,1024]{1,0:T(8,128)(2,1)} %x_ref.19, bf16[1024,1024]{1,0:T(8,128)(2,1)} %refs_1_.15, bf16[1024,1024]{1,0:T(8,128)(2,1)} %refs_1_.15, s16[2,784,128]{2,1,0:T(8,128)(2,1)} %collective-permute-done.14.refs_2_, ...), custom_call_target="tpu_custom_call" | custom-call | flops 1 | bytes 1 | tf_op jit(solution)/shard_map/project/pallas_call | solution.py:183
  81.7 1.8 %collective-permute-done.13.refs_3_ = s16[2,784,128]{2,1,0:T(8,128)(2,1)} collective-permute-done((s16[2,784,128]{2,1,0:T(8,128)(2,1)}, s16[2,784,128]{2,1,0:T(8,128)(2,1)}, u32[]{:S(2)}, u32[]{:S(2)}) %collective-permute-start.13) | collective-permute-done | bytes 401440 | tf_op jit(solution)/shard_map/ppermute | solution.py:578
  83.5 4.7 %project.13 = (s16[2,784,128]{2,1,0:T(8,128)(2,1)}, s16[2,784,128]{2,1,0:T(8,128)(2,1)}) custom-call(s32[8]{0:T(128)} %compare_select_fusion.2.place_ref, bf16[3072,1024]{1,0:T(8,128)(2,1)} %x_ref.19, bf16[1024,1024]{1,0:T(8,128)(2,1)} %refs_1_.15, bf16[1024,1024]{1,0:T(8,128)(2,1)} %refs_1_.15, s16[2,784,128]{2,1,0:T(8,128)(2,1)} %collective-permute-done.12.refs_2_, ...), custom_call_target="tpu_custom_call" | custom-call | flops 1 | bytes 1 | tf_op jit(solution)/shard_map/project/pallas_call | solution.py:183
  88.2 2.4 %collective-permute-start.23 = (s16[2,784,128]{2,1,0:T(8,128)(2,1)}, s16[2,784,128]{2,1,0:T(8,128)(2,1)}, u32[]{:S(2)}, u32[]{:S(2)}) collective-permute-start(s16[2,784,128]{2,1,0:T(8,128)(2,1)} %get-tuple-element.51.refs_2_), channel_id=1, source_target_pairs={{0,2},{2,4},{4,6},{6,7},{7,5},{5,3},{3,1},{1,0},{8,10},{10,12},{12... | collective-permute-start | bytes 1204232 | tf_op jit(solution)/shard_map/ppermute | solution.py:575
  91.6 3.9 %copy.14 = bf16[1024,1024]{0,1:T(8,128)(2,1)} copy(bf16[1024,1024]{1,0:T(8,128)(2,1)} %refs_1_.15) | data formatting | bytes 4194304 | tf_op args[4]
  95.5 1.2 collective-permute-done.18.refs_3_.refs_8_
  96.7 1.9 %add_coded.5.low_ref.refs_0_.refs_12_ = f32[768,128]{1,0:T(8,128)} custom-call(f32[768,128]{1,0:T(8,128)} %get-tuple-element.46.refs_4_.refs_0_, s16[6,144,128]{2,1,0:T(8,128)(2,1)} %collective-permute-done.11.refs_1_, s16[2,784,128]{2,1,0:T(8,128)(2,1)} %get-tuple-element.51.refs_2_, bf16[1536,128]{1,0:T(8,128)(2,1)} %collective-permute-done.18.refs_3_.refs_8_, ...), custom_call_target="tpu_custom_call" | custom-call | flops 1 | bytes 1 | tf_op jit(solution)/shard_map/add_coded/pallas_call | solution.py:221
  98.5 9.4 %factor_gradients.1 = (f32[128,1152]{1,0:T(8,128)}, f32[128,1152]{1,0:T(8,128)}) custom-call(s32[24]{0:T(128)} %job_ref.9, s32[1]{0:T(128)} %bitcast.me_ref, bf16[3072,1024]{1,0:T(8,128)(2,1)} %x_ref.19, bf16[3072,128]{1,0:T(8,128)(2,1)} %get-tuple-element.34.refs_2_.dy_ref, f32[768,128]{1,0:T(8,128)} %add_coded.5.low_ref.refs_0_.refs_12_, ...), custom_call_target="tpu_custom_call" | custom-call | flops 1 | bytes 1 | tf_op jit(solution)/shard_map/factor_gradients/pallas_call | solution.py:352
  107.9 3.2 %collective-permute-start.30 = (f32[128,1152]{1,0:T(8,128)}, f32[128,1152]{1,0:T(8,128)}, u32[]{:S(2)}, u32[]{:S(2)}) collective-permute-start(f32[128,1152]{1,0:T(8,128)} %get-tuple-element.59), channel_id=1, source_target_pairs={{0,8},{8,0},{1,9},{9,1},{2,10},{10,2},{3,11},{11,3},{4,12},{12,4},... | collective-permute-start | bytes 1769480 | tf_op jit(solution)/shard_map/ppermute | solution.py:655
  111.1 1.5 collective-permute-start.22
  112.6 1.2 collective-permute-start.28
  113.9 1.4 collective-permute-start.27
  115.3 4.4 %project.14 = (s16[2,784,128]{2,1,0:T(8,128)(2,1)}, f32[1536,128]{1,0:T(8,128)}) custom-call(s32[8]{0:T(128)} %compare_select_fusion.2.place_ref, bf16[3072,1024]{1,0:T(8,128)(2,1)} %x_ref.19, bf16[1024,1024]{1,0:T(8,128)(2,1)} %refs_1_.15, bf16[1024,1024]{1,0:T(8,128)(2,1)} %refs_1_.15, s16[2,784,128]{2,1,0:T(8,128)(2,1)} %collective-permute-done.20.refs_2_, ...), custom_call_target="tpu_custom_call" | custom-call | flops 1 | bytes 1 | tf_op jit(solution)/shard_map/project/pallas_call | solution.py:183
  119.8 4.5 %project.15 = (s16[2,784,128]{2,1,0:T(8,128)(2,1)}, f32[1536,128]{1,0:T(8,128)}) custom-call(s32[8]{0:T(128)} %compare_select_fusion.2.place_ref, bf16[3072,1024]{1,0:T(8,128)(2,1)} %x_ref.19, bf16[1024,1024]{1,0:T(8,128)(2,1)} %refs_1_.15, bf16[1024,1024]{1,0:T(8,128)(2,1)} %refs_1_.15, s16[2,784,128]{2,1,0:T(8,128)(2,1)} %collective-permute-done.23.refs_2_, ...), custom_call_target="tpu_custom_call" | custom-call | flops 1 | bytes 1 | tf_op jit(solution)/shard_map/project/pallas_call | solution.py:183
  124.6 1.2 collective-permute-start.21
  125.8 5.8 %collective-permute-done.27.refs_9_ = bf16[1536,128]{1,0:T(8,128)(2,1)} collective-permute-done((bf16[1536,128]{1,0:T(8,128)(2,1)}, bf16[1536,128]{1,0:T(8,128)(2,1)}, u32[]{:S(2)}, u32[]{:S(2)}) %collective-permute-start.27) | collective-permute-done | bytes 393248 | tf_op jit(solution)/shard_map/ppermute | solution.py:575
  131.6 1.5 collective-permute-start.25
  133.2 1.4 collective-permute-start.32
  134.6 9.4 %input_gradient.2.refs_14_.refs_6_ = f32[1536,1024]{1,0:T(8,128)} custom-call(s32[24]{0:T(128)} %job_ref.9, s32[8]{0:T(128)} %compare_select_fusion.2.place_ref, bf16[1024,1024]{1,0:T(8,128)(2,1)} %bitcast.8, bf16[1024,1024]{1,0:T(8,128)(2,1)} %bitcast.9, bf16[1024,1024]{1,0:T(8,128)(2,1)} %bitcast.10, bf16[1024,1024]{1,0:T(8,128)(2,1)} %bitcast.11, ...), custom_call_target="tpu_custom_call" | custom-call | flops 1 | bytes 1 | tf_op jit(solution)/shard_map/input_gradient/pallas_call | solution.py:478
  144.0 1.1 add.32
  146.8 9.4 %input_gradient.3.refs_6_.refs_7_ = f32[1536,1024]{1,0:T(8,128)} custom-call(s32[24]{0:T(128)} %job_ref.9, s32[8]{0:T(128)} %compare_select_fusion.2.place_ref, bf16[1024,1024]{1,0:T(8,128)(2,1)} %bitcast.14, bf16[1024,1024]{1,0:T(8,128)(2,1)} %bitcast.15, bf16[1024,1024]{1,0:T(8,128)(2,1)} %bitcast.16, bf16[1024,1024]{1,0:T(8,128)(2,1)} %bitcast.17, ...), custom_call_target="tpu_custom_call" | custom-call | flops 1 | bytes 1 | tf_op jit(solution)/shard_map/input_gradient/pallas_call | solution.py:478
  156.3 1.3 collective-permute-done.32.refs_10_.refs_5_
  157.7 4.7 %place_output.1 = (bf16[32,128,128]{2,1,0:T(8,128)(2,1)}, bf16[16,128,128]{2,1,0:T(8,128)(2,1)}) custom-call(s32[24]{0:T(128)} %group_ref.3, s32[24]{0:T(128)} %slot_ref.3, s32[24]{0:T(128)} %job_ref.9, s32[1]{0:T(128)} %bitcast.me_ref, f32[768,128]{1,0:T(8,128)} %add_coded.5.low_ref.refs_0_.refs_12_, bf16[256,128]{1,0:T(8,128)(2,1)} %b_ref.1, ...), custom_call_target="tpu_custom_call" | custom-call | flops 1 | bytes 1 | tf_op jit(solution)/shard_map/place_output/pallas_call | solution.py:403
  162.4 1.5 collective-permute-start.33
  163.8 10.6 %add_pieces.1 = bf16[3072,1024]{1,0:T(8,128)(2,1)} custom-call(s32[8]{0:T(128)} %compare_select_fusion.2.place_ref, bf16[1024,1024]{1,0:T(8,128)(2,1)} %bitcast.20, bf16[1024,1024]{1,0:T(8,128)(2,1)} %bitcast.21, bf16[1536,128]{1,0:T(8,128)(2,1)} %copy-done, bf16[1536,128]{1,0:T(8,128)(2,1)} %copy-done.6, ...), custom_call_target="tpu_custom_call" | custom-call | flops 1 | bytes 1 | tf_op jit(solution)/shard_map/add_pieces/pallas_call | solution.py:532
  175.3 1.9 %complete.1 = bf16[32,128,128]{2,1,0:T(8,128)(2,1)} custom-call(s32[1]{0:T(128)} %bitcast.me_ref, bf16[16,128,128]{2,1,0:T(8,128)(2,1)} %copy-done.8, bf16[32,128,128]{2,1,0:T(8,128)(2,1)} %get-tuple-element.61.kept_ref.refs_8_), custom_call_target="tpu_custom_call", output_to_operand_aliasing={{}: (2, {})} | custom-call | flops 1 | bytes 1 | tf_op jit(solution)/shard_map/complete/pallas_call | solution.py:421
  (70 shorter events, 9.2 us)
Async XLA Ops:
  0.6 9.0 %copy-start.9 = (bf16[256,128]{1,0:T(8,128)(2,1)S(1)}, bf16[256,128]{1,0:T(8,128)(2,1)}, u32[]{:S(2)}) copy-start(bf16[256,128]{1,0:T(8,128)(2,1)} %b_ref.1) | copy-start | bytes 196612
  1.8 8.6 %collective-permute-start = (bf16[2048,128]{1,0:T(8,128)(2,1)S(1)}, bf16[2048,128]{1,0:T(8,128)(2,1)}, u32[]{:S(2)}, u32[]{:S(2)}) collective-permute-start(bf16[2048,128]{1,0:T(8,128)(2,1)S(1)} %constant_dynamic-slice_fusion), channel_id=1, source_target_pairs={{0,8},{8,0},{1,9},{9,1},{2,10},{10,2},{3,11},{11,3},{4,12},{12,4},... | collective-permute-start | bytes 1572872 | tf_op jit(solution)/shard_map/ppermute | solution.py:584
  6.8 20.6 %collective-permute-start.3 = (s16[2,784,128]{2,1,0:T(8,128)(2,1)}, s16[2,784,128]{2,1,0:T(8,128)(2,1)}, u32[]{:S(2)}, u32[]{:S(2)}) collective-permute-start(s16[2,784,128]{2,1,0:T(8,128)(2,1)} %get-tuple-element.38), channel_id=1, source_target_pairs={{0,1},{2,0},{4,2},{6,4},{7,6},{5,7},{3,5},{1,3},{8,9},{10,8},{12,1... | collective-permute-start | bytes 1204232 | tf_op jit(solution)/shard_map/ppermute | solution.py:578
  9.5 18.0 %collective-permute-start.2 = (s16[2,784,128]{2,1,0:T(8,128)(2,1)}, s16[2,784,128]{2,1,0:T(8,128)(2,1)}, u32[]{:S(2)}, u32[]{:S(2)}) collective-permute-start(s16[2,784,128]{2,1,0:T(8,128)(2,1)} %get-tuple-element.33.refs_0_), channel_id=1, source_target_pairs={{0,2},{2,4},{4,6},{6,7},{7,5},{5,3},{3,1},{1,0},{8,10},{10,12},{12... | collective-permute-start | bytes 1204232 | tf_op jit(solution)/shard_map/ppermute | solution.py:575
  13.4 20.1 %collective-permute-start.5 = (bf16[1536,128]{1,0:T(8,128)(2,1)}, bf16[1536,128]{1,0:T(8,128)(2,1)S(1)}, u32[]{:S(2)}, u32[]{:S(2)}) collective-permute-start(bf16[1536,128]{1,0:T(8,128)(2,1)} %get-tuple-element.40.refs_6_), channel_id=1, source_target_pairs={{0,2},{2,4},{4,6},{6,7},{7,5},{5,3},{3,1},{1,0},{8,10},{10,12},{12... | collective-permute-start | bytes 1179656 | tf_op jit(solution)/shard_map/ppermute | solution.py:575
  26.0 7.6 %collective-permute-start.1 = (s16[6,144,128]{2,1,0:T(8,128)(2,1)}, s16[6,144,128]{2,1,0:T(8,128)(2,1)S(1)}, u32[]{:S(2)}, u32[]{:S(2)}) collective-permute-start(s16[6,144,128]{2,1,0:T(8,128)(2,1)} %get-tuple-element.37.refs_4_), channel_id=1, source_target_pairs={{0,1},{1,0},{2,3},{3,2},{4,5},{5,4},{6,7},{7,6},{8,9},{9,8},{10,11... | collective-permute-start | bytes 663560 | tf_op jit(solution)/shard_map/ppermute | solution.py:581
  26.0 13.7 %collective-permute-start.4 = (bf16[1536,128]{1,0:T(8,128)(2,1)}, bf16[1536,128]{1,0:T(8,128)(2,1)}, u32[]{:S(2)}, u32[]{:S(2)}) collective-permute-start(bf16[1536,128]{1,0:T(8,128)(2,1)} %get-tuple-element.40.refs_6_), channel_id=1, source_target_pairs={{0,1},{2,0},{4,2},{6,4},{7,6},{5,7},{3,5},{1,3},{8,9},{10,8},{12,1... | collective-permute-start | bytes 1179656 | tf_op jit(solution)/shard_map/ppermute | solution.py:578
  27.4 14.5 %collective-permute-start.10 = (bf16[1536,128]{1,0:T(8,128)(2,1)}, bf16[1536,128]{1,0:T(8,128)(2,1)S(1)}, u32[]{:S(2)}, u32[]{:S(2)}) collective-permute-start(bf16[1536,128]{1,0:T(8,128)(2,1)} %get-tuple-element.45.refs_6_), channel_id=1, source_target_pairs={{0,2},{2,4},{4,6},{6,7},{7,5},{5,3},{3,1},{1,0},{8,10},{10,12},{12... | collective-permute-start | bytes 1179656 | tf_op jit(solution)/shard_map/ppermute | solution.py:575
  27.5 19.8 %collective-permute-start.9 = (bf16[1536,128]{1,0:T(8,128)(2,1)}, bf16[1536,128]{1,0:T(8,128)(2,1)}, u32[]{:S(2)}, u32[]{:S(2)}) collective-permute-start(bf16[1536,128]{1,0:T(8,128)(2,1)} %get-tuple-element.45.refs_6_), channel_id=1, source_target_pairs={{0,1},{2,0},{4,2},{6,4},{7,6},{5,7},{3,5},{1,3},{8,9},{10,8},{12,1... | collective-permute-start | bytes 1179656 | tf_op jit(solution)/shard_map/ppermute | solution.py:578
  33.5 0.7 copy-start.10
  33.5 22.4 %collective-permute-start.8 = (s16[2,784,128]{2,1,0:T(8,128)(2,1)}, s16[2,784,128]{2,1,0:T(8,128)(2,1)}, u32[]{:S(2)}, u32[]{:S(2)}) collective-permute-start(s16[2,784,128]{2,1,0:T(8,128)(2,1)} %get-tuple-element.43), channel_id=1, source_target_pairs={{0,1},{2,0},{4,2},{6,4},{7,6},{5,7},{3,5},{1,3},{8,9},{10,8},{12,1... | collective-permute-start | bytes 1204232 | tf_op jit(solution)/shard_map/ppermute | solution.py:578
  34.2 7.8 %copy-start.7 = (bf16[1536,128]{1,0:T(8,128)(2,1)}, bf16[1536,128]{1,0:T(8,128)(2,1)S(1)}, u32[]{:S(2)}) copy-start(bf16[1536,128]{1,0:T(8,128)(2,1)S(1)} %collective-permute-done.5.refs_4_.refs_11_) | copy-start | bytes 1179652
  34.2 21.7 %collective-permute-start.7 = (s16[2,784,128]{2,1,0:T(8,128)(2,1)}, s16[2,784,128]{2,1,0:T(8,128)(2,1)}, u32[]{:S(2)}, u32[]{:S(2)}) collective-permute-start(s16[2,784,128]{2,1,0:T(8,128)(2,1)} %get-tuple-element.35.refs_0_), channel_id=1, source_target_pairs={{0,2},{2,4},{4,6},{6,7},{7,5},{5,3},{3,1},{1,0},{8,10},{10,12},{12... | collective-permute-start | bytes 1204232 | tf_op jit(solution)/shard_map/ppermute | solution.py:575
  39.7 24.8 %collective-permute-start.15 = (s16[2,784,128]{2,1,0:T(8,128)(2,1)}, s16[2,784,128]{2,1,0:T(8,128)(2,1)}, u32[]{:S(2)}, u32[]{:S(2)}) collective-permute-start(s16[2,784,128]{2,1,0:T(8,128)(2,1)} %get-tuple-element.49), channel_id=1, source_target_pairs={{0,1},{2,0},{4,2},{6,4},{7,6},{5,7},{3,5},{1,3},{8,9},{10,8},{12,1... | collective-permute-start | bytes 1204232 | tf_op jit(solution)/shard_map/ppermute | solution.py:578
  42.0 24.8 %copy-start.3 = (bf16[1536,128]{1,0:T(8,128)(2,1)}, bf16[1536,128]{1,0:T(8,128)(2,1)S(1)}, u32[]{:S(2)}) copy-start(bf16[1536,128]{1,0:T(8,128)(2,1)S(1)} %collective-permute-done.10.refs_4_.refs_11_) | copy-start | bytes 1179652
  42.0 24.8 %collective-permute-start.14 = (s16[2,784,128]{2,1,0:T(8,128)(2,1)}, s16[2,784,128]{2,1,0:T(8,128)(2,1)}, u32[]{:S(2)}, u32[]{:S(2)}) collective-permute-start(s16[2,784,128]{2,1,0:T(8,128)(2,1)} %get-tuple-element.39.refs_2_), channel_id=1, source_target_pairs={{0,2},{2,4},{4,6},{6,7},{7,5},{5,3},{3,1},{1,0},{8,10},{10,12},{12... | collective-permute-start | bytes 1204232 | tf_op jit(solution)/shard_map/ppermute | solution.py:575
  47.3 19.4 %collective-permute-start.6 = (s16[6,144,128]{2,1,0:T(8,128)(2,1)}, s16[6,144,128]{2,1,0:T(8,128)(2,1)}, u32[]{:S(2)}, u32[]{:S(2)}) collective-permute-start(s16[6,144,128]{2,1,0:T(8,128)(2,1)} %get-tuple-element.42), channel_id=1, source_target_pairs={{0,2},{1,3},{2,0},{3,1},{4,6},{5,7},{6,4},{7,5},{8,10},{9,11},{10,... | collective-permute-start | bytes 663560 | tf_op jit(solution)/shard_map/ppermute | solution.py:581
  55.9 10.9 %collective-permute-start.17 = (bf16[1536,128]{1,0:T(8,128)(2,1)}, bf16[1536,128]{1,0:T(8,128)(2,1)S(1)}, u32[]{:S(2)}, u32[]{:S(2)}) collective-permute-start(bf16[1536,128]{1,0:T(8,128)(2,1)} %copy-done.7), channel_id=1, source_target_pairs={{0,2},{2,4},{4,6},{6,7},{7,5},{5,3},{3,1},{1,0},{8,10},{10,12},{12... | collective-permute-start | bytes 1179656 | tf_op jit(solution)/shard_map/ppermute | solution.py:575
  55.9 18.9 %collective-permute-start.16 = (bf16[1536,128]{1,0:T(8,128)(2,1)}, bf16[1536,128]{1,0:T(8,128)(2,1)}, u32[]{:S(2)}, u32[]{:S(2)}) collective-permute-start(bf16[1536,128]{1,0:T(8,128)(2,1)} %collective-permute-done.4.refs_3_.refs_7_), channel_id=1, source_target_pairs={{0,1},{2,0},{4,2},{6,4},{7,6},{5,7},{3,5},{1,3},{8,9},{10,8},{12,1... | collective-permute-start | bytes 1179656 | tf_op jit(solution)/shard_map/ppermute | solution.py:578
  64.5 18.9 %collective-permute-start.13 = (s16[2,784,128]{2,1,0:T(8,128)(2,1)}, s16[2,784,128]{2,1,0:T(8,128)(2,1)}, u32[]{:S(2)}, u32[]{:S(2)}) collective-permute-start(s16[2,784,128]{2,1,0:T(8,128)(2,1)} %get-tuple-element.48), channel_id=1, source_target_pairs={{0,1},{2,0},{4,2},{6,4},{7,6},{5,7},{3,5},{1,3},{8,9},{10,8},{12,1... | collective-permute-start | bytes 1204232 | tf_op jit(solution)/shard_map/ppermute | solution.py:578
  66.7 16.7 %collective-permute-start.12 = (s16[2,784,128]{2,1,0:T(8,128)(2,1)}, s16[2,784,128]{2,1,0:T(8,128)(2,1)}, u32[]{:S(2)}, u32[]{:S(2)}) collective-permute-start(s16[2,784,128]{2,1,0:T(8,128)(2,1)} %get-tuple-element.44.refs_2_), channel_id=1, source_target_pairs={{0,2},{2,4},{4,6},{6,7},{7,5},{5,3},{3,1},{1,0},{8,10},{10,12},{12... | collective-permute-start | bytes 1204232 | tf_op jit(solution)/shard_map/ppermute | solution.py:575
  66.8 23.8 %collective-permute-start.19 = (bf16[1536,128]{1,0:T(8,128)(2,1)S(1)}, bf16[1536,128]{1,0:T(8,128)(2,1)}, u32[]{:S(2)}, u32[]{:S(2)}) collective-permute-start(bf16[1536,128]{1,0:T(8,128)(2,1)S(1)} %collective-permute-done.10.refs_4_.refs_11_), channel_id=1, source_target_pairs={{0,2},{2,4},{4,6},{6,7},{7,5},{5,3},{3,1},{1,0},{8,10},{10,12},{12... | collective-permute-start | bytes 1179656 | tf_op jit(solution)/shard_map/ppermute | solution.py:575
  66.8 10.1 %copy-start.4 = (bf16[1536,128]{1,0:T(8,128)(2,1)}, bf16[1536,128]{1,0:T(8,128)(2,1)S(1)}, u32[]{:S(2)}) copy-start(bf16[1536,128]{1,0:T(8,128)(2,1)S(1)} %collective-permute-done.17.refs_6_.refs_10_) | copy-start | bytes 1179652
  66.9 29.8 %collective-permute-start.18 = (bf16[1536,128]{1,0:T(8,128)(2,1)}, bf16[1536,128]{1,0:T(8,128)(2,1)}, u32[]{:S(2)}, u32[]{:S(2)}) collective-permute-start(bf16[1536,128]{1,0:T(8,128)(2,1)} %collective-permute-done.9.refs_3_.refs_7_), channel_id=1, source_target_pairs={{0,1},{2,0},{4,2},{6,4},{7,6},{5,7},{3,5},{1,3},{8,9},{10,8},{12,1... | collective-permute-start | bytes 1179656 | tf_op jit(solution)/shard_map/ppermute | solution.py:578
  74.9 21.8 %collective-permute-start.11 = (s16[6,144,128]{2,1,0:T(8,128)(2,1)}, s16[6,144,128]{2,1,0:T(8,128)(2,1)}, u32[]{:S(2)}, u32[]{:S(2)}) collective-permute-start(s16[6,144,128]{2,1,0:T(8,128)(2,1)} %get-tuple-element.47), channel_id=1, source_target_pairs={{0,4},{1,5},{2,6},{3,7},{4,0},{5,1},{6,2},{7,3},{8,12},{9,13},{10,... | collective-permute-start | bytes 663560 | tf_op jit(solution)/shard_map/ppermute | solution.py:581
  81.7 8.9 %copy-start.2 = (bf16[1024,256]{1,0:T(8,128)(2,1)S(1)}, bf16[1024,256]{1,0:T(8,128)(2,1)}, u32[]{:S(2)}) copy-start(bf16[1024,256]{1,0:T(8,128)(2,1)} %a_ref.1) | copy-start | bytes 1572868
  83.5 29.2 %collective-permute-start.20 = (s16[2,784,128]{2,1,0:T(8,128)(2,1)}, s16[2,784,128]{2,1,0:T(8,128)(2,1)}, u32[]{:S(2)}, u32[]{:S(2)}) collective-permute-start(s16[2,784,128]{2,1,0:T(8,128)(2,1)} %get-tuple-element.50.refs_4_), channel_id=1, source_target_pairs={{0,2},{2,4},{4,6},{6,7},{7,5},{5,3},{3,1},{1,0},{8,10},{10,12},{12... | collective-permute-start | bytes 1204232 | tf_op jit(solution)/shard_map/ppermute | solution.py:575
  88.2 27.1 %collective-permute-start.23 = (s16[2,784,128]{2,1,0:T(8,128)(2,1)}, s16[2,784,128]{2,1,0:T(8,128)(2,1)}, u32[]{:S(2)}, u32[]{:S(2)}) collective-permute-start(s16[2,784,128]{2,1,0:T(8,128)(2,1)} %get-tuple-element.51.refs_2_), channel_id=1, source_target_pairs={{0,2},{2,4},{4,6},{6,7},{7,5},{5,3},{3,1},{1,0},{8,10},{10,12},{12... | collective-permute-start | bytes 1204232 | tf_op jit(solution)/shard_map/ppermute | solution.py:575
  90.5 23.3 %collective-permute-start.24 = (bf16[1536,128]{1,0:T(8,128)(2,1)}, bf16[1536,128]{1,0:T(8,128)(2,1)S(1)}, u32[]{:S(2)}, u32[]{:S(2)}) collective-permute-start(bf16[1536,128]{1,0:T(8,128)(2,1)} %collective-permute-done.16.refs_5_.refs_8_), channel_id=1, source_target_pairs={{0,1},{2,0},{4,2},{6,4},{7,6},{5,7},{3,5},{1,3},{8,9},{10,8},{12,1... | collective-permute-start | bytes 1179656 | tf_op jit(solution)/shard_map/ppermute | solution.py:578
  95.5 17.1 %copy-start.5 = (bf16[1536,128]{1,0:T(8,128)(2,1)S(1)}, bf16[1536,128]{1,0:T(8,128)(2,1)}, u32[]{:S(2)}) copy-start(bf16[1536,128]{1,0:T(8,128)(2,1)} %copy-done.4) | copy-start | bytes 1179652
  107.9 25.3 %collective-permute-start.30 = (f32[128,1152]{1,0:T(8,128)}, f32[128,1152]{1,0:T(8,128)}, u32[]{:S(2)}, u32[]{:S(2)}) collective-permute-start(f32[128,1152]{1,0:T(8,128)} %get-tuple-element.59), channel_id=1, source_target_pairs={{0,8},{8,0},{1,9},{9,1},{2,10},{10,2},{3,11},{11,3},{4,12},{12,4},... | collective-permute-start | bytes 1769480 | tf_op jit(solution)/shard_map/ppermute | solution.py:655
  111.1 13.1 %collective-permute-start.22 = (s16[2,784,128]{2,1,0:T(8,128)(2,1)}, s16[2,784,128]{2,1,0:T(8,128)(2,1)}, u32[]{:S(2)}, u32[]{:S(2)}) collective-permute-start(s16[2,784,128]{2,1,0:T(8,128)(2,1)} %get-tuple-element.55), channel_id=1, source_target_pairs={{0,1},{2,0},{4,2},{6,4},{7,6},{5,7},{3,5},{1,3},{8,9},{10,8},{12,1... | collective-permute-start | bytes 1204232 | tf_op jit(solution)/shard_map/ppermute | solution.py:578
  112.6 12.0 %collective-permute-start.28 = (bf16[1536,128]{1,0:T(8,128)(2,1)S(1)}, bf16[1536,128]{1,0:T(8,128)(2,1)}, u32[]{:S(2)}, u32[]{:S(2)}) collective-permute-start(bf16[1536,128]{1,0:T(8,128)(2,1)S(1)} %copy-done.5), channel_id=1, source_target_pairs={{0,2},{2,4},{4,6},{6,7},{7,5},{5,3},{3,1},{1,0},{8,10},{10,12},{12... | collective-permute-start | bytes 1179656 | tf_op jit(solution)/shard_map/ppermute | solution.py:575
  113.9 5.9 %copy-start = (bf16[1536,128]{1,0:T(8,128)(2,1)}, bf16[1536,128]{1,0:T(8,128)(2,1)S(1)}, u32[]{:S(2)}) copy-start(bf16[1536,128]{1,0:T(8,128)(2,1)S(1)} %collective-permute-done.24.refs_4_.refs_15_.refs_2_) | copy-start | bytes 1179652
  113.9 17.7 %collective-permute-start.27 = (bf16[1536,128]{1,0:T(8,128)(2,1)}, bf16[1536,128]{1,0:T(8,128)(2,1)}, u32[]{:S(2)}, u32[]{:S(2)}) collective-permute-start(bf16[1536,128]{1,0:T(8,128)(2,1)} %collective-permute-done.19.refs_4_.refs_10_), channel_id=1, source_target_pairs={{0,2},{2,4},{4,6},{6,7},{7,5},{5,3},{3,1},{1,0},{8,10},{10,12},{12... | collective-permute-start | bytes 1179656 | tf_op jit(solution)/shard_map/ppermute | solution.py:575
  115.3 17.8 %collective-permute-start.29 = (bf16[1536,128]{1,0:T(8,128)(2,1)}, bf16[1536,128]{1,0:T(8,128)(2,1)}, u32[]{:S(2)}, u32[]{:S(2)}) collective-permute-start(bf16[1536,128]{1,0:T(8,128)(2,1)} %collective-permute-done.18.refs_3_.refs_8_), channel_id=1, source_target_pairs={{0,1},{2,0},{4,2},{6,4},{7,6},{5,7},{3,5},{1,3},{8,9},{10,8},{12,1... | collective-permute-start | bytes 1179656 | tf_op jit(solution)/shard_map/ppermute | solution.py:578
  124.3 32.0 %collective-permute-start.26 = (s16[2,784,128]{2,1,0:T(8,128)(2,1)}, s16[2,784,128]{2,1,0:T(8,128)(2,1)}, u32[]{:S(2)}, u32[]{:S(2)}) collective-permute-start(s16[2,784,128]{2,1,0:T(8,128)(2,1)} %get-tuple-element.58), channel_id=1, source_target_pairs={{0,1},{2,0},{4,2},{6,4},{7,6},{5,7},{3,5},{1,3},{8,9},{10,8},{12,1... | collective-permute-start | bytes 1204232 | tf_op jit(solution)/shard_map/ppermute | solution.py:578
  124.6 31.6 %collective-permute-start.21 = (s16[2,784,128]{2,1,0:T(8,128)(2,1)}, s16[2,784,128]{2,1,0:T(8,128)(2,1)}, u32[]{:S(2)}, u32[]{:S(2)}) collective-permute-start(s16[2,784,128]{2,1,0:T(8,128)(2,1)} %get-tuple-element.54.refs_3_), channel_id=1, source_target_pairs={{0,2},{2,4},{4,6},{6,7},{7,5},{5,3},{3,1},{1,0},{8,10},{10,12},{12... | collective-permute-start | bytes 1204232 | tf_op jit(solution)/shard_map/ppermute | solution.py:575
  131.6 12.4 %copy-start.1 = (f32[128,1152]{1,0:T(8,128)S(1)}, f32[128,1152]{1,0:T(8,128)}, u32[]{:S(2)}) copy-start(f32[128,1152]{1,0:T(8,128)} %get-tuple-element.52.refs_3_) | copy-start | bytes 1769476
  131.6 26.1 %collective-permute-start.25 = (s16[2,784,128]{2,1,0:T(8,128)(2,1)}, s16[2,784,128]{2,1,0:T(8,128)(2,1)}, u32[]{:S(2)}, u32[]{:S(2)}) collective-permute-start(s16[2,784,128]{2,1,0:T(8,128)(2,1)} %get-tuple-element.57.refs_14_), channel_id=1, source_target_pairs={{0,2},{2,4},{4,6},{6,7},{7,5},{5,3},{3,1},{1,0},{8,10},{10,12},{12... | collective-permute-start | bytes 1204232 | tf_op jit(solution)/shard_map/ppermute | solution.py:575
  133.1 23.2 %collective-permute-start.31 = (bf16[1536,128]{1,0:T(8,128)(2,1)}, bf16[1536,128]{1,0:T(8,128)(2,1)S(1)}, u32[]{:S(2)}, u32[]{:S(2)}) collective-permute-start(bf16[1536,128]{1,0:T(8,128)(2,1)} %copy-done), channel_id=1, source_target_pairs={{0,1},{2,0},{4,2},{6,4},{7,6},{5,7},{3,5},{1,3},{8,9},{10,8},{12,1... | collective-permute-start | bytes 1179656 | tf_op jit(solution)/shard_map/ppermute | solution.py:578
  133.2 24.4 %collective-permute-start.32 = (bf16[1536,128]{1,0:T(8,128)(2,1)}, bf16[1536,128]{1,0:T(8,128)(2,1)}, u32[]{:S(2)}, u32[]{:S(2)}) collective-permute-start(bf16[1536,128]{1,0:T(8,128)(2,1)} %collective-permute-done.29.refs_16_.refs_4_), channel_id=1, source_target_pairs={{0,1},{2,0},{4,2},{6,4},{7,6},{5,7},{3,5},{1,3},{8,9},{10,8},{12,1... | collective-permute-start | bytes 1179656 | tf_op jit(solution)/shard_map/ppermute | solution.py:578
  156.3 1.4 copy-start.6
  162.4 12.1 %collective-permute-start.33 = (bf16[16,128,128]{2,1,0:T(8,128)(2,1)}, bf16[16,128,128]{2,1,0:T(8,128)(2,1)S(1)}, u32[]{:S(2)}, u32[]{:S(2)}) collective-permute-start(bf16[16,128,128]{2,1,0:T(8,128)(2,1)} %get-tuple-element.60), channel_id=1, source_target_pairs={{0,8},{8,0},{1,9},{9,1},{2,10},{10,2},{3,11},{11,3},{4,12},{12,4},... | collective-permute-start | bytes 1572872 | tf_op jit(solution)/shard_map/ppermute | solution.py:672
  174.5 0.8 copy-start.8

commit v5 on v4

--- a/solution.py
+++ b/solution.py
@@ -368,6 +368,29 @@
         cost_estimate=cost(),
         name="factor_gradients",
     )(job, me, x, dy_home, low, *after)
+
+
+def add_factors(kept, received, features, after):
+    rows, width = kept.shape
+
+    def kernel(kept_ref, received_ref, *refs):
+        down_ref, up_ref = refs[len(after) :]
+        total = kept_ref[...] + received_ref[...]
+        down_ref[...] = total[:, :features].T
+        up_ref[...] = total[:, features:]
+
+    return pl.pallas_call(
+        kernel,
+        in_specs=[VMEM, VMEM] + [ANY] * len(after),
+        out_specs=[VMEM, VMEM],
+        out_shape=[
+            jax.ShapeDtypeStruct((features, rows), jnp.float32),
+            jax.ShapeDtypeStruct((rows, width - features), jnp.float32),
+        ],
+        compiler_params=params(),
+        cost_estimate=cost(),
+        name="add_factors",
+    )(kept, received, *after)
 
 
 def place_output(own, from_left, from_right, low, b, group, slot, job, me, length, cap, after):
@@ -434,7 +457,7 @@
     )(me, received, kept)
 
 
-def input_gradient(pieces, w_t, place, low, a_t, job, length, step_blocks, stream, after):
+def input_gradient(pieces, w_t, place, low, a_t, job, length, step_blocks, stream, made, after):
     offsets = sorted(pieces)
     count = len(offsets)
     stream_rows, columns = pieces[0].shape
@@ -442,6 +465,7 @@
     depth = count * columns + 2 * ranks
     steps = stream_rows // (step_blocks * length)
     start = stream * steps
+    held = () if made is None else (made,)
 
     def kernel(job_ref, place_ref, *refs):
         weights, parts = refs[:count], refs[count : 2 * count]
@@ -483,28 +507,31 @@
             in_specs=[weight_spec(d) for d in offsets]
             + [row_spec(columns)] * count
             + [whole_spec(low), whole_spec(a_t)]
-            + [ANY] * len(after),
-            out_specs=row_spec(features),
+            + [ANY] * (len(held) + len(after)),
+            out_specs=pl.BlockSpec(
+                (step_rows, features), lambda g, job_ref, place_ref: (g + start, 0)
+            ),
             scratch_shapes=[pltpu.VMEM((depth, features), jnp.bfloat16)],
         ),
-        out_shape=jax.ShapeDtypeStruct((stream_rows, features), jnp.float32),
+        out_shape=jax.ShapeDtypeStruct((job.shape[0] * length, features), jnp.float32),
+        input_output_aliases={2 * count + 4: 0} if held else {},
         compiler_params=params(),
         cost_estimate=cost(),
         name="input_gradient",
-    )(job, place, *([w_t] * count), *[pieces[d] for d in offsets], low, a_t, *after)
+    )(job, place, *([w_t] * count), *[pieces[d] for d in offsets], low, a_t, *held, *after)
 
 
 def add_pieces(pieces, early, w_t, place, steps, after):
     streams = len(pieces)
     offsets = sorted(pieces[0])
     count = len(offsets)
-    stream_rows, columns = early[0].shape[0], pieces[0][offsets[0]].shape[1]
+    stream_rows, columns = pieces[0][offsets[0]].shape
     features = w_t.shape[1]
     step_rows = stream_rows // steps
 
     def kernel(place_ref, *refs):
         weights, parts = refs[:count], refs[count : count * (1 + streams)]
-        held = refs[count * (1 + streams) :][:streams]
+        early_ref = refs[count * (1 + streams)]
         out_ref, factor_ref = refs[-2:]
 
         @pl.when(pl.program_id(0) == 0)
@@ -518,7 +545,7 @@
             def _():
                 lhs = jnp.concatenate([r[...] for r in parts[k * count : (k + 1) * count]], axis=1)
                 out_ref[...] = (
-                    dot32(lhs, factor_ref[...], ((1,), (0,))) + held[k][...]
+                    dot32(lhs, factor_ref[...], ((1,), (0,))) + early_ref[...]
                 ).astype(jnp.bfloat16)
 
     def weight_spec(d):
@@ -536,7 +563,7 @@
             grid=(streams * steps,),
             in_specs=[weight_spec(d) for d in offsets]
             + [row_spec(k, columns) for k in range(streams) for _ in offsets]
-            + [row_spec(k, features) for k in range(streams)]
+            + [pl.BlockSpec((step_rows, features), lambda g, place_ref: (g, 0))]
             + [ANY] * len(after),
             out_specs=pl.BlockSpec((step_rows, features), lambda g, place_ref: (g, 0)),
             scratch_shapes=[pltpu.VMEM((count * columns, features), jnp.bfloat16)],
@@ -545,7 +572,7 @@
         compiler_params=params(),
         cost_estimate=cost(),
         name="add_pieces",
-    )(place, *([w_t] * count), *[p[d] for p in pieces for d in offsets], *early, *after)
+    )(place, *([w_t] * count), *[p[d] for p in pieces for d in offsets], early, *after)
 
 
 def ring(x, group, slot, job, w, a, b, dy):
@@ -600,12 +627,13 @@
         return (r,)
 
     last = first(0, ())
+    last = first(1, last)
     dy_home, *parts = home_gradient(dy, got, group, slot, mine, length, streams, last)
     for k in both:
         held_r.append(right(parts[k]))
         held_l.append(left(parts[k]))
         pieces.append({0: parts[k], size - 1: held_r[k], 1: held_l[k]})
-    last = first(1, (dy_home,))
+    last = (dy_home,)
     low, coded = low_rank(x, a, dy_home, b.T, job, length, last)
     last = (coded,)
     bit = 1
@@ -627,7 +655,8 @@
     kept = sent = None
     for d in range(1, far):
         if d == far - 1:
-            low_step()
+            while bit < size:
+                low_step()
             kept, sent = factor_gradients(
                 x, dy_home, low, job, mine, ranks, length, last + (w_t, a_t)
             )
@@ -649,24 +678,23 @@
                 pieces[k][size - 1 - d] = held_r[k]
             held_l[k] = left(held_l[k])
             pieces[k][1 + d] = held_l[k]
-            if d == 1:
+            if d + k == 2:
                 low_step()
 
-    factors = kept + lax.ppermute(sent, "dp", swap)
-    grad_a, grad_b = factors[:, :features].T, factors[:, features:]
+    grad_a, grad_b = add_factors(kept, lax.ppermute(sent, "dp", swap), features, last[:1])
 
     late = (far - 1, far)
     last = last[:1] + tuple(pieces[k][far - 1] for k in both)
-    early = []
+    early = None
     for k in both:
         ready = {d: v for d, v in pieces[k].items() if d not in late}
-        early.append(
-            input_gradient(ready, w_t, place, low, a_t, job, length, step_blocks // 2, k, last)
+        early = input_gradient(
+            ready, w_t, place, low, a_t, job, length, step_blocks // 2, k, early, last
         )
-        last = (early[k], grad_a, grad_b)
+        last = (grad_b,)
     final = [{d: pieces[k][d] for d in late} for k in both]
     placed, sent = place_output(
-        own, sums_r, sums_l, low, b, group, slot, job, mine, length, cap, last + tuple(pieces[k][far] for k in both)
+        own, sums_r, sums_l, low, b, group, slot, job, mine, length, cap, (early,) + tuple(pieces[k][far] for k in both)
     )
     grad_home = add_pieces(final, early, w_t, place, 2, (placed,))
     output = complete(placed, lax.ppermute(sent, "dp", swap), mine)

time: 178 us -> 171 us (0.961)
  starting transfers between devices: 33.5 us -> 27.3 us
    ppermute x14, starting transfers between devices: 16.4 us -> 11 us  [left(): return lax.ppermute(v, 'tensor', back)]
    ppermute x14, waiting for transfers between devices: 6.66 us -> 11.7 us  [right(): return lax.ppermute(v, 'tensor', ahead)]
    ppermute x3, waiting for transfers between devices: 4.62 us -> 1.24 us  [exchange(): return lax.ppermute(v, 'tensor', [(t, t ^ bit) for t in range(size)])]
    pallas_call x0 -> x1, Pallas kernels: none -> 2.24 us  [add_factors(): pl.pallas_call(kernel, in_specs=[VMEM, VMEM] + [ANY] * len(after), out_sp...]
    ppermute x14, waiting for transfers between devices: 22.3 us -> 20.3 us  [left(): return lax.ppermute(v, 'tensor', back)]
    unnamed x25 -> x27, local copies, waits for them, and re-layouts: 7.2 us -> 8.57 us
  transfers between devices with their start and end apart: 34 -> 34, of which waited for: 10 -> 7; matrix products, arithmetic and copies ran while one was open for 5% -> 4% of each run, Pallas kernels for 51% -> 54%
where the time goes in v5:
time: 171 us; the launch traced here: 170 us
  Pallas kernels  98.9 us (58%)
  waiting for transfers between devices  33.3 us (19%)
  starting transfers between devices  27.3 us (16%)
  local copies, waits for them, and re-layouts  9.65 us (6%)
    pallas_call x8, Pallas kernels, project(): pl.pallas_call(kernel, grid_spec=pltpu.PrefetchScalarGridSpec(num_scalar_...  36.8 us
    ppermute x14, waiting for transfers between devices, left(): return lax.ppermute(v, 'tensor', back)  20.3 us
    pallas_call x2, Pallas kernels, input_gradient(): pl.pallas_call(kernel, grid_spec=pltpu.PrefetchScalarGridSpec(num_scalar_...  18.9 us
    ppermute x14, waiting for transfers between devices, right(): return lax.ppermute(v, 'tensor', ahead)  11.7 us
    ppermute x14, starting transfers between devices, left(): return lax.ppermute(v, 'tensor', back)  11 us
    ppermute x14, starting transfers between devices, right(): return lax.ppermute(v, 'tensor', ahead)  9.81 us
    pallas_call x1, Pallas kernels, add_pieces(): pl.pallas_call(kernel, grid_spec=pltpu.PrefetchScalarGridSpec(num_scalar_...  9.5 us
    pallas_call x1, Pallas kernels, factor_gradients(): pl.pallas_call(kernel, grid_spec=pltpu.PrefetchScalarGridSpec(num_scalar_...  9.37 us
  transfers between devices with their start and end apart: 34, of which 7 were waited for; matrix products, arithmetic and copies ran while one was open for 4% of the time, Pallas kernels for 54%

profile of v5, /device:TPU:1, one launch (start us, length us, event | category | flops | bytes accessed | tf_op | source)
XLA Modules:
  0.0 170.5 jit_solution(181377639688077899)
XLA Ops:
  0.6 1.1 constant_dynamic-slice_fusion
  2.4 4.4 %project.8 = (s16[2,784,128]{2,1,0:T(8,128)(2,1)}, s16[2,784,128]{2,1,0:T(8,128)(2,1)}) custom-call(s32[8]{0:T(128)} %compare_select_fusion.2.place_ref, bf16[3072,1024]{1,0:T(8,128)(2,1)} %x_ref.19, bf16[1024,1024]{1,0:T(8,128)(2,1)} %refs_1_.15, bf16[1024,1024]{1,0:T(8,128)(2,1)} %refs_1_.15), custom_call_target="tpu_custom_call" | custom-call | flops 1 | bytes 1 | tf_op jit(solution)/shard_map/project/pallas_call | solution.py:183
  6.8 2.7 %collective-permute-start.4 = (s16[2,784,128]{2,1,0:T(8,128)(2,1)}, s16[2,784,128]{2,1,0:T(8,128)(2,1)}, u32[]{:S(2)}, u32[]{:S(2)}) collective-permute-start(s16[2,784,128]{2,1,0:T(8,128)(2,1)} %get-tuple-element.35.refs_2_), channel_id=1, source_target_pairs={{0,2},{2,4},{4,6},{6,7},{7,5},{5,3},{3,1},{1,0},{8,10},{10,12},{12... | collective-permute-start | bytes 1204232 | tf_op jit(solution)/shard_map/ppermute | solution.py:602
  9.5 4.6 %project.9 = (s16[2,784,128]{2,1,0:T(8,128)(2,1)}, s16[2,784,128]{2,1,0:T(8,128)(2,1)}) custom-call(s32[8]{0:T(128)} %compare_select_fusion.2.place_ref, bf16[3072,1024]{1,0:T(8,128)(2,1)} %x_ref.19, bf16[1024,1024]{1,0:T(8,128)(2,1)} %refs_1_.15, bf16[1024,1024]{1,0:T(8,128)(2,1)} %refs_1_.15, s16[2,784,128]{2,1,0:T(8,128)(2,1)} %get-tuple-element.35.refs_2_), custom_call_target="tpu_custom_call" | custom-call | flops 1 | bytes 1 | tf_op jit(solution)/shard_map/project/pallas_call | solution.py:183
  14.1 1.3 collective-permute-start.2
  15.6 3.1 %home_gradient.1 = (bf16[3072,128]{1,0:T(8,128)(2,1)}, bf16[1536,128]{1,0:T(8,128)(2,1)}, bf16[1536,128]{1,0:T(8,128)(2,1)}) custom-call(s32[24]{0:T(128)} %group_ref.3, s32[24]{0:T(128)} %slot_ref.3, s32[1]{0:T(128)} %bitcast.me_ref, bf16[4096,128]{1,0:T(8,128)(2,1)} %dy_ref.1, bf16[2048,128]{1,0:T(8,128)(2,1)} %collective-permute-done.received_ref, ...), custom_call_target="tpu_custom_call" | custom-call | flops 1 | bytes 1 | tf_op jit(solution)/shard_map/home_gradient/pallas_call | solution.py:259
  18.7 1.3 collective-permute-start.6
  19.9 0.8 collective-permute-start.7
  21.4 6.6 %collective-permute-done.2.refs_2_ = s16[2,784,128]{2,1,0:T(8,128)(2,1)} collective-permute-done((s16[2,784,128]{2,1,0:T(8,128)(2,1)}, s16[2,784,128]{2,1,0:T(8,128)(2,1)}, u32[]{:S(2)}, u32[]{:S(2)}) %collective-permute-start.2) | collective-permute-done | bytes 401440 | tf_op jit(solution)/shard_map/ppermute | solution.py:602
  28.0 1.3 collective-permute-start.9
  29.3 0.7 copy.14
  30.1 6.6 %low_rank.1 = (f32[768,128]{1,0:T(8,128)}, s16[6,144,128]{2,1,0:T(8,128)(2,1)}) custom-call(s32[24]{0:T(128)} %job_ref.9, bf16[3072,1024]{1,0:T(8,128)(2,1)} %x_ref.19, bf16[1024,256]{1,0:T(8,128)(2,1)} %a_ref.1, bf16[3072,128]{1,0:T(8,128)(2,1)} %get-tuple-element.37.dy_ref.refs_0_, bf16[128,256]{1,0:T(8,128)(2,1)} %bitcast.24, ...), custom_call_target="tpu_custom_call" | custom-call | flops 1 | bytes 1 | tf_op jit(solution)/shard_map/low_rank/pallas_call | solution.py:291
  36.9 4.7 %project.10 = (s16[2,784,128]{2,1,0:T(8,128)(2,1)}, s16[2,784,128]{2,1,0:T(8,128)(2,1)}) custom-call(s32[8]{0:T(128)} %compare_select_fusion.2.place_ref, bf16[3072,1024]{1,0:T(8,128)(2,1)} %x_ref.19, bf16[1024,1024]{1,0:T(8,128)(2,1)} %refs_1_.15, bf16[1024,1024]{1,0:T(8,128)(2,1)} %refs_1_.15, s16[2,784,128]{2,1,0:T(8,128)(2,1)} %collective-permute-done.4.refs_2_, ...), custom_call_target="tpu_custom_call" | custom-call | flops 1 | bytes 1 | tf_op jit(solution)/shard_map/project/pallas_call | solution.py:183
  41.6 1.3 collective-permute-start.11
  43.7 4.7 %project.11 = (s16[2,784,128]{2,1,0:T(8,128)(2,1)}, s16[2,784,128]{2,1,0:T(8,128)(2,1)}) custom-call(s32[8]{0:T(128)} %compare_select_fusion.2.place_ref, bf16[3072,1024]{1,0:T(8,128)(2,1)} %x_ref.19, bf16[1024,1024]{1,0:T(8,128)(2,1)} %refs_1_.15, bf16[1024,1024]{1,0:T(8,128)(2,1)} %refs_1_.15, s16[2,784,128]{2,1,0:T(8,128)(2,1)} %collective-permute-done.2.refs_2_, ...), custom_call_target="tpu_custom_call" | custom-call | flops 1 | bytes 1 | tf_op jit(solution)/shard_map/project/pallas_call | solution.py:183
  48.4 1.2 collective-permute-done.1.refs_1_
  49.6 2.0 %add_coded.3 = (f32[768,128]{1,0:T(8,128)}, s16[6,144,128]{2,1,0:T(8,128)(2,1)}) custom-call(f32[768,128]{1,0:T(8,128)} %get-tuple-element.38.refs_0_, s16[6,144,128]{2,1,0:T(8,128)(2,1)} %collective-permute-done.1.refs_1_, s16[2,784,128]{2,1,0:T(8,128)(2,1)} %get-tuple-element.44.refs_2_, bf16[1536,128]{1,0:T(8,128)(2,1)} %collective-permute-done.8.refs_3_.refs_7_, ...), custom_call_target="tpu_custom_call" | custom-call | flops 1 | bytes 1 | tf_op jit(solution)/shard_map/add_coded/pallas_call | solution.py:221
  51.7 1.3 collective-permute-start.13
  53.1 5.1 %collective-permute-done.11.refs_2_ = s16[2,784,128]{2,1,0:T(8,128)(2,1)} collective-permute-done((s16[2,784,128]{2,1,0:T(8,128)(2,1)}, s16[2,784,128]{2,1,0:T(8,128)(2,1)}, u32[]{:S(2)}, u32[]{:S(2)}) %collective-permute-start.11) | collective-permute-done | bytes 401440 | tf_op jit(solution)/shard_map/ppermute | solution.py:602
  58.2 1.5 collective-permute-start.17
  59.8 7.9 %collective-permute-done.13.refs_3_.refs_8_ = bf16[1536,128]{1,0:T(8,128)(2,1)S(1)} collective-permute-done((bf16[1536,128]{1,0:T(8,128)(2,1)}, bf16[1536,128]{1,0:T(8,128)(2,1)S(1)}, u32[]{:S(2)}, u32[]{:S(2)}) %collective-permute-start.13) | collective-permute-done | bytes 393248 | tf_op jit(solution)/shard_map/ppermute | solution.py:605
  67.6 4.7 %project.12 = (s16[2,784,128]{2,1,0:T(8,128)(2,1)}, s16[2,784,128]{2,1,0:T(8,128)(2,1)}) custom-call(s32[8]{0:T(128)} %compare_select_fusion.2.place_ref, bf16[3072,1024]{1,0:T(8,128)(2,1)} %x_ref.19, bf16[1024,1024]{1,0:T(8,128)(2,1)} %refs_1_.15, bf16[1024,1024]{1,0:T(8,128)(2,1)} %refs_1_.15, s16[2,784,128]{2,1,0:T(8,128)(2,1)} %collective-permute-done.11.refs_2_, ...), custom_call_target="tpu_custom_call" | custom-call | flops 1 | bytes 1 | tf_op jit(solution)/shard_map/project/pallas_call | solution.py:183
  72.3 0.8 copy-done.5
  73.1 2.0 %add_coded.4 = (f32[768,128]{1,0:T(8,128)}, s16[6,144,128]{2,1,0:T(8,128)(2,1)}) custom-call(f32[768,128]{1,0:T(8,128)} %get-tuple-element.46.refs_4_.refs_0_, s16[6,144,128]{2,1,0:T(8,128)(2,1)} %copy-done.11, s16[2,784,128]{2,1,0:T(8,128)(2,1)} %get-tuple-element.49.refs_2_, bf16[1536,128]{1,0:T(8,128)(2,1)} %copy-done.4, bf16[1536,128]{1,0:T(8,128)(2,1)} %copy-done.5), custom_call_target="tpu_custom_call" | custom-call | flops 1 | bytes 1 | tf_op jit(solution)/shard_map/add_coded/pallas_call | solution.py:221
  75.0 3.4 %collective-permute-start.15 = (s16[6,144,128]{2,1,0:T(8,128)(2,1)}, s16[6,144,128]{2,1,0:T(8,128)(2,1)}, u32[]{:S(2)}, u32[]{:S(2)}) collective-permute-start(s16[6,144,128]{2,1,0:T(8,128)(2,1)} %get-tuple-element.51), channel_id=1, source_target_pairs={{0,4},{1,5},{2,6},{3,7},{4,0},{5,1},{6,2},{7,3},{8,12},{9,13},{10,... | collective-permute-start | bytes 663560 | tf_op jit(solution)/shard_map/ppermute | solution.py:608
  78.5 4.8 %project.13 = (s16[2,784,128]{2,1,0:T(8,128)(2,1)}, s16[2,784,128]{2,1,0:T(8,128)(2,1)}) custom-call(s32[8]{0:T(128)} %compare_select_fusion.2.place_ref, bf16[3072,1024]{1,0:T(8,128)(2,1)} %x_ref.19, bf16[1024,1024]{1,0:T(8,128)(2,1)} %refs_1_.15, bf16[1024,1024]{1,0:T(8,128)(2,1)} %refs_1_.15, s16[2,784,128]{2,1,0:T(8,128)(2,1)} %collective-permute-done.16.refs_2_, ...), custom_call_target="tpu_custom_call" | custom-call | flops 1 | bytes 1 | tf_op jit(solution)/shard_map/project/pallas_call | solution.py:183
  83.7 4.8 %collective-permute-done.18.refs_3_.refs_8_ = bf16[1536,128]{1,0:T(8,128)(2,1)} collective-permute-done((bf16[1536,128]{1,0:T(8,128)(2,1)}, bf16[1536,128]{1,0:T(8,128)(2,1)}, u32[]{:S(2)}, u32[]{:S(2)}) %collective-permute-start.18) | collective-permute-done | bytes 393248 | tf_op jit(solution)/shard_map/ppermute | solution.py:605
  88.5 3.9 %copy.15 = bf16[1024,1024]{0,1:T(8,128)(2,1)} copy(bf16[1024,1024]{1,0:T(8,128)(2,1)} %refs_1_.15) | data formatting | bytes 4194304 | tf_op args[4]
  92.4 1.0 copy.16
  93.4 1.9 %add_coded.5.low_ref.refs_0_.refs_12_ = f32[768,128]{1,0:T(8,128)} custom-call(f32[768,128]{1,0:T(8,128)} %get-tuple-element.50.refs_4_.refs_0_, s16[6,144,128]{2,1,0:T(8,128)(2,1)} %collective-permute-done.15.refs_1_, s16[2,784,128]{2,1,0:T(8,128)(2,1)} %get-tuple-element.53.refs_2_, bf16[1536,128]{1,0:T(8,128)(2,1)} %collective-permute-done.18.refs_3_.refs_8_, ...), custom_call_target="tpu_custom_call" | custom-call | flops 1 | bytes 1 | tf_op jit(solution)/shard_map/add_coded/pallas_call | solution.py:221
  95.3 9.4 %factor_gradients.1 = (f32[128,1152]{1,0:T(8,128)}, f32[128,1152]{1,0:T(8,128)}) custom-call(s32[24]{0:T(128)} %job_ref.9, s32[1]{0:T(128)} %bitcast.me_ref, bf16[3072,1024]{1,0:T(8,128)(2,1)} %x_ref.19, bf16[3072,128]{1,0:T(8,128)(2,1)} %get-tuple-element.37.dy_ref.refs_0_, f32[768,128]{1,0:T(8,128)} %add_coded.5.low_ref.refs_0_.refs_12_, ...), custom_call_target="tpu_custom_call" | custom-call | flops 1 | bytes 1 | tf_op jit(solution)/shard_map/factor_gradients/pallas_call | solution.py:352
  104.7 1.9 %collective-permute-start.30 = (f32[128,1152]{1,0:T(8,128)}, f32[128,1152]{1,0:T(8,128)}, u32[]{:S(2)}, u32[]{:S(2)}) collective-permute-start(f32[128,1152]{1,0:T(8,128)} %get-tuple-element.61), channel_id=1, source_target_pairs={{0,8},{8,0},{1,9},{9,1},{2,10},{10,2},{3,11},{11,3},{4,12},{12,4},... | collective-permute-start | bytes 1769480 | tf_op jit(solution)/shard_map/ppermute | solution.py:684
  106.6 1.8 %collective-permute-start.22 = (s16[2,784,128]{2,1,0:T(8,128)(2,1)}, s16[2,784,128]{2,1,0:T(8,128)(2,1)}, u32[]{:S(2)}, u32[]{:S(2)}) collective-permute-start(s16[2,784,128]{2,1,0:T(8,128)(2,1)} %get-tuple-element.57), channel_id=1, source_target_pairs={{0,1},{2,0},{4,2},{6,4},{7,6},{5,7},{3,5},{1,3},{8,9},{10,8},{12,1... | collective-permute-start | bytes 1204232 | tf_op jit(solution)/shard_map/ppermute | solution.py:605
  108.4 1.4 collective-permute-start.29
  110.1 4.4 %project.14 = (s16[2,784,128]{2,1,0:T(8,128)(2,1)}, f32[1536,128]{1,0:T(8,128)}) custom-call(s32[8]{0:T(128)} %compare_select_fusion.2.place_ref, bf16[3072,1024]{1,0:T(8,128)(2,1)} %x_ref.19, bf16[1024,1024]{1,0:T(8,128)(2,1)} %refs_1_.15, bf16[1024,1024]{1,0:T(8,128)(2,1)} %refs_1_.15, s16[2,784,128]{2,1,0:T(8,128)(2,1)} %collective-permute-done.20.refs_2_, ...), custom_call_target="tpu_custom_call" | custom-call | flops 1 | bytes 1 | tf_op jit(solution)/shard_map/project/pallas_call | solution.py:183
  114.5 4.5 %project.15 = (s16[2,784,128]{2,1,0:T(8,128)(2,1)}, f32[1536,128]{1,0:T(8,128)}) custom-call(s32[8]{0:T(128)} %compare_select_fusion.2.place_ref, bf16[3072,1024]{1,0:T(8,128)(2,1)} %x_ref.19, bf16[1024,1024]{1,0:T(8,128)(2,1)} %refs_1_.15, bf16[1024,1024]{1,0:T(8,128)(2,1)} %refs_1_.15, s16[2,784,128]{2,1,0:T(8,128)(2,1)} %collective-permute-done.23.refs_2_, ...), custom_call_target="tpu_custom_call" | custom-call | flops 1 | bytes 1 | tf_op jit(solution)/shard_map/project/pallas_call | solution.py:183
  119.0 1.3 collective-permute-start.26
  120.6 6.2 %collective-permute-done.29.refs_16_.refs_4_ = bf16[1536,128]{1,0:T(8,128)(2,1)} collective-permute-done((bf16[1536,128]{1,0:T(8,128)(2,1)}, bf16[1536,128]{1,0:T(8,128)(2,1)}, u32[]{:S(2)}, u32[]{:S(2)}) %collective-permute-start.29) | collective-permute-done | bytes 393248 | tf_op jit(solution)/shard_map/ppermute | solution.py:605
  126.8 1.3 collective-permute-start.25
  128.2 1.3 collective-permute-start.32
  129.5 9.4 %input_gradient.2.refs_14_ = f32[3072,1024]{1,0:T(8,128)} custom-call(s32[24]{0:T(128)} %job_ref.9, s32[8]{0:T(128)} %compare_select_fusion.2.place_ref, bf16[1024,1024]{1,0:T(8,128)(2,1)} %bitcast.6, bf16[1024,1024]{1,0:T(8,128)(2,1)} %bitcast.7, bf16[1024,1024]{1,0:T(8,128)(2,1)} %bitcast.8, bf16[1024,1024]{1,0:T(8,128)(2,1)} %bitcast.9, ...), custom_call_target="tpu_custom_call" | custom-call | flops 1 | bytes 1 | tf_op jit(solution)/shard_map/input_gradient/pallas_call | solution.py:502
  138.9 2.2 %add_factors.1 = (f32[1024,128]{1,0:T(8,128)}, f32[128,128]{1,0:T(8,128)}) custom-call(f32[128,1152]{1,0:T(8,128)} %get-tuple-element.54.refs_3_.kept_ref, f32[128,1152]{1,0:T(8,128)} %collective-permute-done.30.received_ref, s16[2,784,128]{2,1,0:T(8,128)(2,1)} %get-tuple-element.59.refs_14_.refs_0_), custom_call_target="tpu_custom_call" | custom-call | flops 1 | bytes 1 | tf_op jit(solution)/shard_map/add_factors/pallas_call | solution.py:382
  141.2 9.5 %input_gradient.3.refs_6_ = f32[3072,1024]{1,0:T(8,128)} custom-call(s32[24]{0:T(128)} %job_ref.9, s32[8]{0:T(128)} %compare_select_fusion.2.place_ref, bf16[1024,1024]{1,0:T(8,128)(2,1)} %bitcast.12, bf16[1024,1024]{1,0:T(8,128)(2,1)} %bitcast.13, bf16[1024,1024]{1,0:T(8,128)(2,1)} %bitcast.14, ...), custom_call_target="tpu_custom_call", output_to_operand_aliasing={{}: (16, {})} | custom-call | flops 1 | bytes 1 | tf_op jit(solution)/shard_map/input_gradient/pallas_call | solution.py:502
  150.7 1.4 collective-permute-done.32.refs_8_.refs_5_
  152.9 4.7 %place_output.1 = (bf16[32,128,128]{2,1,0:T(8,128)(2,1)}, bf16[16,128,128]{2,1,0:T(8,128)(2,1)}) custom-call(s32[24]{0:T(128)} %group_ref.3, s32[24]{0:T(128)} %slot_ref.3, s32[24]{0:T(128)} %job_ref.9, s32[1]{0:T(128)} %bitcast.me_ref, f32[768,128]{1,0:T(8,128)} %add_coded.5.low_ref.refs_0_.refs_12_, bf16[256,128]{1,0:T(8,128)(2,1)} %b_ref.1, ...), custom_call_target="tpu_custom_call" | custom-call | flops 1 | bytes 1 | tf_op jit(solution)/shard_map/place_output/pallas_call | solution.py:426
  158.3 9.5 %add_pieces.1 = bf16[3072,1024]{1,0:T(8,128)(2,1)} custom-call(s32[8]{0:T(128)} %compare_select_fusion.2.place_ref, bf16[1024,1024]{1,0:T(8,128)(2,1)} %bitcast.18, bf16[1024,1024]{1,0:T(8,128)(2,1)} %bitcast.19, bf16[1536,128]{1,0:T(8,128)(2,1)} %copy-done, bf16[1536,128]{1,0:T(8,128)(2,1)} %copy-done.7, ...), custom_call_target="tpu_custom_call" | custom-call | flops 1 | bytes 1 | tf_op jit(solution)/shard_map/add_pieces/pallas_call | solution.py:559
  167.8 0.8 copy-done.9
  168.6 1.9 %complete.1 = bf16[32,128,128]{2,1,0:T(8,128)(2,1)} custom-call(s32[1]{0:T(128)} %bitcast.me_ref, bf16[16,128,128]{2,1,0:T(8,128)(2,1)} %copy-done.9, bf16[32,128,128]{2,1,0:T(8,128)(2,1)} %get-tuple-element.64.kept_ref.refs_7_), custom_call_target="tpu_custom_call", output_to_operand_aliasing={{}: (2, {})} | custom-call | flops 1 | bytes 1 | tf_op jit(solution)/shard_map/complete/pallas_call | solution.py:444
  (69 shorter events, 5.3 us)
Async XLA Ops:
  1.7 13.8 %collective-permute-start = (bf16[2048,128]{1,0:T(8,128)(2,1)S(1)}, bf16[2048,128]{1,0:T(8,128)(2,1)}, u32[]{:S(2)}, u32[]{:S(2)}) collective-permute-start(bf16[2048,128]{1,0:T(8,128)(2,1)S(1)} %constant_dynamic-slice_fusion), channel_id=1, source_target_pairs={{0,8},{8,0},{1,9},{9,1},{2,10},{10,2},{3,11},{11,3},{4,12},{12,4},... | collective-permute-start | bytes 1572872 | tf_op jit(solution)/shard_map/ppermute | solution.py:611
  6.8 13.1 %collective-permute-start.4 = (s16[2,784,128]{2,1,0:T(8,128)(2,1)}, s16[2,784,128]{2,1,0:T(8,128)(2,1)}, u32[]{:S(2)}, u32[]{:S(2)}) collective-permute-start(s16[2,784,128]{2,1,0:T(8,128)(2,1)} %get-tuple-element.35.refs_2_), channel_id=1, source_target_pairs={{0,2},{2,4},{4,6},{6,7},{7,5},{5,3},{3,1},{1,0},{8,10},{10,12},{12... | collective-permute-start | bytes 1204232 | tf_op jit(solution)/shard_map/ppermute | solution.py:602
  9.5 19.8 %copy-start.10 = (bf16[256,128]{1,0:T(8,128)(2,1)S(1)}, bf16[256,128]{1,0:T(8,128)(2,1)}, u32[]{:S(2)}) copy-start(bf16[256,128]{1,0:T(8,128)(2,1)} %b_ref.1) | copy-start | bytes 196612
  9.5 11.2 %collective-permute-start.5 = (s16[2,784,128]{2,1,0:T(8,128)(2,1)}, s16[2,784,128]{2,1,0:T(8,128)(2,1)}, u32[]{:S(2)}, u32[]{:S(2)}) collective-permute-start(s16[2,784,128]{2,1,0:T(8,128)(2,1)} %get-tuple-element.41), channel_id=1, source_target_pairs={{0,1},{2,0},{4,2},{6,4},{7,6},{5,7},{3,5},{1,3},{8,9},{10,8},{12,1... | collective-permute-start | bytes 1204232 | tf_op jit(solution)/shard_map/ppermute | solution.py:605
  14.1 13.9 %collective-permute-start.2 = (s16[2,784,128]{2,1,0:T(8,128)(2,1)}, s16[2,784,128]{2,1,0:T(8,128)(2,1)}, u32[]{:S(2)}, u32[]{:S(2)}) collective-permute-start(s16[2,784,128]{2,1,0:T(8,128)(2,1)} %get-tuple-element.36.refs_0_), channel_id=1, source_target_pairs={{0,2},{2,4},{4,6},{6,7},{7,5},{5,3},{3,1},{1,0},{8,10},{10,12},{12... | collective-permute-start | bytes 1204232 | tf_op jit(solution)/shard_map/ppermute | solution.py:602
  15.4 21.3 %collective-permute-start.3 = (s16[2,784,128]{2,1,0:T(8,128)(2,1)}, s16[2,784,128]{2,1,0:T(8,128)(2,1)}, u32[]{:S(2)}, u32[]{:S(2)}) collective-permute-start(s16[2,784,128]{2,1,0:T(8,128)(2,1)} %get-tuple-element.40), channel_id=1, source_target_pairs={{0,1},{2,0},{4,2},{6,4},{7,6},{5,7},{3,5},{1,3},{8,9},{10,8},{12,1... | collective-permute-start | bytes 1204232 | tf_op jit(solution)/shard_map/ppermute | solution.py:605
  18.7 23.0 %collective-permute-start.6 = (bf16[1536,128]{1,0:T(8,128)(2,1)}, bf16[1536,128]{1,0:T(8,128)(2,1)S(1)}, u32[]{:S(2)}, u32[]{:S(2)}) collective-permute-start(bf16[1536,128]{1,0:T(8,128)(2,1)} %get-tuple-element.43.refs_6_), channel_id=1, source_target_pairs={{0,1},{2,0},{4,2},{6,4},{7,6},{5,7},{3,5},{1,3},{8,9},{10,8},{12,1... | collective-permute-start | bytes 1179656 | tf_op jit(solution)/shard_map/ppermute | solution.py:605
  19.9 23.0 %collective-permute-start.7 = (bf16[1536,128]{1,0:T(8,128)(2,1)}, bf16[1536,128]{1,0:T(8,128)(2,1)S(1)}, u32[]{:S(2)}, u32[]{:S(2)}) collective-permute-start(bf16[1536,128]{1,0:T(8,128)(2,1)} %get-tuple-element.43.refs_6_), channel_id=1, source_target_pairs={{0,2},{2,4},{4,6},{6,7},{7,5},{5,3},{3,1},{1,0},{8,10},{10,12},{12... | collective-permute-start | bytes 1179656 | tf_op jit(solution)/shard_map/ppermute | solution.py:602
  20.7 28.9 %collective-permute-start.8 = (bf16[1536,128]{1,0:T(8,128)(2,1)}, bf16[1536,128]{1,0:T(8,128)(2,1)}, u32[]{:S(2)}, u32[]{:S(2)}) collective-permute-start(bf16[1536,128]{1,0:T(8,128)(2,1)} %get-tuple-element.45.refs_6_), channel_id=1, source_target_pairs={{0,1},{2,0},{4,2},{6,4},{7,6},{5,7},{3,5},{1,3},{8,9},{10,8},{12,1... | collective-permute-start | bytes 1179656 | tf_op jit(solution)/shard_map/ppermute | solution.py:605
  28.0 21.6 %collective-permute-start.9 = (bf16[1536,128]{1,0:T(8,128)(2,1)}, bf16[1536,128]{1,0:T(8,128)(2,1)}, u32[]{:S(2)}, u32[]{:S(2)}) collective-permute-start(bf16[1536,128]{1,0:T(8,128)(2,1)} %get-tuple-element.45.refs_6_), channel_id=1, source_target_pairs={{0,2},{2,4},{4,6},{6,7},{7,5},{5,3},{3,1},{1,0},{8,10},{10,12},{12... | collective-permute-start | bytes 1179656 | tf_op jit(solution)/shard_map/ppermute | solution.py:602
  36.7 12.9 %collective-permute-start.1 = (s16[6,144,128]{2,1,0:T(8,128)(2,1)}, s16[6,144,128]{2,1,0:T(8,128)(2,1)}, u32[]{:S(2)}, u32[]{:S(2)}) collective-permute-start(s16[6,144,128]{2,1,0:T(8,128)(2,1)} %get-tuple-element.39.refs_4_), channel_id=1, source_target_pairs={{0,1},{1,0},{2,3},{3,2},{4,5},{5,4},{6,7},{7,6},{8,9},{9,8},{10,11... | collective-permute-start | bytes 663560 | tf_op jit(solution)/shard_map/ppermute | solution.py:608
  41.6 1.5 copy-start.2
  41.6 16.6 %collective-permute-start.11 = (s16[2,784,128]{2,1,0:T(8,128)(2,1)}, s16[2,784,128]{2,1,0:T(8,128)(2,1)}, u32[]{:S(2)}, u32[]{:S(2)}) collective-permute-start(s16[2,784,128]{2,1,0:T(8,128)(2,1)} %get-tuple-element.42.refs_4_), channel_id=1, source_target_pairs={{0,2},{2,4},{4,6},{6,7},{7,5},{5,3},{3,1},{1,0},{8,10},{10,12},{12... | collective-permute-start | bytes 1204232 | tf_op jit(solution)/shard_map/ppermute | solution.py:602
  42.9 0.8 copy-start.3
  42.9 15.3 %collective-permute-start.12 = (s16[2,784,128]{2,1,0:T(8,128)(2,1)}, s16[2,784,128]{2,1,0:T(8,128)(2,1)}, u32[]{:S(2)}, u32[]{:S(2)}) collective-permute-start(s16[2,784,128]{2,1,0:T(8,128)(2,1)} %get-tuple-element.48), channel_id=1, source_target_pairs={{0,1},{2,0},{4,2},{6,4},{7,6},{5,7},{3,5},{1,3},{8,9},{10,8},{12,1... | collective-permute-start | bytes 1204232 | tf_op jit(solution)/shard_map/ppermute | solution.py:605
  51.6 8.1 %collective-permute-start.10 = (s16[6,144,128]{2,1,0:T(8,128)(2,1)}, s16[6,144,128]{2,1,0:T(8,128)(2,1)S(1)}, u32[]{:S(2)}, u32[]{:S(2)}) collective-permute-start(s16[6,144,128]{2,1,0:T(8,128)(2,1)} %get-tuple-element.47), channel_id=1, source_target_pairs={{0,2},{1,3},{2,0},{3,1},{4,6},{5,7},{6,4},{7,5},{8,10},{9,11},{10,... | collective-permute-start | bytes 663560 | tf_op jit(solution)/shard_map/ppermute | solution.py:608
  51.7 15.9 %collective-permute-start.13 = (bf16[1536,128]{1,0:T(8,128)(2,1)}, bf16[1536,128]{1,0:T(8,128)(2,1)S(1)}, u32[]{:S(2)}, u32[]{:S(2)}) collective-permute-start(bf16[1536,128]{1,0:T(8,128)(2,1)} %copy-done.2), channel_id=1, source_target_pairs={{0,1},{2,0},{4,2},{6,4},{7,6},{5,7},{3,5},{1,3},{8,9},{10,8},{12,1... | collective-permute-start | bytes 1179656 | tf_op jit(solution)/shard_map/ppermute | solution.py:605
  52.9 19.4 %collective-permute-start.14 = (bf16[1536,128]{1,0:T(8,128)(2,1)}, bf16[1536,128]{1,0:T(8,128)(2,1)S(1)}, u32[]{:S(2)}, u32[]{:S(2)}) collective-permute-start(bf16[1536,128]{1,0:T(8,128)(2,1)} %copy-done.3), channel_id=1, source_target_pairs={{0,2},{2,4},{4,6},{6,7},{7,5},{5,3},{3,1},{1,0},{8,10},{10,12},{12... | collective-permute-start | bytes 1179656 | tf_op jit(solution)/shard_map/ppermute | solution.py:602
  58.2 20.3 %collective-permute-start.16 = (s16[2,784,128]{2,1,0:T(8,128)(2,1)}, s16[2,784,128]{2,1,0:T(8,128)(2,1)}, u32[]{:S(2)}, u32[]{:S(2)}) collective-permute-start(s16[2,784,128]{2,1,0:T(8,128)(2,1)} %get-tuple-element.44.refs_2_), channel_id=1, source_target_pairs={{0,2},{2,4},{4,6},{6,7},{7,5},{5,3},{3,1},{1,0},{8,10},{10,12},{12... | collective-permute-start | bytes 1204232 | tf_op jit(solution)/shard_map/ppermute | solution.py:602
  58.2 20.3 %collective-permute-start.17 = (s16[2,784,128]{2,1,0:T(8,128)(2,1)}, s16[2,784,128]{2,1,0:T(8,128)(2,1)}, u32[]{:S(2)}, u32[]{:S(2)}) collective-permute-start(s16[2,784,128]{2,1,0:T(8,128)(2,1)} %get-tuple-element.52), channel_id=1, source_target_pairs={{0,1},{2,0},{4,2},{6,4},{7,6},{5,7},{3,5},{1,3},{8,9},{10,8},{12,1... | collective-permute-start | bytes 1204232 | tf_op jit(solution)/shard_map/ppermute | solution.py:605
  59.7 7.9 %copy-start.11 = (s16[6,144,128]{2,1,0:T(8,128)(2,1)}, s16[6,144,128]{2,1,0:T(8,128)(2,1)S(1)}, u32[]{:S(2)}) copy-start(s16[6,144,128]{2,1,0:T(8,128)(2,1)S(1)} %collective-permute-done.10.refs_1_) | copy-start | bytes 663556
  59.7 28.8 %collective-permute-start.18 = (bf16[1536,128]{1,0:T(8,128)(2,1)}, bf16[1536,128]{1,0:T(8,128)(2,1)}, u32[]{:S(2)}, u32[]{:S(2)}) collective-permute-start(bf16[1536,128]{1,0:T(8,128)(2,1)} %collective-permute-done.8.refs_3_.refs_7_), channel_id=1, source_target_pairs={{0,1},{2,0},{4,2},{6,4},{7,6},{5,7},{3,5},{1,3},{8,9},{10,8},{12,1... | collective-permute-start | bytes 1179656 | tf_op jit(solution)/shard_map/ppermute | solution.py:605
  67.6 4.7 %copy-start.4 = (bf16[1536,128]{1,0:T(8,128)(2,1)}, bf16[1536,128]{1,0:T(8,128)(2,1)S(1)}, u32[]{:S(2)}) copy-start(bf16[1536,128]{1,0:T(8,128)(2,1)S(1)} %collective-permute-done.13.refs_3_.refs_8_) | copy-start | bytes 1179652
  67.6 25.8 %collective-permute-start.19 = (bf16[1536,128]{1,0:T(8,128)(2,1)}, bf16[1536,128]{1,0:T(8,128)(2,1)}, u32[]{:S(2)}, u32[]{:S(2)}) collective-permute-start(bf16[1536,128]{1,0:T(8,128)(2,1)} %collective-permute-done.9.refs_4_.refs_11_), channel_id=1, source_target_pairs={{0,2},{2,4},{4,6},{6,7},{7,5},{5,3},{3,1},{1,0},{8,10},{10,12},{12... | collective-permute-start | bytes 1179656 | tf_op jit(solution)/shard_map/ppermute | solution.py:602
  72.3 0.8 copy-start.5
  75.0 18.4 %collective-permute-start.15 = (s16[6,144,128]{2,1,0:T(8,128)(2,1)}, s16[6,144,128]{2,1,0:T(8,128)(2,1)}, u32[]{:S(2)}, u32[]{:S(2)}) collective-permute-start(s16[6,144,128]{2,1,0:T(8,128)(2,1)} %get-tuple-element.51), channel_id=1, source_target_pairs={{0,4},{1,5},{2,6},{3,7},{4,0},{5,1},{6,2},{7,3},{8,12},{9,13},{10,... | collective-permute-start | bytes 663560 | tf_op jit(solution)/shard_map/ppermute | solution.py:608
  78.5 29.9 %collective-permute-start.20 = (s16[2,784,128]{2,1,0:T(8,128)(2,1)}, s16[2,784,128]{2,1,0:T(8,128)(2,1)}, u32[]{:S(2)}, u32[]{:S(2)}) collective-permute-start(s16[2,784,128]{2,1,0:T(8,128)(2,1)} %get-tuple-element.49.refs_2_), channel_id=1, source_target_pairs={{0,2},{2,4},{4,6},{6,7},{7,5},{5,3},{3,1},{1,0},{8,10},{10,12},{12... | collective-permute-start | bytes 1204232 | tf_op jit(solution)/shard_map/ppermute | solution.py:602
  78.5 13.9 %copy-start.1 = (bf16[1024,256]{1,0:T(8,128)(2,1)S(1)}, bf16[1024,256]{1,0:T(8,128)(2,1)}, u32[]{:S(2)}) copy-start(bf16[1024,256]{1,0:T(8,128)(2,1)} %a_ref.1) | copy-start | bytes 1572868
  83.3 26.5 %collective-permute-start.23 = (s16[2,784,128]{2,1,0:T(8,128)(2,1)}, s16[2,784,128]{2,1,0:T(8,128)(2,1)}, u32[]{:S(2)}, u32[]{:S(2)}) collective-permute-start(s16[2,784,128]{2,1,0:T(8,128)(2,1)} %get-tuple-element.53.refs_2_), channel_id=1, source_target_pairs={{0,2},{2,4},{4,6},{6,7},{7,5},{5,3},{3,1},{1,0},{8,10},{10,12},{12... | collective-permute-start | bytes 1204232 | tf_op jit(solution)/shard_map/ppermute | solution.py:602
  88.5 20.0 %collective-permute-start.24 = (bf16[1536,128]{1,0:T(8,128)(2,1)}, bf16[1536,128]{1,0:T(8,128)(2,1)S(1)}, u32[]{:S(2)}, u32[]{:S(2)}) collective-permute-start(bf16[1536,128]{1,0:T(8,128)(2,1)} %copy-done.4), channel_id=1, source_target_pairs={{0,1},{2,0},{4,2},{6,4},{7,6},{5,7},{3,5},{1,3},{8,9},{10,8},{12,1... | collective-permute-start | bytes 1179656 | tf_op jit(solution)/shard_map/ppermute | solution.py:605
  93.4 15.0 %copy-start.6 = (bf16[1536,128]{1,0:T(8,128)(2,1)S(1)}, bf16[1536,128]{1,0:T(8,128)(2,1)}, u32[]{:S(2)}) copy-start(bf16[1536,128]{1,0:T(8,128)(2,1)} %copy-done.5) | copy-start | bytes 1179652
  104.7 23.5 %collective-permute-start.30 = (f32[128,1152]{1,0:T(8,128)}, f32[128,1152]{1,0:T(8,128)}, u32[]{:S(2)}, u32[]{:S(2)}) collective-permute-start(f32[128,1152]{1,0:T(8,128)} %get-tuple-element.61), channel_id=1, source_target_pairs={{0,8},{8,0},{1,9},{9,1},{2,10},{10,2},{3,11},{11,3},{4,12},{12,4},... | collective-permute-start | bytes 1769480 | tf_op jit(solution)/shard_map/ppermute | solution.py:684
  106.6 12.4 %collective-permute-start.22 = (s16[2,784,128]{2,1,0:T(8,128)(2,1)}, s16[2,784,128]{2,1,0:T(8,128)(2,1)}, u32[]{:S(2)}, u32[]{:S(2)}) collective-permute-start(s16[2,784,128]{2,1,0:T(8,128)(2,1)} %get-tuple-element.57), channel_id=1, source_target_pairs={{0,1},{2,0},{4,2},{6,4},{7,6},{5,7},{3,5},{1,3},{8,9},{10,8},{12,1... | collective-permute-start | bytes 1204232 | tf_op jit(solution)/shard_map/ppermute | solution.py:605
  108.4 11.9 %collective-permute-start.28 = (bf16[1536,128]{1,0:T(8,128)(2,1)S(1)}, bf16[1536,128]{1,0:T(8,128)(2,1)}, u32[]{:S(2)}, u32[]{:S(2)}) collective-permute-start(bf16[1536,128]{1,0:T(8,128)(2,1)S(1)} %copy-done.6), channel_id=1, source_target_pairs={{0,2},{2,4},{4,6},{6,7},{7,5},{5,3},{3,1},{1,0},{8,10},{10,12},{12... | collective-permute-start | bytes 1179656 | tf_op jit(solution)/shard_map/ppermute | solution.py:602
  108.4 6.1 %copy-start = (bf16[1536,128]{1,0:T(8,128)(2,1)}, bf16[1536,128]{1,0:T(8,128)(2,1)S(1)}, u32[]{:S(2)}) copy-start(bf16[1536,128]{1,0:T(8,128)(2,1)S(1)} %collective-permute-done.24.refs_4_.refs_15_.refs_2_) | copy-start | bytes 1179652
  108.4 18.3 %collective-permute-start.29 = (bf16[1536,128]{1,0:T(8,128)(2,1)}, bf16[1536,128]{1,0:T(8,128)(2,1)}, u32[]{:S(2)}, u32[]{:S(2)}) collective-permute-start(bf16[1536,128]{1,0:T(8,128)(2,1)} %collective-permute-done.18.refs_3_.refs_8_), channel_id=1, source_target_pairs={{0,1},{2,0},{4,2},{6,4},{7,6},{5,7},{3,5},{1,3},{8,9},{10,8},{12,1... | collective-permute-start | bytes 1179656 | tf_op jit(solution)/shard_map/ppermute | solution.py:605
  109.9 18.2 %collective-permute-start.27 = (bf16[1536,128]{1,0:T(8,128)(2,1)}, bf16[1536,128]{1,0:T(8,128)(2,1)}, u32[]{:S(2)}, u32[]{:S(2)}) collective-permute-start(bf16[1536,128]{1,0:T(8,128)(2,1)} %collective-permute-done.19.refs_4_.refs_10_), channel_id=1, source_target_pairs={{0,2},{2,4},{4,6},{6,7},{7,5},{5,3},{3,1},{1,0},{8,10},{10,12},{12... | collective-permute-start | bytes 1179656 | tf_op jit(solution)/shard_map/ppermute | solution.py:602
  119.0 31.6 %collective-permute-start.26 = (s16[2,784,128]{2,1,0:T(8,128)(2,1)}, s16[2,784,128]{2,1,0:T(8,128)(2,1)}, u32[]{:S(2)}, u32[]{:S(2)}) collective-permute-start(s16[2,784,128]{2,1,0:T(8,128)(2,1)} %get-tuple-element.60), channel_id=1, source_target_pairs={{0,1},{2,0},{4,2},{6,4},{7,6},{5,7},{3,5},{1,3},{8,9},{10,8},{12,1... | collective-permute-start | bytes 1204232 | tf_op jit(solution)/shard_map/ppermute | solution.py:605
  120.3 30.3 %collective-permute-start.21 = (s16[2,784,128]{2,1,0:T(8,128)(2,1)}, s16[2,784,128]{2,1,0:T(8,128)(2,1)}, u32[]{:S(2)}, u32[]{:S(2)}) collective-permute-start(s16[2,784,128]{2,1,0:T(8,128)(2,1)} %get-tuple-element.56.refs_3_), channel_id=1, source_target_pairs={{0,2},{2,4},{4,6},{6,7},{7,5},{5,3},{3,1},{1,0},{8,10},{10,12},{12... | collective-permute-start | bytes 1204232 | tf_op jit(solution)/shard_map/ppermute | solution.py:602
  126.8 25.4 %collective-permute-start.25 = (s16[2,784,128]{2,1,0:T(8,128)(2,1)}, s16[2,784,128]{2,1,0:T(8,128)(2,1)}, u32[]{:S(2)}, u32[]{:S(2)}) collective-permute-start(s16[2,784,128]{2,1,0:T(8,128)(2,1)} %get-tuple-element.59.refs_14_.refs_0_), channel_id=1, source_target_pairs={{0,2},{2,4},{4,6},{6,7},{7,5},{5,3},{3,1},{1,0},{8,10},{10,12},{12... | collective-permute-start | bytes 1204232 | tf_op jit(solution)/shard_map/ppermute | solution.py:602
  128.0 22.6 %collective-permute-start.31 = (bf16[1536,128]{1,0:T(8,128)(2,1)}, bf16[1536,128]{1,0:T(8,128)(2,1)S(1)}, u32[]{:S(2)}, u32[]{:S(2)}) collective-permute-start(bf16[1536,128]{1,0:T(8,128)(2,1)} %copy-done), channel_id=1, source_target_pairs={{0,1},{2,0},{4,2},{6,4},{7,6},{5,7},{3,5},{1,3},{8,9},{10,8},{12,1... | collective-permute-start | bytes 1179656 | tf_op jit(solution)/shard_map/ppermute | solution.py:605
  128.2 23.9 %collective-permute-start.32 = (bf16[1536,128]{1,0:T(8,128)(2,1)}, bf16[1536,128]{1,0:T(8,128)(2,1)S(1)}, u32[]{:S(2)}, u32[]{:S(2)}) collective-permute-start(bf16[1536,128]{1,0:T(8,128)(2,1)} %collective-permute-done.29.refs_16_.refs_4_), channel_id=1, source_target_pairs={{0,1},{2,0},{4,2},{6,4},{7,6},{5,7},{3,5},{1,3},{8,9},{10,8},{12,1... | collective-permute-start | bytes 1179656 | tf_op jit(solution)/shard_map/ppermute | solution.py:605
  150.7 1.5 copy-start.7
  152.1 0.7 copy-start.8
  157.6 10.2 %collective-permute-start.33 = (bf16[16,128,128]{2,1,0:T(8,128)(2,1)}, bf16[16,128,128]{2,1,0:T(8,128)(2,1)S(1)}, u32[]{:S(2)}, u32[]{:S(2)}) collective-permute-start(bf16[16,128,128]{2,1,0:T(8,128)(2,1)} %get-tuple-element.63), channel_id=1, source_target_pairs={{0,8},{8,0},{1,9},{9,1},{2,10},{10,2},{3,11},{11,3},{4,12},{12,4},... | collective-permute-start | bytes 1572872 | tf_op jit(solution)/shard_map/ppermute | solution.py:700
  167.8 0.8 copy-start.9

commit v6 on v5

--- a/solution.py
+++ b/solution.py
@@ -662,6 +662,8 @@
             )
             last = (kept,)
         for k in both:
+            if d == 2 and k == 0:
+                last += (w_t, a_t)
             if near > d:
                 turn_r, turn_l = terms(
                     k, (far - d, size - (near - d)), (sums_r[k], sums_l[k]), False, last
@@ -684,14 +686,14 @@
     grad_a, grad_b = add_factors(kept, lax.ppermute(sent, "dp", swap), features, last[:1])
 
     late = (far - 1, far)
-    last = last[:1] + tuple(pieces[k][far - 1] for k in both)
+    last = last[:1] + (pieces[0][far - 1],)
     early = None
     for k in both:
         ready = {d: v for d, v in pieces[k].items() if d not in late}
         early = input_gradient(
             ready, w_t, place, low, a_t, job, length, step_blocks // 2, k, early, last
         )
-        last = (grad_b,)
+        last = (grad_b, pieces[1][far - 1])
     final = [{d: pieces[k][d] for d in late} for k in both]
     placed, sent = place_output(
         own, sums_r, sums_l, low, b, group, slot, job, mine, length, cap, (early,) + tuple(pieces[k][far] for k in both)

time: 171 us -> 171 us (level)
  starting transfers between devices: 27.3 us -> 31.9 us
  waiting for transfers between devices: 33.3 us -> 29.3 us
    ppermute x14, waiting for transfers between devices: 20.3 us -> 9.92 us  [left(): return lax.ppermute(v, 'tensor', back)]
    ppermute x14, waiting for transfers between devices: 11.7 us -> 18.3 us  [right(): return lax.ppermute(v, 'tensor', ahead)]
    ppermute x1, starting transfers between devices: 1.91 us -> 6.45 us  [ring(): lax.ppermute(sent, 'dp', swap)]
    unnamed x27 -> x25, local copies, waits for them, and re-layouts: 8.57 us -> 7.42 us
where the time goes in v6:
time: 171 us; the launch traced here: 170 us
  Pallas kernels  98.6 us (58%)
  starting transfers between devices  31.9 us (19%)
  waiting for transfers between devices  29.3 us (17%)
  local copies, waits for them, and re-layouts  8.51 us (5%)
    pallas_call x8, Pallas kernels, project(): pl.pallas_call(kernel, grid_spec=pltpu.PrefetchScalarGridSpec(num_scalar_...  36.6 us
    pallas_call x2, Pallas kernels, input_gradient(): pl.pallas_call(kernel, grid_spec=pltpu.PrefetchScalarGridSpec(num_scalar_...  18.8 us
    ppermute x14, waiting for transfers between devices, right(): return lax.ppermute(v, 'tensor', ahead)  18.3 us
    ppermute x14, starting transfers between devices, left(): return lax.ppermute(v, 'tensor', back)  11 us
    ppermute x14, waiting for transfers between devices, left(): return lax.ppermute(v, 'tensor', back)  9.92 us
    ppermute x14, starting transfers between devices, right(): return lax.ppermute(v, 'tensor', ahead)  9.55 us
    pallas_call x1, Pallas kernels, add_pieces(): pl.pallas_call(kernel, grid_spec=pltpu.PrefetchScalarGridSpec(num_scalar_...  9.5 us
    pallas_call x1, Pallas kernels, factor_gradients(): pl.pallas_call(kernel, grid_spec=pltpu.PrefetchScalarGridSpec(num_scalar_...  9.37 us
  transfers between devices with their start and end apart: 34, of which 7 were waited for; matrix products, arithmetic and copies ran while one was open for 4% of the time, Pallas kernels for 54%

profile of v6, /device:TPU:1, one launch (start us, length us, event | category | flops | bytes accessed | tf_op | source)
XLA Modules:
  0.0 169.7 jit_solution(12365478770136690596)
XLA Ops:
  0.6 1.1 constant_dynamic-slice_fusion
  2.4 4.4 %project.8 = (s16[2,784,128]{2,1,0:T(8,128)(2,1)}, s16[2,784,128]{2,1,0:T(8,128)(2,1)}) custom-call(s32[8]{0:T(128)} %compare_select_fusion.2.place_ref, bf16[3072,1024]{1,0:T(8,128)(2,1)} %x_ref.19, bf16[1024,1024]{1,0:T(8,128)(2,1)} %refs_1_.15, bf16[1024,1024]{1,0:T(8,128)(2,1)} %refs_1_.15), custom_call_target="tpu_custom_call" | custom-call | flops 1 | bytes 1 | tf_op jit(solution)/shard_map/project/pallas_call | solution.py:183
  6.8 2.7 %collective-permute-start.4 = (s16[2,784,128]{2,1,0:T(8,128)(2,1)}, s16[2,784,128]{2,1,0:T(8,128)(2,1)}, u32[]{:S(2)}, u32[]{:S(2)}) collective-permute-start(s16[2,784,128]{2,1,0:T(8,128)(2,1)} %get-tuple-element.35.refs_2_), channel_id=1, source_target_pairs={{0,2},{2,4},{4,6},{6,7},{7,5},{5,3},{3,1},{1,0},{8,10},{10,12},{12... | collective-permute-start | bytes 1204232 | tf_op jit(solution)/shard_map/ppermute | solution.py:602
  9.5 4.6 %project.9 = (s16[2,784,128]{2,1,0:T(8,128)(2,1)}, s16[2,784,128]{2,1,0:T(8,128)(2,1)}) custom-call(s32[8]{0:T(128)} %compare_select_fusion.2.place_ref, bf16[3072,1024]{1,0:T(8,128)(2,1)} %x_ref.19, bf16[1024,1024]{1,0:T(8,128)(2,1)} %refs_1_.15, bf16[1024,1024]{1,0:T(8,128)(2,1)} %refs_1_.15, s16[2,784,128]{2,1,0:T(8,128)(2,1)} %get-tuple-element.35.refs_2_), custom_call_target="tpu_custom_call" | custom-call | flops 1 | bytes 1 | tf_op jit(solution)/shard_map/project/pallas_call | solution.py:183
  14.1 1.3 collective-permute-start.2
  15.6 3.1 %home_gradient.1 = (bf16[3072,128]{1,0:T(8,128)(2,1)}, bf16[1536,128]{1,0:T(8,128)(2,1)}, bf16[1536,128]{1,0:T(8,128)(2,1)}) custom-call(s32[24]{0:T(128)} %group_ref.3, s32[24]{0:T(128)} %slot_ref.3, s32[1]{0:T(128)} %bitcast.me_ref, bf16[4096,128]{1,0:T(8,128)(2,1)} %dy_ref.1, bf16[2048,128]{1,0:T(8,128)(2,1)} %collective-permute-done.received_ref, ...), custom_call_target="tpu_custom_call" | custom-call | flops 1 | bytes 1 | tf_op jit(solution)/shard_map/home_gradient/pallas_call | solution.py:259
  18.7 1.3 collective-permute-start.6
  19.9 0.8 collective-permute-start.7
  21.4 6.6 %collective-permute-done.2.refs_2_ = s16[2,784,128]{2,1,0:T(8,128)(2,1)} collective-permute-done((s16[2,784,128]{2,1,0:T(8,128)(2,1)}, s16[2,784,128]{2,1,0:T(8,128)(2,1)}, u32[]{:S(2)}, u32[]{:S(2)}) %collective-permute-start.2) | collective-permute-done | bytes 401440 | tf_op jit(solution)/shard_map/ppermute | solution.py:602
  28.0 1.3 collective-permute-start.9
  29.3 0.7 copy.14
  30.1 6.7 %low_rank.1 = (f32[768,128]{1,0:T(8,128)}, s16[6,144,128]{2,1,0:T(8,128)(2,1)}) custom-call(s32[24]{0:T(128)} %job_ref.9, bf16[3072,1024]{1,0:T(8,128)(2,1)} %x_ref.19, bf16[1024,256]{1,0:T(8,128)(2,1)} %a_ref.1, bf16[3072,128]{1,0:T(8,128)(2,1)} %get-tuple-element.37.dy_ref.refs_0_, bf16[128,256]{1,0:T(8,128)(2,1)} %bitcast.26, ...), custom_call_target="tpu_custom_call" | custom-call | flops 1 | bytes 1 | tf_op jit(solution)/shard_map/low_rank/pallas_call | solution.py:291
  37.0 4.7 %project.10 = (s16[2,784,128]{2,1,0:T(8,128)(2,1)}, s16[2,784,128]{2,1,0:T(8,128)(2,1)}) custom-call(s32[8]{0:T(128)} %compare_select_fusion.2.place_ref, bf16[3072,1024]{1,0:T(8,128)(2,1)} %x_ref.19, bf16[1024,1024]{1,0:T(8,128)(2,1)} %refs_1_.15, bf16[1024,1024]{1,0:T(8,128)(2,1)} %refs_1_.15, s16[2,784,128]{2,1,0:T(8,128)(2,1)} %collective-permute-done.4.refs_2_, ...), custom_call_target="tpu_custom_call" | custom-call | flops 1 | bytes 1 | tf_op jit(solution)/shard_map/project/pallas_call | solution.py:183
  41.6 1.3 collective-permute-start.11
  42.9 0.8 copy-done.3
  43.9 4.7 %project.11 = (s16[2,784,128]{2,1,0:T(8,128)(2,1)}, s16[2,784,128]{2,1,0:T(8,128)(2,1)}) custom-call(s32[8]{0:T(128)} %compare_select_fusion.2.place_ref, bf16[3072,1024]{1,0:T(8,128)(2,1)} %x_ref.19, bf16[1024,1024]{1,0:T(8,128)(2,1)} %refs_1_.15, bf16[1024,1024]{1,0:T(8,128)(2,1)} %refs_1_.15, s16[2,784,128]{2,1,0:T(8,128)(2,1)} %collective-permute-done.2.refs_2_, ...), custom_call_target="tpu_custom_call" | custom-call | flops 1 | bytes 1 | tf_op jit(solution)/shard_map/project/pallas_call | solution.py:183
  48.6 1.0 collective-permute-done.1.refs_1_
  49.6 2.0 %add_coded.3 = (f32[768,128]{1,0:T(8,128)}, s16[6,144,128]{2,1,0:T(8,128)(2,1)}) custom-call(f32[768,128]{1,0:T(8,128)} %get-tuple-element.38.refs_0_, s16[6,144,128]{2,1,0:T(8,128)(2,1)} %collective-permute-done.1.refs_1_, s16[2,784,128]{2,1,0:T(8,128)(2,1)} %get-tuple-element.44.refs_2_, bf16[1536,128]{1,0:T(8,128)(2,1)} %collective-permute-done.8.refs_3_.refs_7_, ...), custom_call_target="tpu_custom_call" | custom-call | flops 1 | bytes 1 | tf_op jit(solution)/shard_map/add_coded/pallas_call | solution.py:221
  51.8 1.4 collective-permute-start.13
  53.3 4.9 %collective-permute-done.11.refs_2_ = s16[2,784,128]{2,1,0:T(8,128)(2,1)} collective-permute-done((s16[2,784,128]{2,1,0:T(8,128)(2,1)}, s16[2,784,128]{2,1,0:T(8,128)(2,1)}, u32[]{:S(2)}, u32[]{:S(2)}) %collective-permute-start.11) | collective-permute-done | bytes 401440 | tf_op jit(solution)/shard_map/ppermute | solution.py:602
  58.2 1.5 collective-permute-start.17
  59.7 7.8 %collective-permute-done.13.refs_3_.refs_8_ = bf16[1536,128]{1,0:T(8,128)(2,1)S(1)} collective-permute-done((bf16[1536,128]{1,0:T(8,128)(2,1)}, bf16[1536,128]{1,0:T(8,128)(2,1)S(1)}, u32[]{:S(2)}, u32[]{:S(2)}) %collective-permute-start.13) | collective-permute-done | bytes 393248 | tf_op jit(solution)/shard_map/ppermute | solution.py:605
  67.5 4.1 %copy.15 = bf16[1024,1024]{0,1:T(8,128)(2,1)} copy(bf16[1024,1024]{1,0:T(8,128)(2,1)} %refs_1_.15) | data formatting | bytes 4194304 | tf_op args[4]
  71.6 1.0 copy.16
  72.6 4.7 %project.12 = (s16[2,784,128]{2,1,0:T(8,128)(2,1)}, s16[2,784,128]{2,1,0:T(8,128)(2,1)}) custom-call(s32[8]{0:T(128)} %compare_select_fusion.2.place_ref, bf16[3072,1024]{1,0:T(8,128)(2,1)} %x_ref.19, bf16[1024,1024]{1,0:T(8,128)(2,1)} %refs_1_.15, bf16[1024,1024]{1,0:T(8,128)(2,1)} %refs_1_.15, s16[2,784,128]{2,1,0:T(8,128)(2,1)} %collective-permute-done.11.refs_2_, ...), custom_call_target="tpu_custom_call" | custom-call | flops 1 | bytes 1 | tf_op jit(solution)/shard_map/project/pallas_call | solution.py:183
  77.3 2.0 %add_coded.4 = (f32[768,128]{1,0:T(8,128)}, s16[6,144,128]{2,1,0:T(8,128)(2,1)}) custom-call(f32[768,128]{1,0:T(8,128)} %get-tuple-element.46.refs_4_.refs_0_, s16[6,144,128]{2,1,0:T(8,128)(2,1)} %copy-done.10, s16[2,784,128]{2,1,0:T(8,128)(2,1)} %get-tuple-element.49.refs_2_, bf16[1536,128]{1,0:T(8,128)(2,1)} %copy-done.4, ...), custom_call_target="tpu_custom_call" | custom-call | flops 1 | bytes 1 | tf_op jit(solution)/shard_map/add_coded/pallas_call | solution.py:221
  79.3 3.5 %collective-permute-start.15 = (s16[6,144,128]{2,1,0:T(8,128)(2,1)}, s16[6,144,128]{2,1,0:T(8,128)(2,1)}, u32[]{:S(2)}, u32[]{:S(2)}) collective-permute-start(s16[6,144,128]{2,1,0:T(8,128)(2,1)} %get-tuple-element.51), channel_id=1, source_target_pairs={{0,4},{1,5},{2,6},{3,7},{4,0},{5,1},{6,2},{7,3},{8,12},{9,13},{10,... | collective-permute-start | bytes 663560 | tf_op jit(solution)/shard_map/ppermute | solution.py:608
  82.9 4.7 %project.13 = (s16[2,784,128]{2,1,0:T(8,128)(2,1)}, s16[2,784,128]{2,1,0:T(8,128)(2,1)}) custom-call(s32[8]{0:T(128)} %compare_select_fusion.2.place_ref, bf16[3072,1024]{1,0:T(8,128)(2,1)} %x_ref.19, bf16[1024,1024]{1,0:T(8,128)(2,1)} %refs_1_.15, bf16[1024,1024]{1,0:T(8,128)(2,1)} %refs_1_.15, s16[2,784,128]{2,1,0:T(8,128)(2,1)} %collective-permute-done.16.refs_2_, ...), custom_call_target="tpu_custom_call" | custom-call | flops 1 | bytes 1 | tf_op jit(solution)/shard_map/project/pallas_call | solution.py:183
  87.8 1.3 collective-permute-start.24
  89.2 1.9 %add_coded.5.low_ref.refs_0_.refs_12_ = f32[768,128]{1,0:T(8,128)} custom-call(f32[768,128]{1,0:T(8,128)} %get-tuple-element.50.refs_4_.refs_0_, s16[6,144,128]{2,1,0:T(8,128)(2,1)} %collective-permute-done.15.refs_1_, s16[2,784,128]{2,1,0:T(8,128)(2,1)} %get-tuple-element.53.refs_2_, bf16[1536,128]{1,0:T(8,128)(2,1)} %collective-permute-done.18.refs_3_.refs_8_, ...), custom_call_target="tpu_custom_call" | custom-call | flops 1 | bytes 1 | tf_op jit(solution)/shard_map/add_coded/pallas_call | solution.py:221
  91.0 9.4 %factor_gradients.1 = (f32[128,1152]{1,0:T(8,128)}, f32[128,1152]{1,0:T(8,128)}) custom-call(s32[24]{0:T(128)} %job_ref.9, s32[1]{0:T(128)} %bitcast.me_ref, bf16[3072,1024]{1,0:T(8,128)(2,1)} %x_ref.19, bf16[3072,128]{1,0:T(8,128)(2,1)} %get-tuple-element.37.dy_ref.refs_0_, f32[768,128]{1,0:T(8,128)} %add_coded.5.low_ref.refs_0_.refs_12_, ...), custom_call_target="tpu_custom_call" | custom-call | flops 1 | bytes 1 | tf_op jit(solution)/shard_map/factor_gradients/pallas_call | solution.py:352
  100.4 6.4 %collective-permute-start.29 = (f32[128,1152]{1,0:T(8,128)}, f32[128,1152]{1,0:T(8,128)}, u32[]{:S(2)}, u32[]{:S(2)}) collective-permute-start(f32[128,1152]{1,0:T(8,128)} %get-tuple-element.61), channel_id=1, source_target_pairs={{0,8},{8,0},{1,9},{9,1},{2,10},{10,2},{3,11},{11,3},{4,12},{12,4},... | collective-permute-start | bytes 1769480 | tf_op jit(solution)/shard_map/ppermute | solution.py:686
  106.9 1.0 collective-permute-start.22
  108.4 1.4 collective-permute-start.30
  109.8 4.4 %project.14 = (s16[2,784,128]{2,1,0:T(8,128)(2,1)}, f32[1536,128]{1,0:T(8,128)}) custom-call(s32[8]{0:T(128)} %compare_select_fusion.2.place_ref, bf16[3072,1024]{1,0:T(8,128)(2,1)} %x_ref.19, bf16[1024,1024]{1,0:T(8,128)(2,1)} %refs_1_.15, bf16[1024,1024]{1,0:T(8,128)(2,1)} %refs_1_.15, s16[2,784,128]{2,1,0:T(8,128)(2,1)} %collective-permute-done.20.refs_2_, ...), custom_call_target="tpu_custom_call" | custom-call | flops 1 | bytes 1 | tf_op jit(solution)/shard_map/project/pallas_call | solution.py:183
  114.2 4.5 %project.15 = (s16[2,784,128]{2,1,0:T(8,128)(2,1)}, f32[1536,128]{1,0:T(8,128)}) custom-call(s32[8]{0:T(128)} %compare_select_fusion.2.place_ref, bf16[3072,1024]{1,0:T(8,128)(2,1)} %x_ref.19, bf16[1024,1024]{1,0:T(8,128)(2,1)} %refs_1_.15, bf16[1024,1024]{1,0:T(8,128)(2,1)} %refs_1_.15, s16[2,784,128]{2,1,0:T(8,128)(2,1)} %collective-permute-done.23.refs_2_, ...), custom_call_target="tpu_custom_call" | custom-call | flops 1 | bytes 1 | tf_op jit(solution)/shard_map/project/pallas_call | solution.py:183
  118.7 1.0 collective-permute-start.26
  120.3 6.7 %collective-permute-done.27.refs_9_ = bf16[1536,128]{1,0:T(8,128)(2,1)} collective-permute-done((bf16[1536,128]{1,0:T(8,128)(2,1)}, bf16[1536,128]{1,0:T(8,128)(2,1)}, u32[]{:S(2)}, u32[]{:S(2)}) %collective-permute-start.27) | collective-permute-done | bytes 393248 | tf_op jit(solution)/shard_map/ppermute | solution.py:602
  127.5 1.0 collective-permute-start.31
  128.7 9.4 %input_gradient.2.refs_14_ = f32[3072,1024]{1,0:T(8,128)} custom-call(s32[24]{0:T(128)} %job_ref.9, s32[8]{0:T(128)} %compare_select_fusion.2.place_ref, bf16[1024,1024]{1,0:T(8,128)(2,1)} %bitcast.7, bf16[1024,1024]{1,0:T(8,128)(2,1)} %bitcast.8, bf16[1024,1024]{1,0:T(8,128)(2,1)} %bitcast.9, bf16[1024,1024]{1,0:T(8,128)(2,1)} %bitcast.10, ...), custom_call_target="tpu_custom_call" | custom-call | flops 1 | bytes 1 | tf_op jit(solution)/shard_map/input_gradient/pallas_call | solution.py:502
  138.1 2.2 %add_factors.1 = (f32[1024,128]{1,0:T(8,128)}, f32[128,128]{1,0:T(8,128)}) custom-call(f32[128,1152]{1,0:T(8,128)} %get-tuple-element.54.refs_3_.kept_ref, f32[128,1152]{1,0:T(8,128)} %collective-permute-done.29.received_ref, s16[2,784,128]{2,1,0:T(8,128)(2,1)} %get-tuple-element.59.refs_14_.refs_0_), custom_call_target="tpu_custom_call" | custom-call | flops 1 | bytes 1 | tf_op jit(solution)/shard_map/add_factors/pallas_call | solution.py:382
  140.4 9.5 %input_gradient.3.refs_6_ = f32[3072,1024]{1,0:T(8,128)} custom-call(s32[24]{0:T(128)} %job_ref.9, s32[8]{0:T(128)} %compare_select_fusion.2.place_ref, bf16[1024,1024]{1,0:T(8,128)(2,1)} %bitcast.13, bf16[1024,1024]{1,0:T(8,128)(2,1)} %bitcast.14, bf16[1024,1024]{1,0:T(8,128)(2,1)} %bitcast.15, ...), custom_call_target="tpu_custom_call", output_to_operand_aliasing={{}: (16, {})} | custom-call | flops 1 | bytes 1 | tf_op jit(solution)/shard_map/input_gradient/pallas_call | solution.py:502
  149.9 2.1 %collective-permute-done.32.refs_8_.refs_5_ = bf16[1536,128]{1,0:T(8,128)(2,1)} collective-permute-done((bf16[1536,128]{1,0:T(8,128)(2,1)S(1)}, bf16[1536,128]{1,0:T(8,128)(2,1)}, u32[]{:S(2)}, u32[]{:S(2)}) %collective-permute-start.32) | collective-permute-done | bytes 393248 | tf_op jit(solution)/shard_map/ppermute | solution.py:605
  152.0 4.7 %place_output.1 = (bf16[32,128,128]{2,1,0:T(8,128)(2,1)}, bf16[16,128,128]{2,1,0:T(8,128)(2,1)}) custom-call(s32[24]{0:T(128)} %group_ref.3, s32[24]{0:T(128)} %slot_ref.3, s32[24]{0:T(128)} %job_ref.9, s32[1]{0:T(128)} %bitcast.me_ref, f32[768,128]{1,0:T(8,128)} %add_coded.5.low_ref.refs_0_.refs_12_, bf16[256,128]{1,0:T(8,128)(2,1)} %b_ref.1, ...), custom_call_target="tpu_custom_call" | custom-call | flops 1 | bytes 1 | tf_op jit(solution)/shard_map/place_output/pallas_call | solution.py:426
  156.7 0.8 collective-permute-start.33
  157.5 9.5 %add_pieces.1 = bf16[3072,1024]{1,0:T(8,128)(2,1)} custom-call(s32[8]{0:T(128)} %compare_select_fusion.2.place_ref, bf16[1024,1024]{1,0:T(8,128)(2,1)} %bitcast.19, bf16[1024,1024]{1,0:T(8,128)(2,1)} %bitcast.20, bf16[1536,128]{1,0:T(8,128)(2,1)} %copy-done, bf16[1536,128]{1,0:T(8,128)(2,1)} %copy-done.7, bf16[1536,128]{1,0:T(8,128)(2,1)} %copy-done.6, ...), custom_call_target="tpu_custom_call" | custom-call | flops 1 | bytes 1 | tf_op jit(solution)/shard_map/add_pieces/pallas_call | solution.py:559
  167.0 0.8 copy-done.8
  167.8 1.9 %complete.1 = bf16[32,128,128]{2,1,0:T(8,128)(2,1)} custom-call(s32[1]{0:T(128)} %bitcast.me_ref, bf16[16,128,128]{2,1,0:T(8,128)(2,1)} %copy-done.8, bf16[32,128,128]{2,1,0:T(8,128)(2,1)} %get-tuple-element.64.kept_ref.refs_7_), custom_call_target="tpu_custom_call", output_to_operand_aliasing={{}: (2, {})} | custom-call | flops 1 | bytes 1 | tf_op jit(solution)/shard_map/complete/pallas_call | solution.py:444
  (67 shorter events, 4.7 us)
Async XLA Ops:
  1.7 13.8 %collective-permute-start = (bf16[2048,128]{1,0:T(8,128)(2,1)S(1)}, bf16[2048,128]{1,0:T(8,128)(2,1)}, u32[]{:S(2)}, u32[]{:S(2)}) collective-permute-start(bf16[2048,128]{1,0:T(8,128)(2,1)S(1)} %constant_dynamic-slice_fusion), channel_id=1, source_target_pairs={{0,8},{8,0},{1,9},{9,1},{2,10},{10,2},{3,11},{11,3},{4,12},{12,4},... | collective-permute-start | bytes 1572872 | tf_op jit(solution)/shard_map/ppermute | solution.py:611
  6.8 13.1 %collective-permute-start.4 = (s16[2,784,128]{2,1,0:T(8,128)(2,1)}, s16[2,784,128]{2,1,0:T(8,128)(2,1)}, u32[]{:S(2)}, u32[]{:S(2)}) collective-permute-start(s16[2,784,128]{2,1,0:T(8,128)(2,1)} %get-tuple-element.35.refs_2_), channel_id=1, source_target_pairs={{0,2},{2,4},{4,6},{6,7},{7,5},{5,3},{3,1},{1,0},{8,10},{10,12},{12... | collective-permute-start | bytes 1204232 | tf_op jit(solution)/shard_map/ppermute | solution.py:602
  9.5 19.8 %copy-start.9 = (bf16[256,128]{1,0:T(8,128)(2,1)S(1)}, bf16[256,128]{1,0:T(8,128)(2,1)}, u32[]{:S(2)}) copy-start(bf16[256,128]{1,0:T(8,128)(2,1)} %b_ref.1) | copy-start | bytes 196612
  9.5 11.2 %collective-permute-start.5 = (s16[2,784,128]{2,1,0:T(8,128)(2,1)}, s16[2,784,128]{2,1,0:T(8,128)(2,1)}, u32[]{:S(2)}, u32[]{:S(2)}) collective-permute-start(s16[2,784,128]{2,1,0:T(8,128)(2,1)} %get-tuple-element.41), channel_id=1, source_target_pairs={{0,1},{2,0},{4,2},{6,4},{7,6},{5,7},{3,5},{1,3},{8,9},{10,8},{12,1... | collective-permute-start | bytes 1204232 | tf_op jit(solution)/shard_map/ppermute | solution.py:605
  14.1 13.9 %collective-permute-start.2 = (s16[2,784,128]{2,1,0:T(8,128)(2,1)}, s16[2,784,128]{2,1,0:T(8,128)(2,1)}, u32[]{:S(2)}, u32[]{:S(2)}) collective-permute-start(s16[2,784,128]{2,1,0:T(8,128)(2,1)} %get-tuple-element.36.refs_0_), channel_id=1, source_target_pairs={{0,2},{2,4},{4,6},{6,7},{7,5},{5,3},{3,1},{1,0},{8,10},{10,12},{12... | collective-permute-start | bytes 1204232 | tf_op jit(solution)/shard_map/ppermute | solution.py:602
  15.4 21.3 %collective-permute-start.3 = (s16[2,784,128]{2,1,0:T(8,128)(2,1)}, s16[2,784,128]{2,1,0:T(8,128)(2,1)}, u32[]{:S(2)}, u32[]{:S(2)}) collective-permute-start(s16[2,784,128]{2,1,0:T(8,128)(2,1)} %get-tuple-element.40), channel_id=1, source_target_pairs={{0,1},{2,0},{4,2},{6,4},{7,6},{5,7},{3,5},{1,3},{8,9},{10,8},{12,1... | collective-permute-start | bytes 1204232 | tf_op jit(solution)/shard_map/ppermute | solution.py:605
  18.7 23.0 %collective-permute-start.6 = (bf16[1536,128]{1,0:T(8,128)(2,1)}, bf16[1536,128]{1,0:T(8,128)(2,1)S(1)}, u32[]{:S(2)}, u32[]{:S(2)}) collective-permute-start(bf16[1536,128]{1,0:T(8,128)(2,1)} %get-tuple-element.43.refs_6_), channel_id=1, source_target_pairs={{0,1},{2,0},{4,2},{6,4},{7,6},{5,7},{3,5},{1,3},{8,9},{10,8},{12,1... | collective-permute-start | bytes 1179656 | tf_op jit(solution)/shard_map/ppermute | solution.py:605
  19.9 23.0 %collective-permute-start.7 = (bf16[1536,128]{1,0:T(8,128)(2,1)}, bf16[1536,128]{1,0:T(8,128)(2,1)S(1)}, u32[]{:S(2)}, u32[]{:S(2)}) collective-permute-start(bf16[1536,128]{1,0:T(8,128)(2,1)} %get-tuple-element.43.refs_6_), channel_id=1, source_target_pairs={{0,2},{2,4},{4,6},{6,7},{7,5},{5,3},{3,1},{1,0},{8,10},{10,12},{12... | collective-permute-start | bytes 1179656 | tf_op jit(solution)/shard_map/ppermute | solution.py:602
  20.7 28.9 %collective-permute-start.8 = (bf16[1536,128]{1,0:T(8,128)(2,1)}, bf16[1536,128]{1,0:T(8,128)(2,1)}, u32[]{:S(2)}, u32[]{:S(2)}) collective-permute-start(bf16[1536,128]{1,0:T(8,128)(2,1)} %get-tuple-element.45.refs_6_), channel_id=1, source_target_pairs={{0,1},{2,0},{4,2},{6,4},{7,6},{5,7},{3,5},{1,3},{8,9},{10,8},{12,1... | collective-permute-start | bytes 1179656 | tf_op jit(solution)/shard_map/ppermute | solution.py:605
  28.0 21.6 %collective-permute-start.9 = (bf16[1536,128]{1,0:T(8,128)(2,1)}, bf16[1536,128]{1,0:T(8,128)(2,1)}, u32[]{:S(2)}, u32[]{:S(2)}) collective-permute-start(bf16[1536,128]{1,0:T(8,128)(2,1)} %get-tuple-element.45.refs_6_), channel_id=1, source_target_pairs={{0,2},{2,4},{4,6},{6,7},{7,5},{5,3},{3,1},{1,0},{8,10},{10,12},{12... | collective-permute-start | bytes 1179656 | tf_op jit(solution)/shard_map/ppermute | solution.py:602
  36.7 12.9 %collective-permute-start.1 = (s16[6,144,128]{2,1,0:T(8,128)(2,1)}, s16[6,144,128]{2,1,0:T(8,128)(2,1)}, u32[]{:S(2)}, u32[]{:S(2)}) collective-permute-start(s16[6,144,128]{2,1,0:T(8,128)(2,1)} %get-tuple-element.39.refs_4_), channel_id=1, source_target_pairs={{0,1},{1,0},{2,3},{3,2},{4,5},{5,4},{6,7},{7,6},{8,9},{9,8},{10,11... | collective-permute-start | bytes 663560 | tf_op jit(solution)/shard_map/ppermute | solution.py:608
  41.6 2.3 %copy-start.2 = (bf16[1536,128]{1,0:T(8,128)(2,1)}, bf16[1536,128]{1,0:T(8,128)(2,1)S(1)}, u32[]{:S(2)}) copy-start(bf16[1536,128]{1,0:T(8,128)(2,1)S(1)} %collective-permute-done.6.refs_5_.refs_7_) | copy-start | bytes 1179652
  41.6 16.6 %collective-permute-start.11 = (s16[2,784,128]{2,1,0:T(8,128)(2,1)}, s16[2,784,128]{2,1,0:T(8,128)(2,1)}, u32[]{:S(2)}, u32[]{:S(2)}) collective-permute-start(s16[2,784,128]{2,1,0:T(8,128)(2,1)} %get-tuple-element.42.refs_4_), channel_id=1, source_target_pairs={{0,2},{2,4},{4,6},{6,7},{7,5},{5,3},{3,1},{1,0},{8,10},{10,12},{12... | collective-permute-start | bytes 1204232 | tf_op jit(solution)/shard_map/ppermute | solution.py:602
  42.9 0.8 copy-start.3
  43.7 27.9 %copy-start.1 = (bf16[1024,256]{1,0:T(8,128)(2,1)S(1)}, bf16[1024,256]{1,0:T(8,128)(2,1)}, u32[]{:S(2)}) copy-start(bf16[1024,256]{1,0:T(8,128)(2,1)} %a_ref.1) | copy-start | bytes 1572868
  43.7 14.5 %collective-permute-start.12 = (s16[2,784,128]{2,1,0:T(8,128)(2,1)}, s16[2,784,128]{2,1,0:T(8,128)(2,1)}, u32[]{:S(2)}, u32[]{:S(2)}) collective-permute-start(s16[2,784,128]{2,1,0:T(8,128)(2,1)} %get-tuple-element.48), channel_id=1, source_target_pairs={{0,1},{2,0},{4,2},{6,4},{7,6},{5,7},{3,5},{1,3},{8,9},{10,8},{12,1... | collective-permute-start | bytes 1204232 | tf_op jit(solution)/shard_map/ppermute | solution.py:605
  51.6 8.1 %collective-permute-start.10 = (s16[6,144,128]{2,1,0:T(8,128)(2,1)}, s16[6,144,128]{2,1,0:T(8,128)(2,1)S(1)}, u32[]{:S(2)}, u32[]{:S(2)}) collective-permute-start(s16[6,144,128]{2,1,0:T(8,128)(2,1)} %get-tuple-element.47), channel_id=1, source_target_pairs={{0,2},{1,3},{2,0},{3,1},{4,6},{5,7},{6,4},{7,5},{8,10},{9,11},{10,... | collective-permute-start | bytes 663560 | tf_op jit(solution)/shard_map/ppermute | solution.py:608
  51.8 15.7 %collective-permute-start.13 = (bf16[1536,128]{1,0:T(8,128)(2,1)}, bf16[1536,128]{1,0:T(8,128)(2,1)S(1)}, u32[]{:S(2)}, u32[]{:S(2)}) collective-permute-start(bf16[1536,128]{1,0:T(8,128)(2,1)} %copy-done.2), channel_id=1, source_target_pairs={{0,1},{2,0},{4,2},{6,4},{7,6},{5,7},{3,5},{1,3},{8,9},{10,8},{12,1... | collective-permute-start | bytes 1179656 | tf_op jit(solution)/shard_map/ppermute | solution.py:605
  53.2 24.1 %collective-permute-start.14 = (bf16[1536,128]{1,0:T(8,128)(2,1)}, bf16[1536,128]{1,0:T(8,128)(2,1)}, u32[]{:S(2)}, u32[]{:S(2)}) collective-permute-start(bf16[1536,128]{1,0:T(8,128)(2,1)} %copy-done.3), channel_id=1, source_target_pairs={{0,2},{2,4},{4,6},{6,7},{7,5},{5,3},{3,1},{1,0},{8,10},{10,12},{12... | collective-permute-start | bytes 1179656 | tf_op jit(solution)/shard_map/ppermute | solution.py:602
  58.2 24.6 %collective-permute-start.16 = (s16[2,784,128]{2,1,0:T(8,128)(2,1)}, s16[2,784,128]{2,1,0:T(8,128)(2,1)}, u32[]{:S(2)}, u32[]{:S(2)}) collective-permute-start(s16[2,784,128]{2,1,0:T(8,128)(2,1)} %get-tuple-element.44.refs_2_), channel_id=1, source_target_pairs={{0,2},{2,4},{4,6},{6,7},{7,5},{5,3},{3,1},{1,0},{8,10},{10,12},{12... | collective-permute-start | bytes 1204232 | tf_op jit(solution)/shard_map/ppermute | solution.py:602
  58.2 24.7 %collective-permute-start.17 = (s16[2,784,128]{2,1,0:T(8,128)(2,1)}, s16[2,784,128]{2,1,0:T(8,128)(2,1)}, u32[]{:S(2)}, u32[]{:S(2)}) collective-permute-start(s16[2,784,128]{2,1,0:T(8,128)(2,1)} %get-tuple-element.52), channel_id=1, source_target_pairs={{0,1},{2,0},{4,2},{6,4},{7,6},{5,7},{3,5},{1,3},{8,9},{10,8},{12,1... | collective-permute-start | bytes 1204232 | tf_op jit(solution)/shard_map/ppermute | solution.py:605
  59.7 7.8 %copy-start.10 = (s16[6,144,128]{2,1,0:T(8,128)(2,1)}, s16[6,144,128]{2,1,0:T(8,128)(2,1)S(1)}, u32[]{:S(2)}) copy-start(s16[6,144,128]{2,1,0:T(8,128)(2,1)S(1)} %collective-permute-done.10.refs_1_) | copy-start | bytes 663556
  59.7 28.1 %collective-permute-start.18 = (bf16[1536,128]{1,0:T(8,128)(2,1)}, bf16[1536,128]{1,0:T(8,128)(2,1)}, u32[]{:S(2)}, u32[]{:S(2)}) collective-permute-start(bf16[1536,128]{1,0:T(8,128)(2,1)} %collective-permute-done.8.refs_3_.refs_7_), channel_id=1, source_target_pairs={{0,1},{2,0},{4,2},{6,4},{7,6},{5,7},{3,5},{1,3},{8,9},{10,8},{12,1... | collective-permute-start | bytes 1179656 | tf_op jit(solution)/shard_map/ppermute | solution.py:605
  67.5 9.8 %copy-start.4 = (bf16[1536,128]{1,0:T(8,128)(2,1)}, bf16[1536,128]{1,0:T(8,128)(2,1)S(1)}, u32[]{:S(2)}) copy-start(bf16[1536,128]{1,0:T(8,128)(2,1)S(1)} %collective-permute-done.13.refs_3_.refs_8_) | copy-start | bytes 1179652
  67.5 21.6 %collective-permute-start.19 = (bf16[1536,128]{1,0:T(8,128)(2,1)}, bf16[1536,128]{1,0:T(8,128)(2,1)}, u32[]{:S(2)}, u32[]{:S(2)}) collective-permute-start(bf16[1536,128]{1,0:T(8,128)(2,1)} %collective-permute-done.9.refs_4_.refs_11_), channel_id=1, source_target_pairs={{0,2},{2,4},{4,6},{6,7},{7,5},{5,3},{3,1},{1,0},{8,10},{10,12},{12... | collective-permute-start | bytes 1179656 | tf_op jit(solution)/shard_map/ppermute | solution.py:602
  79.3 8.5 %copy-start.5 = (bf16[1536,128]{1,0:T(8,128)(2,1)S(1)}, bf16[1536,128]{1,0:T(8,128)(2,1)}, u32[]{:S(2)}) copy-start(bf16[1536,128]{1,0:T(8,128)(2,1)} %copy-done.4) | copy-start | bytes 1179652
  79.3 9.9 %collective-permute-start.15 = (s16[6,144,128]{2,1,0:T(8,128)(2,1)}, s16[6,144,128]{2,1,0:T(8,128)(2,1)}, u32[]{:S(2)}, u32[]{:S(2)}) collective-permute-start(s16[6,144,128]{2,1,0:T(8,128)(2,1)} %get-tuple-element.51), channel_id=1, source_target_pairs={{0,4},{1,5},{2,6},{3,7},{4,0},{5,1},{6,2},{7,3},{8,12},{9,13},{10,... | collective-permute-start | bytes 663560 | tf_op jit(solution)/shard_map/ppermute | solution.py:608
  82.8 25.0 %collective-permute-start.20 = (s16[2,784,128]{2,1,0:T(8,128)(2,1)}, s16[2,784,128]{2,1,0:T(8,128)(2,1)}, u32[]{:S(2)}, u32[]{:S(2)}) collective-permute-start(s16[2,784,128]{2,1,0:T(8,128)(2,1)} %get-tuple-element.49.refs_2_), channel_id=1, source_target_pairs={{0,2},{2,4},{4,6},{6,7},{7,5},{5,3},{3,1},{1,0},{8,10},{10,12},{12... | collective-permute-start | bytes 1204232 | tf_op jit(solution)/shard_map/ppermute | solution.py:602
  87.6 20.8 %collective-permute-start.23 = (s16[2,784,128]{2,1,0:T(8,128)(2,1)}, s16[2,784,128]{2,1,0:T(8,128)(2,1)}, u32[]{:S(2)}, u32[]{:S(2)}) collective-permute-start(s16[2,784,128]{2,1,0:T(8,128)(2,1)} %get-tuple-element.53.refs_2_), channel_id=1, source_target_pairs={{0,2},{2,4},{4,6},{6,7},{7,5},{5,3},{3,1},{1,0},{8,10},{10,12},{12... | collective-permute-start | bytes 1204232 | tf_op jit(solution)/shard_map/ppermute | solution.py:602
  87.8 20.5 %collective-permute-start.24 = (bf16[1536,128]{1,0:T(8,128)(2,1)S(1)}, bf16[1536,128]{1,0:T(8,128)(2,1)S(1)}, u32[]{:S(2)}, u32[]{:S(2)}) collective-permute-start(bf16[1536,128]{1,0:T(8,128)(2,1)S(1)} %copy-done.5), channel_id=1, source_target_pairs={{0,1},{2,0},{4,2},{6,4},{7,6},{5,7},{3,5},{1,3},{8,9},{10,8},{12,1... | collective-permute-start | bytes 1179656 | tf_op jit(solution)/shard_map/ppermute | solution.py:605
  100.4 28.1 %collective-permute-start.29 = (f32[128,1152]{1,0:T(8,128)}, f32[128,1152]{1,0:T(8,128)}, u32[]{:S(2)}, u32[]{:S(2)}) collective-permute-start(f32[128,1152]{1,0:T(8,128)} %get-tuple-element.61), channel_id=1, source_target_pairs={{0,8},{8,0},{1,9},{9,1},{2,10},{10,2},{3,11},{11,3},{4,12},{12,4},... | collective-permute-start | bytes 1769480 | tf_op jit(solution)/shard_map/ppermute | solution.py:686
  106.9 11.9 %collective-permute-start.22 = (s16[2,784,128]{2,1,0:T(8,128)(2,1)}, s16[2,784,128]{2,1,0:T(8,128)(2,1)}, u32[]{:S(2)}, u32[]{:S(2)}) collective-permute-start(s16[2,784,128]{2,1,0:T(8,128)(2,1)} %get-tuple-element.57), channel_id=1, source_target_pairs={{0,1},{2,0},{4,2},{6,4},{7,6},{5,7},{3,5},{1,3},{8,9},{10,8},{12,1... | collective-permute-start | bytes 1204232 | tf_op jit(solution)/shard_map/ppermute | solution.py:605
  107.8 11.9 %collective-permute-start.28 = (bf16[1536,128]{1,0:T(8,128)(2,1)}, bf16[1536,128]{1,0:T(8,128)(2,1)}, u32[]{:S(2)}, u32[]{:S(2)}) collective-permute-start(bf16[1536,128]{1,0:T(8,128)(2,1)} %collective-permute-done.14.refs_4_.refs_10_), channel_id=1, source_target_pairs={{0,2},{2,4},{4,6},{6,7},{7,5},{5,3},{3,1},{1,0},{8,10},{10,12},{12... | collective-permute-start | bytes 1179656 | tf_op jit(solution)/shard_map/ppermute | solution.py:602
  108.3 5.9 %copy-start = (bf16[1536,128]{1,0:T(8,128)(2,1)}, bf16[1536,128]{1,0:T(8,128)(2,1)S(1)}, u32[]{:S(2)}) copy-start(bf16[1536,128]{1,0:T(8,128)(2,1)S(1)} %collective-permute-done.24.refs_4_.refs_15_.refs_2_) | copy-start | bytes 1179652
  108.3 18.7 %collective-permute-start.27 = (bf16[1536,128]{1,0:T(8,128)(2,1)}, bf16[1536,128]{1,0:T(8,128)(2,1)}, u32[]{:S(2)}, u32[]{:S(2)}) collective-permute-start(bf16[1536,128]{1,0:T(8,128)(2,1)} %collective-permute-done.19.refs_4_.refs_10_), channel_id=1, source_target_pairs={{0,2},{2,4},{4,6},{6,7},{7,5},{5,3},{3,1},{1,0},{8,10},{10,12},{12... | collective-permute-start | bytes 1179656 | tf_op jit(solution)/shard_map/ppermute | solution.py:602
  108.4 19.1 %collective-permute-start.30 = (bf16[1536,128]{1,0:T(8,128)(2,1)}, bf16[1536,128]{1,0:T(8,128)(2,1)S(1)}, u32[]{:S(2)}, u32[]{:S(2)}) collective-permute-start(bf16[1536,128]{1,0:T(8,128)(2,1)} %collective-permute-done.18.refs_3_.refs_8_), channel_id=1, source_target_pairs={{0,1},{2,0},{4,2},{6,4},{7,6},{5,7},{3,5},{1,3},{8,9},{10,8},{12,1... | collective-permute-start | bytes 1179656 | tf_op jit(solution)/shard_map/ppermute | solution.py:605
  118.7 31.1 %collective-permute-start.26 = (s16[2,784,128]{2,1,0:T(8,128)(2,1)}, s16[2,784,128]{2,1,0:T(8,128)(2,1)}, u32[]{:S(2)}, u32[]{:S(2)}) collective-permute-start(s16[2,784,128]{2,1,0:T(8,128)(2,1)} %get-tuple-element.60), channel_id=1, source_target_pairs={{0,1},{2,0},{4,2},{6,4},{7,6},{5,7},{3,5},{1,3},{8,9},{10,8},{12,1... | collective-permute-start | bytes 1204232 | tf_op jit(solution)/shard_map/ppermute | solution.py:605
  119.7 30.1 %collective-permute-start.21 = (s16[2,784,128]{2,1,0:T(8,128)(2,1)}, s16[2,784,128]{2,1,0:T(8,128)(2,1)}, u32[]{:S(2)}, u32[]{:S(2)}) collective-permute-start(s16[2,784,128]{2,1,0:T(8,128)(2,1)} %get-tuple-element.56.refs_3_), channel_id=1, source_target_pairs={{0,2},{2,4},{4,6},{6,7},{7,5},{5,3},{3,1},{1,0},{8,10},{10,12},{12... | collective-permute-start | bytes 1204232 | tf_op jit(solution)/shard_map/ppermute | solution.py:602
  127.0 25.0 %collective-permute-start.25 = (s16[2,784,128]{2,1,0:T(8,128)(2,1)}, s16[2,784,128]{2,1,0:T(8,128)(2,1)}, u32[]{:S(2)}, u32[]{:S(2)}) collective-permute-start(s16[2,784,128]{2,1,0:T(8,128)(2,1)} %get-tuple-element.59.refs_14_.refs_0_), channel_id=1, source_target_pairs={{0,2},{2,4},{4,6},{6,7},{7,5},{5,3},{3,1},{1,0},{8,10},{10,12},{12... | collective-permute-start | bytes 1204232 | tf_op jit(solution)/shard_map/ppermute | solution.py:602
  127.5 10.6 %copy-start.6 = (bf16[1536,128]{1,0:T(8,128)(2,1)}, bf16[1536,128]{1,0:T(8,128)(2,1)S(1)}, u32[]{:S(2)}) copy-start(bf16[1536,128]{1,0:T(8,128)(2,1)S(1)} %collective-permute-done.30.refs_16_.refs_4_) | copy-start | bytes 1179652
  127.5 22.3 %collective-permute-start.31 = (bf16[1536,128]{1,0:T(8,128)(2,1)}, bf16[1536,128]{1,0:T(8,128)(2,1)S(1)}, u32[]{:S(2)}, u32[]{:S(2)}) collective-permute-start(bf16[1536,128]{1,0:T(8,128)(2,1)} %copy-done), channel_id=1, source_target_pairs={{0,1},{2,0},{4,2},{6,4},{7,6},{5,7},{3,5},{1,3},{8,9},{10,8},{12,1... | collective-permute-start | bytes 1179656 | tf_op jit(solution)/shard_map/ppermute | solution.py:605
  128.5 23.5 %collective-permute-start.32 = (bf16[1536,128]{1,0:T(8,128)(2,1)S(1)}, bf16[1536,128]{1,0:T(8,128)(2,1)}, u32[]{:S(2)}, u32[]{:S(2)}) collective-permute-start(bf16[1536,128]{1,0:T(8,128)(2,1)S(1)} %collective-permute-done.30.refs_16_.refs_4_), channel_id=1, source_target_pairs={{0,1},{2,0},{4,2},{6,4},{7,6},{5,7},{3,5},{1,3},{8,9},{10,8},{12,1... | collective-permute-start | bytes 1179656 | tf_op jit(solution)/shard_map/ppermute | solution.py:605
  149.8 2.1 %copy-start.7 = (bf16[1536,128]{1,0:T(8,128)(2,1)}, bf16[1536,128]{1,0:T(8,128)(2,1)S(1)}, u32[]{:S(2)}) copy-start(bf16[1536,128]{1,0:T(8,128)(2,1)S(1)} %collective-permute-done.31.refs_7_.refs_3_) | copy-start | bytes 1179652
  156.7 10.3 %collective-permute-start.33 = (bf16[16,128,128]{2,1,0:T(8,128)(2,1)}, bf16[16,128,128]{2,1,0:T(8,128)(2,1)S(1)}, u32[]{:S(2)}, u32[]{:S(2)}) collective-permute-start(bf16[16,128,128]{2,1,0:T(8,128)(2,1)} %get-tuple-element.63), channel_id=1, source_target_pairs={{0,8},{8,0},{1,9},{9,1},{2,10},{10,2},{3,11},{11,3},{4,12},{12,4},... | collective-permute-start | bytes 1572872 | tf_op jit(solution)/shard_map/ppermute | solution.py:702
  167.0 0.8 copy-start.8
